TPU v7x, 32 devices: a whole 2x2x4 slice. The times are simulated.
32 devices in a mesh: dp: 2 (over core), seq: 4 (over y, x), tensor: 4 (over z).
Axes of the slice: x: 2, y: 2, z: 4, core: 2. Of those that a mesh axis runs over, the one named last changes fastest.
Arguments:
- query_rows: bfloat16 [2, 768, 3072], P('dp', 'seq', 'tensor'), may hold values from -12 to 12
- key_rows: bfloat16 [2, 768, 3072], P('dp', 'seq', 'tensor'), may hold values from -12 to 12
- value_rows: bfloat16 [2, 768, 3072], P('dp', 'seq', 'tensor'), may hold values from -6 to 6
- lengths: int32 [2], P('dp'), may hold values from 384 to 768, as said below
- out_weight: bfloat16 [3072, 3072], P('seq', 'tensor'), may hold values from -4.1875 to 4.1875
- gate_vector: float32 [2, 3072], P('dp'), may hold values from 0.5 to 1.5
- cotangent: bfloat16 [2, 768, 3072], P('dp', 'seq', 'tensor'), may hold values from -12 to 12
Outputs:
- branch_out: bfloat16 [2, 768, 3072], P('dp', 'seq', 'tensor')
- grad_query: bfloat16 [2, 768, 3072], P('dp', 'seq', 'tensor')
- grad_key: bfloat16 [2, 768, 3072], P('dp', 'seq', 'tensor')
- grad_value: bfloat16 [2, 768, 3072], P('dp', 'seq', 'tensor')
- grad_weight: float32 [3072, 3072], P('seq', 'tensor')
- grad_gate: float32 [2, 3072], P('dp', 'tensor')
Inputs may be any that keep to these rules, and one draw needn't show every extreme that they name: `lengths`: some clip has all 768 positions live.
All inputs are finite; a program needn't handle non-finite values.
Results may differ from a plain program's by a relative error of at most 0.035.
Values may be sent and summed in bfloat16 or wider, within the bound.
No kernel may reach another device: no remote copies, remote signals or barrier semaphores. Data moves between devices by JAX's collectives and lax.ppermute only.
A program may use at most 64 MiB of HBM per device.

v0:
```python
import math

import jax
import jax.numpy as jnp
from jax import lax
from jax.sharding import PartitionSpec as P

HD = 128


MASKED_SCORE = -1e30


def block_rows(piece_rows):
    return math.gcd(piece_rows, 512)


def query_terms(
    query_heads, grad_heads, row_lse, row_delta, key_block, value_block, key_live, score_scale
):
    scores = (
        jnp.einsum("thd,shd->ths", query_heads, key_block, preferred_element_type=jnp.float32)
        * score_scale
    )
    probs = jnp.where(key_live[None, None, :], jnp.exp(scores - row_lse[:, :, None]), 0.0)
    grad_probs = jnp.einsum(
        "thd,shd->ths", grad_heads, value_block, preferred_element_type=jnp.float32
    )
    dscores = (probs * (grad_probs - row_delta[:, :, None]) * score_scale).astype(jnp.bfloat16)
    return jnp.einsum("ths,shd->thd", dscores, key_block, preferred_element_type=jnp.float32)


def key_terms(
    query_block, grad_block, lse_block, delta_block, key_heads, value_heads, key_live, score_scale
):
    scores = (
        jnp.einsum("shd,thd->sht", query_block, key_heads, preferred_element_type=jnp.float32)
        * score_scale
    )
    probs = jnp.where(key_live[None, None, :], jnp.exp(scores - lse_block[:, :, None]), 0.0)
    value_part = jnp.einsum(
        "sht,shd->thd", probs.astype(jnp.bfloat16), grad_block, preferred_element_type=jnp.float32
    )
    grad_probs = jnp.einsum(
        "shd,thd->sht", grad_block, value_heads, preferred_element_type=jnp.float32
    )
    dscores = (probs * (grad_probs - delta_block[:, :, None]) * score_scale).astype(jnp.bfloat16)
    key_part = jnp.einsum("sht,shd->thd", dscores, query_block, preferred_element_type=jnp.float32)
    return (key_part, value_part)


def shards(query_rows, key_rows, value_rows, lengths, out_weight, gate_vector, cotangent):
    tokens = query_rows.shape[1]
    local_width = query_rows.shape[2]
    head_count = local_width // HD
    score_scale = 1.0 / math.sqrt(HD)
    length = lengths[0]
    query_local = query_rows[0]
    key_local = key_rows[0]
    value_local = value_rows[0]
    query_heads = query_local.reshape(tokens, head_count, HD)
    key_heads = key_local.reshape(tokens, head_count, HD)
    value_heads = value_local.reshape(tokens, head_count, HD)
    head_zeros = jnp.zeros((tokens, head_count, HD), jnp.float32)
    start_top = jnp.full((tokens, head_count), MASKED_SCORE, jnp.float32)
    start_total = jnp.zeros((tokens, head_count), jnp.float32)
    key_piece = lax.all_gather(key_local, "seq", axis=0, tiled=True)
    value_piece = lax.all_gather(value_local, "seq", axis=0, tiled=True)
    piece_rows = key_piece.shape[0]
    step_rows = block_rows(piece_rows)

    def forward_block_step(block_index, state):
        row_top, row_total, summed = state
        offset = block_index * step_rows
        key_block = lax.dynamic_slice_in_dim(key_piece, offset, step_rows, 0).reshape(
            step_rows, head_count, HD
        )
        value_block = lax.dynamic_slice_in_dim(value_piece, offset, step_rows, 0).reshape(
            step_rows, head_count, HD
        )
        key_live = offset + jnp.arange(step_rows) < length
        scores = (
            jnp.einsum("thd,shd->ths", query_heads, key_block, preferred_element_type=jnp.float32)
            * score_scale
        )
        masked = jnp.where(key_live[None, None, :], scores, MASKED_SCORE)
        new_top = jnp.maximum(row_top, jnp.max(masked, axis=2))
        weights = jnp.where(key_live[None, None, :], jnp.exp(masked - new_top[:, :, None]), 0.0)
        shrink = jnp.exp(row_top - new_top)
        row_total = row_total * shrink + jnp.sum(weights, axis=2)
        summed = summed * shrink[:, :, None] + jnp.einsum(
            "ths,shd->thd",
            weights.astype(jnp.bfloat16),
            value_block,
            preferred_element_type=jnp.float32,
        )
        return (new_top, row_total, summed)

    row_top, row_total, summed = lax.fori_loop(
        0, piece_rows // step_rows, forward_block_step, (start_top, start_total, head_zeros)
    )
    attended_heads = (summed / row_total[:, :, None]).astype(jnp.bfloat16)
    attended = attended_heads.reshape(tokens, local_width)
    row_lse = row_top + jnp.log(row_total)
    weight_whole = lax.all_gather(out_weight, "seq", axis=0, tiled=True)
    partial_value = jnp.einsum(
        "tk,rk->tr", attended, weight_whole, preferred_element_type=jnp.float32
    )
    projected = lax.psum_scatter(
        partial_value.astype(jnp.bfloat16), "tensor", scatter_dimension=1, tiled=True
    ).astype(jnp.float32)
    out_width = projected.shape[1]
    gate_local = lax.dynamic_slice_in_dim(
        gate_vector[0], lax.axis_index("tensor") * out_width, out_width
    )
    cot_rows = cotangent[0].astype(jnp.float32)
    branch = (gate_local[None, :] * projected).astype(jnp.bfloat16)
    gate_grad = lax.psum(jnp.sum(cot_rows * projected, axis=0), "seq")
    grad_proj = (gate_local[None, :] * cot_rows).astype(jnp.bfloat16)
    grad_full = lax.all_gather(grad_proj, "tensor", axis=1, tiled=True)
    grad_att = jnp.dot(grad_full, weight_whole, preferred_element_type=jnp.float32).astype(
        jnp.bfloat16
    )
    row_share = lax.psum_scatter(
        jnp.einsum("tr,tk->rk", grad_full, attended, preferred_element_type=jnp.float32).astype(
            jnp.bfloat16
        ),
        "seq",
        scatter_dimension=0,
        tiled=True,
    )
    grad_weight = lax.psum(row_share, "dp").astype(jnp.float32)
    grad_heads = grad_att.reshape(tokens, head_count, HD)
    row_delta = jnp.sum(grad_heads.astype(jnp.float32) * attended_heads.astype(jnp.float32), axis=2)
    all_lse, all_delta = (
        lax.all_gather(row_lse, "seq", axis=0, tiled=True),
        lax.all_gather(row_delta, "seq", axis=0, tiled=True),
    )
    key_offset = lax.axis_index("seq") * tokens
    local_live = key_offset + jnp.arange(tokens) < length
    query_key_piece = lax.all_gather(key_local, "seq", axis=0, tiled=True)
    query_value_piece = lax.all_gather(value_local, "seq", axis=0, tiled=True)
    piece_rows = query_key_piece.shape[0]
    query_step_rows = block_rows(piece_rows)

    def query_block_step(block_index, state):
        offset = block_index * query_step_rows
        key_block = lax.dynamic_slice_in_dim(query_key_piece, offset, query_step_rows, 0).reshape(
            query_step_rows, head_count, HD
        )
        value_block = lax.dynamic_slice_in_dim(
            query_value_piece, offset, query_step_rows, 0
        ).reshape(query_step_rows, head_count, HD)
        key_live = offset + jnp.arange(query_step_rows) < length
        return state + query_terms(
            query_heads,
            grad_heads,
            row_lse,
            row_delta,
            key_block,
            value_block,
            key_live,
            score_scale,
        )

    grad_q = lax.fori_loop(0, piece_rows // query_step_rows, query_block_step, head_zeros)
    query_piece = lax.all_gather(query_local, "seq", axis=0, tiled=True)
    grad_piece = lax.all_gather(grad_att, "seq", axis=0, tiled=True)
    piece_rows = query_piece.shape[0]
    key_step_rows = block_rows(piece_rows)

    def key_block_step(block_index, state):
        offset = block_index * key_step_rows
        query_block = lax.dynamic_slice_in_dim(query_piece, offset, key_step_rows, 0).reshape(
            key_step_rows, head_count, HD
        )
        grad_block = lax.dynamic_slice_in_dim(grad_piece, offset, key_step_rows, 0).reshape(
            key_step_rows, head_count, HD
        )
        lse_block = lax.dynamic_slice_in_dim(all_lse, offset, key_step_rows, 0)
        delta_block = lax.dynamic_slice_in_dim(all_delta, offset, key_step_rows, 0)
        key_part, value_part = key_terms(
            query_block,
            grad_block,
            lse_block,
            delta_block,
            key_heads,
            value_heads,
            local_live,
            score_scale,
        )
        return (state[0] + key_part, state[1] + value_part)

    grad_k, grad_v = lax.fori_loop(
        0, piece_rows // key_step_rows, key_block_step, (head_zeros, head_zeros)
    )
    grad_query = grad_q.reshape(tokens, local_width).astype(jnp.bfloat16)
    grad_key = grad_k.reshape(tokens, local_width).astype(jnp.bfloat16)
    grad_value = grad_v.reshape(tokens, local_width).astype(jnp.bfloat16)
    return (
        branch[None],
        grad_query[None],
        grad_key[None],
        grad_value[None],
        grad_weight,
        gate_grad[None],
    )


def solution(mesh):
    placed = (
        P("dp", "seq", "tensor"),
        P("dp", "seq", "tensor"),
        P("dp", "seq", "tensor"),
        P("dp"),
        P("seq", "tensor"),
        P("dp", None),
        P("dp", "seq", "tensor"),
    )
    return jax.shard_map(
        shards,
        mesh=mesh,
        in_specs=placed,
        out_specs=(
            P("dp", "seq", "tensor"),
            P("dp", "seq", "tensor"),
            P("dp", "seq", "tensor"),
            P("dp", "seq", "tensor"),
            P("seq", "tensor"),
            P("dp", "tensor"),
        ),
        check_vma=False,
    )
```

profile of v0, /device:TPU:0, one launch (start us, length us, event | category | flops | bytes accessed | tf_op | source)
XLA Modules:
  0.0 351.2 jit_solution(8281250905136310308)
XLA Ops:
  8.0 0.7 all-gather.20.cloned.1.call-update
  8.8 1.7 fusion.49
  11.5 0.8 copy.77
  12.3 28.0 %all-gather.18.cloned.1.call-done = bf16[1,768,768]{2,1,0:T(8,128)(2,1)} async-done(((bf16[1,192,768]{2,1,0:T(8,128)(2,1)}), bf16[1,768,768]{2,1,0:T(8,128)(2,1)}) %all-gather.18.cloned.1.call-update) | async-done | bytes 1179664 | tf_op jit(solution)/shard_map/all_gather | solution.py:67
  40.3 1.6 copy.76
  41.9 28.0 %all-gather.20.cloned.1.call-done = bf16[1,768,768]{2,1,0:T(8,128)(2,1)} async-done(((bf16[1,192,768]{2,1,0:T(8,128)(2,1)}), bf16[1,768,768]{2,1,0:T(8,128)(2,1)}) %all-gather.20.cloned.1.call-update) | async-done | bytes 1179664 | tf_op jit(solution)/shard_map/all_gather | solution.py:68
  69.9 2.4 copy.78
  72.3 10.0 %while.48 = (s32[]{:T(128)}, f32[192,6]{0,1:T(8,128)S(1)}, f32[192,6]{0,1:T(8,128)S(1)}, f32[192,6,128]{2,0,1:T(8,128)S(1)}, s32[]{:T(128)}, /*index=5*/bf16[768...) while((s32[]{:T(128)}, f32[192,6]{0,1:T(8,128)S(1)}, ...), condition=%wide.region_3.4_spmd.clone, body=%wide.region_0.3_spmd.clone.sunk | while | flops 154097792 | bytes 8627423 | solution.py:99
  72.3 1.1 constant_dynamic-slice_fusion.12
  75.6 1.1 constant_dynamic-slice_fusion.12
  78.9 1.1 constant_dynamic-slice_fusion.12
  82.4 20.2 %all-gather.14.cloned.1.call-done = bf16[192,3072]{1,0:T(8,128)(2,1)} async-done(((bf16[192,768]{1,0:T(8,128)(2,1)}), bf16[192,3072]{1,0:T(8,128)(2,1)}) %all-gather.14.cloned.1.call-update) | async-done | bytes 1179664 | tf_op jit(solution)/shard_map/all_gather | solution.py:120
  102.5 57.9 %all-gather.12.cloned.1.call-done = bf16[3072,768]{1,0:T(8,128)(2,1)} async-done(((bf16[768,768]{1,0:T(8,128)(2,1)}), bf16[3072,768]{1,0:T(8,128)(2,1)}) %all-gather.12.cloned.1.call-update) | async-done | bytes 4718608 | tf_op jit(solution)/shard_map/all_gather | solution.py:105
  160.5 3.8 %convolution_convert_fusion.2 = bf16[192,768]{1,0:T(8,128)(2,1)S(1)} fusion(bf16[192,3072]{1,0:T(8,128)(2,1)} %all-gather.14.cloned.1.call-done, bf16[3072,768]{1,0:T(8,128)(2,1)} %all-gather.12.cloned.1.call-done), kind=kOutput, calls=%fused_computation.70 | convolution fusion | flops 906117120 | bytes 6193152 | tf_op jit(solution)/shard_map/dot_general | solution.py:121
  164.3 1.1 reshape.119
  165.4 2.3 multiply_reduce_fusion
  167.7 0.8 copy-done.6
  168.4 3.6 %convolution_convert_fusion = bf16[3072,768]{1,0:T(8,128)(2,1)} fusion(bf16[192,3072]{1,0:T(8,128)(2,1)S(1)} %copy-done.3, bf16[24,8,6,128]{3,2,1,0:T(8,128)(2,1)S(1)} %bitcast.182), kind=kOutput, calls=%fused_computation.68 | convolution fusion | flops 908328960 | bytes 6193152 | tf_op jit(solution)/shard_map/tr,tk->rk/dot_general | solution.py:125
  172.7 0.7 all-gather.16.cloned.1.call-update
  173.8 1.4 reshape_squeeze.11
  175.2 0.8 copy.91
  175.9 0.8 copy.93
  177.3 8.3 %all-gather.3 = f32[4,192,6]{1,2,0:T(8,128)S(1)} all-gather(f32[1,192,6]{1,2,0:T(8,128)} %bitcast.6), channel_id=1, replica_groups=mesh['dp'=2,'seq'=4,'tensor'=4] {'seq'}, dimensions={0}, use_global_device_ids=true | all-gather | bytes 23040 | tf_op jit(solution)/shard_map/all_gather | solution.py:136
  185.6 0.7 reshape.125
  186.3 1.6 copy.85
  187.9 0.8 copy_bitcast_fusion
  188.7 5.2 %convolution_convert_fusion.1 = bf16[192,3072]{1,0:T(8,128)(2,1)} fusion(bf16[3072,768]{1,0:T(8,128)(2,1)} %all-gather.12.cloned.1.call-done, bf16[24,8,6,128]{3,2,1,0:T(8,128)(2,1)S(1)} %bitcast.183), kind=kOutput, calls=%fused_computation.69 | convolution fusion | flops 906559488 | bytes 6193152 | tf_op jit(solution)/shard_map/tk,rk->tr/dot_general | solution.py:106
  193.9 18.6 %while.49 = (s32[]{:T(128)}, f32[192,6,128]{2,0,1:T(8,128)}, bf16[768,768]{0,1:T(8,128)(2,1)S(1)}, s32[]{:T(128)}, bf16[192,6,128]{2,0,1:T(8,128)(2,1)}, /*index...) while((s32[]{:T(128)}, f32[192,6,128]{2,0,1:T(8,128)}, ...), condition=%wide.region_7.8_spmd.clone, body=%wide.region_6.7_spmd.clone.sunk | while | flops 228852224 | bytes 7696129 | solution.py:166
  194.0 1.9 constant_dynamic-slice_fusion.13
  196.1 1.2 add_compare_fusion.7
  197.3 2.7 fusion.116
  200.0 1.9 constant_dynamic-slice_fusion.13
  202.2 1.2 add_compare_fusion.7
  203.4 2.9 fusion.116
  206.3 1.9 constant_dynamic-slice_fusion.13
  208.4 1.2 add_compare_fusion.7
  209.6 2.9 fusion.116
  212.5 1.3 convert_element_type.113
  214.0 1.1 convert_element_type.114
  215.2 7.7 %all-gather.4 = f32[4,192,6]{1,2,0:T(8,128)S(1)} all-gather(f32[1,192,6]{1,2,0:T(8,128)S(1)} %copy.88), channel_id=1, replica_groups=mesh['dp'=2,'seq'=4,'tensor'=4] {'seq'}, dimensions={0}, use_global_device_ids=true | all-gather | bytes 23040 | tf_op jit(solution)/shard_map/all_gather | solution.py:137
  222.9 0.7 reshape.127
  223.6 6.3 %reduce-scatter.5.cloned.1.call-done = bf16[768,768]{1,0:T(8,128)(2,1)} async-done(((bf16[3072,768]{1,0:T(8,128)(2,1)}), bf16[768,768]{1,0:T(8,128)(2,1)}) %reduce-scatter.5.cloned.1.call-update) | async-done | bytes 1179664 | tf_op jit(solution)/shard_map/reduce_scatter | solution.py:124
  229.9 29.4 %all-gather.22.cloned.1.call-done = bf16[1,768,768]{2,1,0:T(8,128)(2,1)} async-done(((bf16[1,192,768]{2,1,0:T(8,128)(2,1)}), bf16[1,768,768]{2,1,0:T(8,128)(2,1)}) %all-gather.22.cloned.1.call-update) | async-done | bytes 1179664 | tf_op jit(solution)/shard_map/all_gather | solution.py:167
  259.3 30.2 %all-gather.16.cloned.1.call-done = bf16[768,768]{1,0:T(8,128)(2,1)} async-done(((bf16[192,768]{1,0:T(8,128)(2,1)}), bf16[768,768]{1,0:T(8,128)(2,1)}) %all-gather.16.cloned.1.call-update) | async-done | bytes 1179664 | tf_op jit(solution)/shard_map/all_gather | solution.py:168
  289.4 20.7 %while.50 = (s32[]{:T(128)}, f32[192,6,128]{2,0,1:T(8,128)S(1)}, f32[192,6,128]{2,0,1:T(8,128)S(1)}, bf16[768,768]{1,0:T(8,128)(2,1)}, bf16[192,6,128]{2,0,1:T(8...) while((s32[]{:T(128)}, f32[192,6,128]{2,0,1:T(8,128)S(1)}, ...), condition=%wide.region_9.10_spmd.clone, body=%wide.region_8.9_spmd.clone.sunk | while | flops 304939392 | bytes 11244126 | solution.py:194
  289.4 1.2 constant_dynamic-slice_fusion.14
  290.8 1.3 constant_dynamic-slice_fusion.15
  292.8 1.3 fusion.124
  294.3 1.6 fusion.125
  296.4 1.2 constant_dynamic-slice_fusion.14
  297.7 1.3 constant_dynamic-slice_fusion.15
  299.7 1.3 fusion.124
  301.2 1.6 fusion.125
  303.3 1.2 constant_dynamic-slice_fusion.14
  304.6 1.3 constant_dynamic-slice_fusion.15
  306.6 1.3 fusion.124
  308.1 1.6 fusion.125
  310.4 1.1 convert_element_type.116
  311.8 1.1 convert_element_type.118
  312.8 8.1 %reduce-scatter.3.cloned.1.call-done = bf16[192,768]{1,0:T(8,128)(2,1)} async-done(((bf16[192,3072]{1,0:T(8,128)(2,1)}), bf16[192,768]{1,0:T(8,128)(2,1)}) %reduce-scatter.3.cloned.1.call-update) | async-done | bytes 294928 | tf_op jit(solution)/shard_map/reduce_scatter | solution.py:109
  321.0 1.8 fusion.50
  322.8 10.4 %psum.15 = f32[1,768]{1,0:T(1,128)} all-reduce(f32[1,768]{1,0:T(1,128)S(1)} %broadcast_in_dim.137), channel_id=1, replica_groups=mesh['dp'=2,'seq'=4,'tensor'=4] {'seq'}, use_global_device_ids=true, to_apply=%region_13.14 | all-reduce | flops 768 | bytes 6144 | tf_op jit(solution)/shard_map/psum | solution.py:118
  333.2 8.7 %all-reduce.2.cloned.1.call-done = bf16[768,768]{1,0:T(8,128)(2,1)} async-done(((bf16[768,768]{1,0:T(8,128)(2,1)}), bf16[768,768]{1,0:T(8,128)(2,1)}) %all-reduce.2.cloned.1.call-update) | async-done | bytes 1179664 | tf_op jit(solution)/shard_map/psum | solution.py:132
  341.9 2.8 convert_element_type.120
  (109 shorter events, 16.2 us)
Async XLA Ops:
  7.2 1.6 copy-start
  7.2 33.1 %all-gather.18.cloned.1.call-start = ((), (), s32[]{:S(2)}) async-start(), calls=%async_computation.8 | async-start | bytes 1474560 | tf_op jit(solution)/shard_map/all_gather | solution.py:67
  7.9 3.3 copy-start.10
  7.9 62.0 %all-gather.20.cloned.1.call-start = ((), (), s32[]{:S(2)}) async-start(), calls=%async_computation.9 | async-start | bytes 1474560 | tf_op jit(solution)/shard_map/all_gather | solution.py:68
  8.7 93.9 %all-gather.14.cloned.1.call-start = ((), (), s32[]{:S(2)}) async-start(), calls=%async_computation.4 | async-start | bytes 1474560 | tf_op jit(solution)/shard_map/all_gather | solution.py:120
  10.5 149.9 %all-gather.12.cloned.1.call-start = ((), (), s32[]{:S(2)}) async-start(), calls=%async_computation.2 | async-start | bytes 5898240 | tf_op jit(solution)/shard_map/all_gather | solution.py:105
  11.1 218.7 %reduce-scatter.5.cloned.1.call-start = ((), (), s32[]{:S(2)}) async-start(), calls=%async_computation.6 | async-start | bytes 5898240 | tf_op jit(solution)/shard_map/reduce_scatter | solution.py:124
  72.3 1.8 copy-start.2
  75.6 1.8 copy-start.2
  78.9 1.8 copy-start.2
  164.3 7.8 %copy-start.4 = (bf16[192,768]{1,0:T(8,128)(2,1)}, bf16[192,768]{1,0:T(8,128)(2,1)S(1)}, u32[]{:S(2)}) copy-start(bf16[192,768]{1,0:T(8,128)(2,1)S(1)} %convolution_convert_fusion.2) | copy-start | bytes 884740
  164.3 4.1 %copy-start.3 = (bf16[192,3072]{1,0:T(8,128)(2,1)S(1)}, bf16[192,3072]{1,0:T(8,128)(2,1)}, u32[]{:S(2)}) copy-start(bf16[192,3072]{1,0:T(8,128)(2,1)} %all-gather.14.cloned.1.call-done) | copy-start | bytes 3538948
  167.6 0.8 copy-start.6
  172.0 1.4 copy-start.9
  172.0 87.2 %all-gather.22.cloned.1.call-start = ((), (), s32[]{:S(2)}) async-start(), calls=%async_computation.10 | async-start | bytes 1474560 | tf_op jit(solution)/shard_map/all_gather | solution.py:167
  172.6 116.8 %all-gather.16.cloned.1.call-start = ((), (), s32[]{:S(2)}) async-start(), calls=%async_computation.5 | async-start | bytes 1474560 | tf_op jit(solution)/shard_map/all_gather | solution.py:168
  173.4 147.6 %reduce-scatter.3.cloned.1.call-start = ((), (), s32[]{:S(2)}) async-start(), calls=%async_computation.3 | async-start | bytes 1474560 | tf_op jit(solution)/shard_map/reduce_scatter | solution.py:109
  173.8 14.1 %copy-start.5 = (bf16[192,768]{1,0:T(8,128)(2,1)S(1)}, bf16[192,768]{1,0:T(8,128)(2,1)}, u32[]{:S(2)}) copy-start(bf16[192,768]{1,0:T(8,128)(2,1)} %copy-done.4) | copy-start | bytes 884740
  175.9 12.7 %copy-start.7 = (bf16[192,6,128]{2,1,0:T(8,128)(2,1)S(1)}, bf16[192,6,128]{2,1,0:T(8,128)(2,1)}, u32[]{:S(2)}) copy-start(bf16[192,6,128]{2,1,0:T(8,128)(2,1)} %copy-done.6) | copy-start | bytes 884740
  193.9 148.0 %all-reduce.2.cloned.1.call-start = ((), (), s32[]{:S(2)}) async-start(), calls=%async_computation.7 | async-start | bytes 2359296 | tf_op jit(solution)/shard_map/psum | solution.py:132
  193.9 1.9 copy-start.1
  194.0 1.9 copy-start.12
  200.0 1.9 copy-start.1
  200.0 1.9 copy-start.12
  206.3 1.9 copy-start.1
  206.3 1.9 copy-start.12
  212.5 2.6 copy-start.11
  311.5 9.5 %copy-start.8 = (bf16[1,192,768]{2,1,0:T(8,128)(2,1)S(1)}, bf16[1,192,768]{2,1,0:T(8,128)(2,1)}, u32[]{:S(2)}) copy-start(bf16[1,192,768]{2,1,0:T(8,128)(2,1)} %param.19) | copy-start | bytes 884740
Sparse Core Ops, SparseCore 0:
  9.9 30.4 all-gather.17
  42.2 27.7 all-gather.19
  72.1 30.4 all-gather.13
  104.2 56.1 all-gather.11
  172.2 57.6 reduce-scatter.4
  231.5 27.7 all-gather.21
  261.7 27.7 all-gather.15
  291.8 29.1 reduce-scatter.2
  323.3 18.5 all-reduce.1
where the time goes:
time: 352 us; the launch traced here: 351 us
  waiting for transfers between devices  220 us (62%)
  local copies, waits for them, and re-layouts  35.3 us (10%)
  matrix products  35.1 us (10%)
  blocking collectives  26.4 us (8%)
  other arithmetic  19.6 us (6%)
  between operations  14.1 us (4%)
    all_gather x1, waiting for transfers between devices, shards(): weight_whole = lax.all_gather(out_weight, 'seq', axis=0, tiled=True)  57.9 us
    all_gather x1, waiting for transfers between devices, shards(): grad_piece = lax.all_gather(grad_att, 'seq', axis=0, tiled=True)  30.2 us
    all_gather x1, waiting for transfers between devices, shards(): query_piece = lax.all_gather(query_local, 'seq', axis=0, tiled=True)  29.4 us
    all_gather x1, waiting for transfers between devices, shards(): key_piece = lax.all_gather(key_local, 'seq', axis=0, tiled=True)  28 us
    all_gather x1, waiting for transfers between devices, shards(): value_piece = lax.all_gather(value_local, 'seq', axis=0, tiled=True)  28 us
    all_gather x1, waiting for transfers between devices, shards(): grad_full = lax.all_gather(grad_proj, 'tensor', axis=1, tiled=True)  20.2 us
    unnamed x30, local copies, waits for them, and re-layouts  10.8 us
    psum x1, blocking collectives, shards(): gate_grad = lax.psum(jnp.sum(cot_rows * projected, axis=0), 'seq')  10.4 us
  transfers between devices with their start and end apart: 9, of which 9 were waited for; matrix products, arithmetic and copies ran while one was open for 22% of the time, Pallas kernels for 0%

commit v1 on v0

--- a/solution.py
+++ b/solution.py
@@ -1,8 +1,11 @@
+import functools
 import math
 
 import jax
 import jax.numpy as jnp
 from jax import lax
+from jax.experimental import pallas as pl
+from jax.experimental.pallas import tpu as pltpu
 from jax.sharding import PartitionSpec as P
 
 HD = 128
@@ -49,7 +52,7 @@
     return (key_part, value_part)
 
 
-def shards(query_rows, key_rows, value_rows, lengths, out_weight, gate_vector, cotangent):
+def general_shards(query_rows, key_rows, value_rows, lengths, out_weight, gate_vector, cotangent):
     tokens = query_rows.shape[1]
     local_width = query_rows.shape[2]
     head_count = local_width // HD
@@ -207,6 +210,331 @@
     )
 
 
+VMEM_LIMIT = 40 * 1024 * 1024
+NT = (((1,), (1,)), ((), ()))
+TN = (((0,), (0,)), ((), ()))
+NN = (((1,), (0,)), ((), ()))
+
+
+def mm(left, right, dims):
+    return lax.dot_general(left, right, dims, preferred_element_type=jnp.float32)
+
+
+def lane_block(index, width):
+    return pl.ds(pl.multiple_of(index * width, HD), width)
+
+
+def call(kernel, out_shape, args, flops=0, smem=(), scratch=()):
+    nbytes = sum(a.size * a.dtype.itemsize for a in args)
+    nbytes += sum(math.prod(o.shape) * o.dtype.itemsize for o in jax.tree.leaves(out_shape))
+    return pl.pallas_call(
+        kernel,
+        out_shape=out_shape,
+        in_specs=[
+            pl.BlockSpec(memory_space=pltpu.SMEM if i in smem else pltpu.VMEM)
+            for i in range(len(args))
+        ],
+        out_specs=jax.tree.map(lambda _: pl.BlockSpec(memory_space=pltpu.VMEM), out_shape),
+        scratch_shapes=list(scratch),
+        compiler_params=pltpu.CompilerParams(vmem_limit_bytes=VMEM_LIMIT),
+        cost_estimate=pl.CostEstimate(flops=flops, bytes_accessed=nbytes, transcendentals=0),
+    )(*args)
+
+
+def xor_pairs(count, k):
+    return [(i, i ^ k) for i in range(count)]
+
+
+def pack_kernel(n, q_ref, k_ref, v_ref, *out_refs):
+    s = lax.axis_index("seq")
+    half = q_ref.shape[1] // 2
+    for k in range(n):
+        j = s ^ k
+        own = lane_block(j, HD)
+        shared = lane_block(n + j // 2, HD)
+        out = out_refs[k]
+        for i in range(2):
+            rows = slice(i * half, (i + 1) * half)
+            out[i] = k_ref[0, rows, own]
+            out[2 + i] = k_ref[0, rows, shared]
+            out[4 + i] = v_ref[0, rows, own]
+            out[6 + i] = v_ref[0, rows, shared]
+            out[8 + i] = q_ref[0, rows, own]
+        out[10] = q_ref[0, pl.ds(pl.multiple_of((j % 2) * half, half), half), shared]
+
+
+def rows_of(packs, first):
+    return jnp.concatenate([p[first + i] for p in packs for i in range(2)], axis=0)
+
+
+def unit_queries(packs, unit):
+    if unit < 2:
+        return rows_of(packs[2 * unit : 2 * unit + 2], 8)
+    return jnp.concatenate([p[10] for p in packs], axis=0)
+
+
+def live_bias(s, n, rows, length):
+    parts = []
+    for k in range(n):
+        place = (s ^ k) * rows + lax.broadcasted_iota(jnp.int32, (rows, 1), 0)
+        parts.append(jnp.where(place < length, 0.0, MASKED_SCORE))
+    return jnp.concatenate(parts, axis=0)
+
+
+def forward_kernel(n, scale, len_ref, *refs):
+    packs, (o_ref, lse_ref) = refs[:n], refs[n:]
+    s, t = lax.axis_index("seq"), lax.axis_index("tensor")
+    half = packs[0].shape[1]
+    bias = live_bias(s, n, 2 * half, len_ref[0])
+    for unit in range(3):
+        keys = rows_of(packs, 0 if unit < 2 else 2)
+        values = rows_of(packs, 4 if unit < 2 else 6)
+        scores = mm(keys, unit_queries(packs, unit), NT) * scale + bias
+        top = jnp.max(scores, axis=0, keepdims=True)
+        weights = jnp.exp(scores - top)
+        total = jnp.sum(weights, axis=0, keepdims=True)
+        summed = mm(values, weights.astype(jnp.bfloat16), TN)
+        attended = (summed / total).T.astype(jnp.bfloat16)
+        lse_ref[unit : unit + 1, :] = top + jnp.log(total)
+        if unit < 2:
+            for i in range(2):
+                slot = (s ^ (2 * unit + i)) ^ t
+                for h in range(2):
+                    at = (2 * i + h) * half
+                    o_ref[slot, h] = attended[at : at + half]
+        else:
+            for k in range(n):
+                o_ref[(s ^ k) ^ t, 2] = attended[k * half : (k + 1) * half]
+
+
+def grad_attended_kernel(n, gate_ref, w_ref, *refs):
+    cots, (gp_ref, *out_refs) = refs[:n], refs[n:]
+    s = lax.axis_index("seq")
+    rows = cots[0].shape[1]
+    half = rows // 2
+    gate = gate_ref[:, lane_block(s, w_ref.shape[0])]
+    for i in range(n):
+        gp_ref[i * rows : (i + 1) * rows, :] = (gate * cots[i][0].astype(jnp.float32)).astype(
+            jnp.bfloat16
+        )
+    full = mm(gp_ref[...], w_ref[...], NN).astype(jnp.bfloat16)
+    share = refs[-1]
+    share[...] = full
+    for k in range(n):
+        j = s ^ k
+        own = lane_block(j, HD)
+        shared = lane_block(n + j // 2, HD)
+        out = out_refs[k]
+        for i in range(n):
+            for h in range(2):
+                out[i, h] = share[i * rows + h * half : i * rows + (h + 1) * half, own]
+            out[i, 2] = share[pl.ds(pl.multiple_of(i * rows + (j % 2) * half, half), half), shared]
+
+
+def backward_kernel(n, scale, len_ref, lse_ref, o_ref, *refs):
+    packs, grads, outs = refs[:n], refs[n : 2 * n], refs[2 * n :]
+    s, t = lax.axis_index("seq"), lax.axis_index("tensor")
+    half = packs[0].shape[1]
+    bias = live_bias(s, n, 2 * half, len_ref[0])
+
+    def grad_tile(slot, tile):
+        total = grads[0][slot, tile].astype(jnp.float32)
+        for g in grads[1:]:
+            total = total + g[slot, tile].astype(jnp.float32)
+        return total.astype(jnp.bfloat16)
+
+    for head in range(2):
+        units = (0, 1) if head == 0 else (2,)
+        keys = rows_of(packs, 2 * head)
+        values = rows_of(packs, 4 + 2 * head)
+        keys_t = keys.T
+        grad_keys = grad_values = None
+        for unit in units:
+            queries = unit_queries(packs, unit)
+            if unit < 2:
+                tiles = [((s ^ (2 * unit + i)) ^ t, h) for i in range(2) for h in range(2)]
+            else:
+                tiles = [((s ^ k) ^ t, 2) for k in range(n)]
+            grad = jnp.concatenate([grad_tile(*tile) for tile in tiles], axis=0)
+            attended = jnp.concatenate([o_ref[slot, tile] for slot, tile in tiles], axis=0)
+            product = grad.astype(jnp.float32) * attended.astype(jnp.float32)
+            delta = jnp.sum(product.T, axis=0, keepdims=True)
+            scores = mm(keys, queries, NT) * scale + bias
+            probs = jnp.exp(scores - lse_ref[unit : unit + 1, :])
+            grad_probs = mm(values, grad, NT)
+            dscores = (probs * (grad_probs - delta) * scale).astype(jnp.bfloat16)
+            value_part = mm(probs.astype(jnp.bfloat16), grad, NN)
+            key_part = mm(dscores, queries, NN)
+            grad_values = value_part if grad_values is None else grad_values + value_part
+            grad_keys = key_part if grad_keys is None else grad_keys + key_part
+            grad_query = mm(keys_t, dscores, NN).T.astype(jnp.bfloat16)
+            if unit < 2:
+                for i in range(2):
+                    for h in range(2):
+                        at = (2 * i + h) * half
+                        outs[2 * unit + i][8 + h] = grad_query[at : at + half]
+            else:
+                for k in range(n):
+                    outs[k][10] = grad_query[k * half : (k + 1) * half]
+        for k in range(n):
+            for h in range(2):
+                rows = slice((2 * k + h) * half, (2 * k + h + 1) * half)
+                outs[k][2 * head + h] = grad_keys[rows].astype(jnp.bfloat16)
+                outs[k][4 + 2 * head + h] = grad_values[rows].astype(jnp.bfloat16)
+
+
+def unpack_kernel(n, *refs):
+    packs, (dq_ref, dk_ref, dv_ref) = refs[:n], refs[n:]
+    s = lax.axis_index("seq")
+    half = packs[0].shape[1]
+    for k in range(n):
+        own = lane_block(s ^ k, HD)
+        for h in range(2):
+            rows = slice(h * half, (h + 1) * half)
+            dk_ref[0, rows, own] = packs[k][h]
+            dv_ref[0, rows, own] = packs[k][4 + h]
+            dq_ref[0, rows, own] = packs[k][8 + h]
+    for pair in range(0, n, 2):
+        shared = lane_block(n + (s ^ pair) // 2, HD)
+        for h in range(2):
+            rows = slice(h * half, (h + 1) * half)
+            for first, ref in ((2, dk_ref), (6, dv_ref)):
+                total = packs[pair][first + h].astype(jnp.float32)
+                total = total + packs[pair + 1][first + h].astype(jnp.float32)
+                ref[0, rows, shared] = total.astype(jnp.bfloat16)
+        for k in (pair, pair + 1):
+            rows = pl.ds(pl.multiple_of(((s ^ k) % 2) * half, half), half)
+            dq_ref[0, rows, shared] = packs[k][10]
+
+
+def project_kernel(n, w_ref, *refs):
+    packs, (own_ref, *send_refs), all_ref = refs[:n], refs[n : 2 * n], refs[2 * n]
+    s = lax.axis_index("seq")
+    half = packs[0].shape[2]
+    rows = 2 * half
+    for k in range(n):
+        j = s ^ k
+        own = lane_block(j, HD)
+        shared = lane_block(n + j // 2, HD)
+        for i in range(n):
+            for h in range(2):
+                at = i * rows + h * half
+                all_ref[at : at + half, own] = packs[k][i, h]
+            at = pl.multiple_of(i * rows + (j % 2) * half, half)
+            all_ref[pl.ds(at, half), shared] = packs[k][i, 2]
+    weight = w_ref[...]
+    for i in range(n):
+        part = mm(all_ref[i * rows : (i + 1) * rows, :], weight, NT)
+        if i == 0:
+            own_ref[...] = part
+        else:
+            send_refs[i - 1][...] = part.astype(jnp.bfloat16)
+
+
+def grad_weight_kernel(gp_ref, all_ref, out_ref):
+    out_ref[...] = mm(gp_ref[...], all_ref[...], TN).astype(jnp.bfloat16)
+
+
+def branch_kernel(n, gate_ref, cot_ref, own_ref, *refs):
+    parts, (branch_ref, gate_grad_ref) = refs[: n - 1], refs[n - 1 :]
+    s = lax.axis_index("seq")
+    projected = own_ref[...]
+    for part in parts:
+        projected = projected + part[...].astype(jnp.float32)
+    gate = gate_ref[:, lane_block(s, projected.shape[1])]
+    branch_ref[0] = (gate * projected).astype(jnp.bfloat16)
+    gate_grad_ref[...] = jnp.sum(cot_ref[0].astype(jnp.float32) * projected, axis=0, keepdims=True)
+
+
+def square_shards(
+    n, query_rows, key_rows, value_rows, lengths, out_weight, gate_vector, cotangent
+):
+    tokens, width = query_rows.shape[1:]
+    half = tokens // 2
+    scale = 1.0 / math.sqrt(HD)
+    bf16, f32 = jnp.bfloat16, jnp.float32
+    shape = jax.ShapeDtypeStruct
+    both = ("seq", "tensor")
+
+    cots = [
+        lax.ppermute(
+            cotangent,
+            both,
+            [(a * n + b, b * n + (a ^ k)) for a in range(n) for b in range(n)],
+        )
+        for k in range(n)
+    ]
+    packs = call(
+        functools.partial(pack_kernel, n),
+        [shape((11, half, HD), bf16)] * n,
+        (query_rows, key_rows, value_rows),
+    )
+    packs = [packs[0]] + [lax.ppermute(packs[k], "seq", xor_pairs(n, k)) for k in range(1, n)]
+    unit_flops = 2 * n * tokens * 2 * tokens * HD
+    attended, lse = call(
+        functools.partial(forward_kernel, n, scale),
+        [shape((n, 3, half, HD), bf16), shape((3, 2 * tokens), f32)],
+        (lengths, *packs),
+        flops=6 * unit_flops,
+        smem=(0,),
+    )
+    heads = [attended] + [lax.ppermute(attended, "seq", xor_pairs(n, k)) for k in range(1, n)]
+    grad_proj, *grads = call(
+        functools.partial(grad_attended_kernel, n),
+        [shape((n * tokens, width), bf16)] + [shape((n, 3, half, HD), bf16)] * n,
+        (gate_vector, out_weight, *cots),
+        flops=2 * n * tokens * width * width,
+        scratch=[pltpu.VMEM((n * tokens, width), bf16)],
+    )
+    grads = [grads[0]] + [lax.ppermute(grads[k], "seq", xor_pairs(n, k)) for k in range(1, n)]
+    *parts, attended_all = call(
+        functools.partial(project_kernel, n),
+        [shape((tokens, width), f32)]
+        + [shape((tokens, width), bf16)] * (n - 1)
+        + [shape((n * tokens, width), bf16)],
+        (out_weight, *heads),
+        flops=2 * n * tokens * width * width,
+    )
+    parts = [parts[0]] + [lax.ppermute(parts[k], "tensor", xor_pairs(n, k)) for k in range(1, n)]
+    weight_part = call(
+        grad_weight_kernel,
+        shape((width, width), bf16),
+        (grad_proj, attended_all),
+        flops=2 * n * tokens * width * width,
+    )
+    other_part = lax.ppermute(weight_part, "dp", xor_pairs(2, 1))
+    grad_weight = weight_part.astype(f32) + other_part.astype(f32)
+    outs = call(
+        functools.partial(backward_kernel, n, scale),
+        [shape((11, half, HD), bf16)] * n,
+        (lengths, lse, attended, *packs, *grads),
+        flops=15 * unit_flops,
+        smem=(0,),
+    )
+    outs = [outs[0]] + [lax.ppermute(outs[k], "seq", xor_pairs(n, k)) for k in range(1, n)]
+    branch, gate_part = call(
+        functools.partial(branch_kernel, n),
+        [shape((1, tokens, width), bf16), shape((1, width), f32)],
+        (gate_vector, cots[0], *parts),
+    )
+    branch = lax.ppermute(
+        branch, both, [(a * n + b, b * n + a) for a in range(n) for b in range(n)]
+    )
+    gates = [
+        lax.ppermute(
+            gate_part, both, [(a * n + b, (b ^ k) * n + a) for a in range(n) for b in range(n)]
+        )
+        for k in range(n)
+    ]
+    grad_gate = (gates[0] + gates[1]) + (gates[2] + gates[3])
+    grad_query, grad_key, grad_value = call(
+        functools.partial(unpack_kernel, n),
+        [shape((1, tokens, width), bf16)] * 3,
+        tuple(outs),
+    )
+    return (branch, grad_query, grad_key, grad_value, grad_weight, grad_gate)
+
+
 def solution(mesh):
     placed = (
         P("dp", "seq", "tensor"),
@@ -217,8 +545,23 @@
         P("dp", None),
         P("dp", "seq", "tensor"),
     )
+    n = mesh.shape["seq"]
+
+    def body(query_rows, *rest):
+        tokens, width = query_rows.shape[1:]
+        square = (
+            n == 4
+            and mesh.shape["tensor"] == n
+            and mesh.shape["dp"] == 2
+            and width == (n + n // 2) * HD
+            and tokens % 64 == 0
+        )
+        if square:
+            return square_shards(n, query_rows, *rest)
+        return general_shards(query_rows, *rest)
+
     return jax.shard_map(
-        shards,
+        body,
         mesh=mesh,
         in_specs=placed,
         out_specs=(

time: 352 us -> 125 us (0.36)
  the two profiles are of different devices: /device:TPU:0 before, /device:TPU:4 now
where the time goes in v1:
time: 125 us
  starting transfers between devices  53.7 us (43%)
  waiting for transfers between devices  53.4 us (43%)
  Pallas kernels  10.7 us (9%)
  local copies, waits for them, and re-layouts  3.6 us (3%)
  other arithmetic  2.24 us (2%)
  between operations  1.42 us (1%)
    ppermute x4, waiting for transfers between devices, square_shards(): lax.ppermute(gate_part, both, [(a * n + b, (b ^ k) * n + a) for a in rang...  18 us
    ppermute x3, starting transfers between devices, square_shards(): lax.ppermute(attended, 'seq', xor_pairs(n, k))  13.8 us
    ppermute x4, starting transfers between devices, square_shards(): lax.ppermute(cotangent, both, [(a * n + b, b * n + (a ^ k)) for a in rang...  13.7 us
    ppermute x3, waiting for transfers between devices, square_shards(): lax.ppermute(grads[k], 'seq', xor_pairs(n, k))  11.7 us
    ppermute x3, waiting for transfers between devices, square_shards(): lax.ppermute(parts[k], 'tensor', xor_pairs(n, k))  11.1 us
    pallas_call x8, Pallas kernels, call(): pl.pallas_call(kernel, out_shape=out_shape, in_specs=[pl.BlockSpec(memory...  10.7 us
    ppermute x3, waiting for transfers between devices, square_shards(): lax.ppermute(attended, 'seq', xor_pairs(n, k))  9.4 us
    ppermute x4, starting transfers between devices, square_shards(): lax.ppermute(gate_part, both, [(a * n + b, (b ^ k) * n + a) for a in rang...  7.25 us
  transfers between devices with their start and end apart: 25, of which 9 were waited for; matrix products, arithmetic and copies ran while one was open for 0% of the time, Pallas kernels for 6%

profile of v1, /device:TPU:4, one launch (start us, length us, event | category | flops | bytes accessed | tf_op | source)
XLA Modules:
  0.0 125.0 jit_solution(17223248990470293282)
XLA Ops:
  0.6 1.0 copy-done
  1.6 1.0 copy-done.1
  2.6 1.0 copy-done.2
  3.5 0.2 shard_map.118
  3.7 1.6 %collective-permute-start.1 = (bf16[11,96,128]{2,1,0:T(8,128)(2,1)S(1)}, bf16[11,96,128]{2,1,0:T(8,128)(2,1)S(1)}, u32[]{:S(2)}, u32[]{:S(2)}) collective-permute-start(bf16[11,96,128]{2,1,0:T(8,128)(2,1)S(1)} %get-tuple-element.32), channel_id=1, source_target_pairs={{0,4},{4,0},{8,12},{12,8},{1,5},{5,1},{9,13},{13,9},{2,6},{6,2},{1... | collective-permute-start | bytes 811016 | tf_op jit(solution)/shard_map/ppermute | solution.py:472
  5.3 0.5 collective-permute-start.2
  5.8 1.5 %collective-permute-start.3 = (bf16[11,96,128]{2,1,0:T(8,128)(2,1)S(1)}, bf16[11,96,128]{2,1,0:T(8,128)(2,1)S(1)}, u32[]{:S(2)}, u32[]{:S(2)}) collective-permute-start(bf16[11,96,128]{2,1,0:T(8,128)(2,1)S(1)} %get-tuple-element.34), channel_id=1, source_target_pairs={{0,12},{4,8},{8,4},{12,0},{1,13},{5,9},{9,5},{13,1},{2,14},{6,10},... | collective-permute-start | bytes 811016 | tf_op jit(solution)/shard_map/ppermute | solution.py:472
  7.3 3.5 %collective-permute-start.11 = (bf16[1,192,768]{2,1,0:T(8,128)(2,1)}, bf16[1,192,768]{2,1,0:T(8,128)(2,1)S(1)}, u32[]{:S(2)}, u32[]{:S(2)}) collective-permute-start(bf16[1,192,768]{2,1,0:T(8,128)(2,1)} %param.13), channel_id=1, source_target_pairs={{0,1},{1,5},{2,9},{3,13},{4,0},{5,4},{6,8},{7,12},{8,3},{9,7},{10,... | collective-permute-start | bytes 884744 | tf_op jit(solution)/shard_map/ppermute | solution.py:460
  10.8 2.3 %collective-permute-start = (bf16[1,192,768]{2,1,0:T(8,128)(2,1)}, bf16[1,192,768]{2,1,0:T(8,128)(2,1)S(1)}, u32[]{:S(2)}, u32[]{:S(2)}) collective-permute-start(bf16[1,192,768]{2,1,0:T(8,128)(2,1)} %param.13), channel_id=1, source_target_pairs={{0,0},{1,4},{2,8},{3,12},{4,1},{5,5},{6,9},{7,13},{8,2},{9,6},{10,... | collective-permute-start | bytes 884744 | tf_op jit(solution)/shard_map/ppermute | solution.py:460
  13.1 0.0 collective-permute-done.1.refs_1_
  13.2 7.9 %collective-permute-start.13 = (bf16[1,192,768]{2,1,0:T(8,128)(2,1)}, bf16[1,192,768]{2,1,0:T(8,128)(2,1)S(1)}, u32[]{:S(2)}, u32[]{:S(2)}) collective-permute-start(bf16[1,192,768]{2,1,0:T(8,128)(2,1)} %param.13), channel_id=1, source_target_pairs={{0,3},{1,7},{2,11},{3,15},{4,2},{5,6},{6,10},{7,14},{8,1},{9,5},{1... | collective-permute-start | bytes 884744 | tf_op jit(solution)/shard_map/ppermute | solution.py:460
  21.0 0.0 collective-permute-done.2.refs_2_
  21.0 0.0 collective-permute-start.12
  21.7 0.0 collective-permute-done.3.refs_3_
  21.7 2.0 %shard_map.119 = (bf16[4,3,96,128]{3,2,1,0:T(8,128)(2,1)S(1)}, f32[3,384]{1,0:T(4,128)S(1)}) custom-call(s32[1]{0:T(128)S(6)} %copy.14.len_ref, bf16[11,96,128]{2,1,0:T(8,128)(2,1)S(1)} %get-tuple-element.31.refs_0_, bf16[11,96,128]{2,1,0:T(8,128)(2,1)S(1)} %collective-permute-done.1.refs_1_, bf16[11,96,128]{2,1,0:T(8,128)(2,1)S(1)} %collective-permute-done.2.refs_2_, ...), custom_call_target="tpu_custom_call" | custom-call | flops 452984832 | bytes 1380868 | tf_op jit(solution)/shard_map/pallas_call | solution.py:230
  23.7 11.1 %collective-permute-start.6 = (bf16[4,3,96,128]{3,2,1,0:T(8,128)(2,1)S(1)}, bf16[4,3,96,128]{3,2,1,0:T(8,128)(2,1)S(1)}, u32[]{:S(2)}, u32[]{:S(2)}) collective-permute-start(bf16[4,3,96,128]{3,2,1,0:T(8,128)(2,1)S(1)} %get-tuple-element.35.refs_0_.o_ref), channel_id=1, source_target_pairs={{0,12},{4,8},{8,4},{12,0},{1,13},{5,9},{9,5},{13,1},{2,14},{6,10},... | collective-permute-start | bytes 884744 | tf_op jit(solution)/shard_map/ppermute | solution.py:481
  34.8 0.0 collective-permute-done.11.refs_1_
  34.8 2.8 %collective-permute-start.5 = (bf16[4,3,96,128]{3,2,1,0:T(8,128)(2,1)S(1)}, bf16[4,3,96,128]{3,2,1,0:T(8,128)(2,1)S(1)}, u32[]{:S(2)}, u32[]{:S(2)}) collective-permute-start(bf16[4,3,96,128]{3,2,1,0:T(8,128)(2,1)S(1)} %get-tuple-element.35.refs_0_.o_ref), channel_id=1, source_target_pairs={{0,8},{4,12},{8,0},{12,4},{1,9},{5,13},{9,1},{13,5},{2,10},{6,14},... | collective-permute-start | bytes 884744 | tf_op jit(solution)/shard_map/ppermute | solution.py:481
  37.6 3.1 %collective-permute-done.cot_ref.refs_0_ = bf16[1,192,768]{2,1,0:T(8,128)(2,1)S(1)} collective-permute-done((bf16[1,192,768]{2,1,0:T(8,128)(2,1)}, bf16[1,192,768]{2,1,0:T(8,128)(2,1)S(1)}, u32[]{:S(2)}, u32[]{:S(2)}) %collective-permute-start) | collective-permute-done | bytes 294944 | tf_op jit(solution)/shard_map/ppermute | solution.py:460
  40.7 0.0 collective-permute-start.4
  40.7 0.0 collective-permute-done.13.refs_3_
  40.7 0.0 collective-permute-done.12.refs_2_
  40.8 1.4 %shard_map.122 = (bf16[768,768]{1,0:T(8,128)(2,1)S(1)}, bf16[4,3,96,128]{3,2,1,0:T(8,128)(2,1)S(1)}, bf16[4,3,96,128]{3,2,1,0:T(8,128)(2,1)S(1)}, bf16[4,3,96,12...) custom-call(f32[1,3072]{1,0:T(1,128)S(1)} %copy-done.3, bf16[768,768]{1,0:T(8,128)(2,1)S(1)} %copy-done.4, ...), custom_call_target="tpu_custom_call" | custom-call | flops 905969664 | bytes 4730880 | tf_op jit(solution)/shard_map/pallas_call | solution.py:230
  42.2 5.7 %collective-permute-done.6.refs_3_ = bf16[4,3,96,128]{3,2,1,0:T(8,128)(2,1)S(1)} collective-permute-done((bf16[4,3,96,128]{3,2,1,0:T(8,128)(2,1)S(1)}, bf16[4,3,96,128]{3,2,1,0:T(8,128)(2,1)S(1)}, u32[]{:S(2)}, u32[]{:S(2)}) %collective-permute-start.6) | collective-permute-done | bytes 294944 | tf_op jit(solution)/shard_map/ppermute | solution.py:481
  47.9 0.9 collective-permute-done.5.refs_2_
  48.7 2.8 %collective-permute-done.4.refs_1_ = bf16[4,3,96,128]{3,2,1,0:T(8,128)(2,1)S(1)} collective-permute-done((bf16[4,3,96,128]{3,2,1,0:T(8,128)(2,1)S(1)}, bf16[4,3,96,128]{3,2,1,0:T(8,128)(2,1)S(1)}, u32[]{:S(2)}, u32[]{:S(2)}) %collective-permute-start.4) | collective-permute-done | bytes 294944 | tf_op jit(solution)/shard_map/ppermute | solution.py:481
  51.6 1.8 %shard_map.120 = (f32[192,768]{1,0:T(8,128)S(1)}, bf16[192,768]{1,0:T(8,128)(2,1)S(1)}, bf16[192,768]{1,0:T(8,128)(2,1)S(1)}, bf16[192,768]{1,0:T(8,128)(2,1)S(1)}, bf16[768,768]{1,0:T(8,128)(2,1)S(1)}) custom-call(bf16[768,768]{1,0:T(8,128)(2,1)S(1)} %copy-done.4, bf16[4,3,96,128]{3,2,1,0:T(8,128)(2,1)S(1)} %get-tuple-element.35.refs_0_.o_ref, ...), custom_call_target="tpu_custom_call" | custom-call | flops 905969664 | bytes 5013504 | tf_op jit(solution)/shard_map/pallas_call | solution.py:230
  53.4 1.1 shard_map.125
  54.5 0.1 collective-permute-start.20
  54.6 2.5 %collective-permute-start.14 = (bf16[4,3,96,128]{3,2,1,0:T(8,128)(2,1)S(1)}, bf16[4,3,96,128]{3,2,1,0:T(8,128)(2,1)S(1)}, u32[]{:S(2)}, u32[]{:S(2)}) collective-permute-start(bf16[4,3,96,128]{3,2,1,0:T(8,128)(2,1)S(1)} %get-tuple-element.43), channel_id=1, source_target_pairs={{0,4},{4,0},{8,12},{12,8},{1,5},{5,1},{9,13},{13,9},{2,6},{6,2},{1... | collective-permute-start | bytes 884744 | tf_op jit(solution)/shard_map/ppermute | solution.py:489
  57.2 0.0 collective-permute-start.15
  57.2 1.5 %collective-permute-start.16 = (bf16[4,3,96,128]{3,2,1,0:T(8,128)(2,1)S(1)}, bf16[4,3,96,128]{3,2,1,0:T(8,128)(2,1)S(1)}, u32[]{:S(2)}, u32[]{:S(2)}) collective-permute-start(bf16[4,3,96,128]{3,2,1,0:T(8,128)(2,1)S(1)} %get-tuple-element.45), channel_id=1, source_target_pairs={{0,12},{4,8},{8,4},{12,0},{1,13},{5,9},{9,5},{13,1},{2,14},{6,10},... | collective-permute-start | bytes 884744 | tf_op jit(solution)/shard_map/ppermute | solution.py:489
  58.7 2.2 %collective-permute-start.7 = (bf16[192,768]{1,0:T(8,128)(2,1)S(1)}, bf16[192,768]{1,0:T(8,128)(2,1)S(1)}, u32[]{:S(2)}, u32[]{:S(2)}) collective-permute-start(bf16[192,768]{1,0:T(8,128)(2,1)S(1)} %get-tuple-element.37), channel_id=1, source_target_pairs={{0,1},{1,0},{2,3},{3,2},{4,5},{5,4},{6,7},{7,6},{8,9},{9,8},{10,11... | collective-permute-start | bytes 884744 | tf_op jit(solution)/shard_map/ppermute | solution.py:498
  60.9 4.1 %collective-permute-done.14.refs_5_ = bf16[4,3,96,128]{3,2,1,0:T(8,128)(2,1)S(1)} collective-permute-done((bf16[4,3,96,128]{3,2,1,0:T(8,128)(2,1)S(1)}, bf16[4,3,96,128]{3,2,1,0:T(8,128)(2,1)S(1)}, u32[]{:S(2)}, u32[]{:S(2)}) %collective-permute-start.14) | collective-permute-done | bytes 294944 | tf_op jit(solution)/shard_map/ppermute | solution.py:489
  65.0 0.0 collective-permute-start.8
  65.0 7.5 %collective-permute-done.15.refs_6_ = bf16[4,3,96,128]{3,2,1,0:T(8,128)(2,1)S(1)} collective-permute-done((bf16[4,3,96,128]{3,2,1,0:T(8,128)(2,1)S(1)}, bf16[4,3,96,128]{3,2,1,0:T(8,128)(2,1)S(1)}, u32[]{:S(2)}, u32[]{:S(2)}) %collective-permute-start.15) | collective-permute-done | bytes 294944 | tf_op jit(solution)/shard_map/ppermute | solution.py:489
  72.6 0.0 collective-permute-start.9
  72.6 0.0 collective-permute-done.16.refs_7_
  72.6 2.8 %shard_map.123 = (bf16[11,96,128]{2,1,0:T(8,128)(2,1)S(1)}, bf16[11,96,128]{2,1,0:T(8,128)(2,1)S(1)}, bf16[11,96,128]{2,1,0:T(8,128)(2,1)S(1)}, bf16[11,96,128]{2,1,0:T(8,128)(2,1)S(1)}) custom-call(s32[1]{0:T(128)S(6)} %copy.14.len_ref, f32[3,384]{1,0:T(4,128)S(1)} %get-tuple-element.41.lse_ref, ...), custom_call_target="tpu_custom_call" | custom-call | flops 1132462080 | bytes 3641860 | tf_op jit(solution)/shard_map/pallas_call | solution.py:230
  75.4 0.3 collective-permute-start.17
  75.7 0.0 collective-permute-done.7.refs_0_
  75.7 1.7 %collective-permute-start.18 = (bf16[11,96,128]{2,1,0:T(8,128)(2,1)S(1)}, bf16[11,96,128]{2,1,0:T(8,128)(2,1)S(1)}, u32[]{:S(2)}, u32[]{:S(2)}) collective-permute-start(bf16[11,96,128]{2,1,0:T(8,128)(2,1)S(1)} %get-tuple-element.48), channel_id=1, source_target_pairs={{0,8},{4,12},{8,0},{12,4},{1,9},{5,13},{9,1},{13,5},{2,10},{6,14},... | collective-permute-start | bytes 811016 | tf_op jit(solution)/shard_map/ppermute | solution.py:514
  77.4 11.1 %collective-permute-done.8.refs_1_ = bf16[192,768]{1,0:T(8,128)(2,1)S(1)} collective-permute-done((bf16[192,768]{1,0:T(8,128)(2,1)S(1)}, bf16[192,768]{1,0:T(8,128)(2,1)S(1)}, u32[]{:S(2)}, u32[]{:S(2)}) %collective-permute-start.8) | collective-permute-done | bytes 294944 | tf_op jit(solution)/shard_map/ppermute | solution.py:498
  88.5 0.8 collective-permute-start.19
  89.3 0.0 collective-permute-done.9.refs_2_
  89.3 0.2 shard_map.121
  89.6 6.1 %collective-permute-start.10 = (bf16[1,192,768]{2,1,0:T(8,128)(2,1)S(1)}, bf16[1,192,768]{2,1,0:T(8,128)(2,1)S(1)}, u32[]{:S(2)}, u32[]{:S(2)}) collective-permute-start(bf16[1,192,768]{2,1,0:T(8,128)(2,1)S(1)} %get-tuple-element.40), channel_id=1, source_target_pairs={{0,0},{1,4},{2,8},{3,12},{4,1},{5,5},{6,9},{7,13},{8,2},{9,6},{10,... | collective-permute-start | bytes 884744 | tf_op jit(solution)/shard_map/ppermute | solution.py:520
  95.6 0.0 collective-permute-done.17.refs_1_
  95.6 0.5 collective-permute-start.24
  96.2 0.0 collective-permute-done.18.refs_2_
  96.2 3.8 %collective-permute-start.23 = (f32[1,768]{1,0:T(1,128)S(1)}, f32[1,768]{1,0:T(1,128)S(1)}, u32[]{:S(2)}, u32[]{:S(2)}) collective-permute-start(f32[1,768]{1,0:T(1,128)S(1)} %get-tuple-element.55), channel_id=1, source_target_pairs={{0,8},{1,12},{2,0},{3,4},{4,9},{5,13},{6,1},{7,5},{8,10},{9,14},{1... | collective-permute-start | bytes 9224 | tf_op jit(solution)/shard_map/ppermute | solution.py:524
  100.0 0.0 collective-permute-done.19.refs_3_
  100.0 1.0 collective-permute-start.22
  101.0 13.7 %collective-permute-done.24 = f32[1,768]{1,0:T(1,128)S(1)} collective-permute-done((f32[1,768]{1,0:T(1,128)S(1)}, f32[1,768]{1,0:T(1,128)S(1)}, u32[]{:S(2)}, u32[]{:S(2)}) %collective-permute-start.24) | collective-permute-done | bytes 3104 | tf_op jit(solution)/shard_map/ppermute | solution.py:524
  114.7 1.9 %collective-permute-start.21 = (f32[1,768]{1,0:T(1,128)S(1)}, f32[1,768]{1,0:T(1,128)S(1)}, u32[]{:S(2)}, u32[]{:S(2)}) collective-permute-start(f32[1,768]{1,0:T(1,128)S(1)} %get-tuple-element.55), channel_id=1, source_target_pairs={{0,0},{1,4},{2,8},{3,12},{4,1},{5,5},{6,9},{7,13},{8,2},{9,6},{10,... | collective-permute-start | bytes 9224 | tf_op jit(solution)/shard_map/ppermute | solution.py:524
  116.7 1.1 shard_map.124
  117.7 0.0 collective-permute-done.23
  117.7 0.0 collective-permute-done.22
  117.7 4.3 %collective-permute-done.21 = f32[1,768]{1,0:T(1,128)S(1)} collective-permute-done((f32[1,768]{1,0:T(1,128)S(1)}, f32[1,768]{1,0:T(1,128)S(1)}, u32[]{:S(2)}, u32[]{:S(2)}) %collective-permute-start.21) | collective-permute-done | bytes 3104 | tf_op jit(solution)/shard_map/ppermute | solution.py:524
  122.0 0.6 add_add_fusion
  122.6 0.0 collective-permute-done.10
  122.6 0.0 collective-permute-done.20
  122.6 1.7 %convert_add_fusion = f32[768,768]{1,0:T(8,128)} fusion(bf16[768,768]{1,0:T(8,128)(2,1)S(1)} %collective-permute-done.20, bf16[768,768]{1,0:T(8,128)(2,1)S(1)} %shard_map.125), kind=kLoop, calls=%fused_computation | loop fusion | flops 1769472 | bytes 4718592 | tf_op jit(solution)/shard_map/add | solution.py:506
  124.3 0.7 copy.15
  (7 shorter events, 0.0 us)
Async XLA Ops:
  0.6 1.0 copy-start
  1.6 1.0 copy-start.1
  2.6 1.0 copy-start.2
  3.5 37.2 %copy-start.3 = (f32[1,3072]{1,0:T(1,128)S(1)}, f32[1,3072]{1,0:T(1,128)}, u32[]{:S(2)}) copy-start(f32[1,3072]{1,0:T(1,128)} %gate_ref.3) | copy-start | bytes 36868
  3.5 37.2 %copy-start.4 = (bf16[768,768]{1,0:T(8,128)(2,1)S(1)}, bf16[768,768]{1,0:T(8,128)(2,1)}, u32[]{:S(2)}) copy-start(bf16[768,768]{1,0:T(8,128)(2,1)} %w_ref.3) | copy-start | bytes 3538948
  3.7 9.4 %collective-permute-start.1 = (bf16[11,96,128]{2,1,0:T(8,128)(2,1)S(1)}, bf16[11,96,128]{2,1,0:T(8,128)(2,1)S(1)}, u32[]{:S(2)}, u32[]{:S(2)}) collective-permute-start(bf16[11,96,128]{2,1,0:T(8,128)(2,1)S(1)} %get-tuple-element.32), channel_id=1, source_target_pairs={{0,4},{4,0},{8,12},{12,8},{1,5},{5,1},{9,13},{13,9},{2,6},{6,2},{1... | collective-permute-start | bytes 811016 | tf_op jit(solution)/shard_map/ppermute | solution.py:472
  5.3 15.8 %collective-permute-start.2 = (bf16[11,96,128]{2,1,0:T(8,128)(2,1)S(1)}, bf16[11,96,128]{2,1,0:T(8,128)(2,1)S(1)}, u32[]{:S(2)}, u32[]{:S(2)}) collective-permute-start(bf16[11,96,128]{2,1,0:T(8,128)(2,1)S(1)} %get-tuple-element.33), channel_id=1, source_target_pairs={{0,8},{4,12},{8,0},{12,4},{1,9},{5,13},{9,1},{13,5},{2,10},{6,14},... | collective-permute-start | bytes 811016 | tf_op jit(solution)/shard_map/ppermute | solution.py:472
  5.8 15.9 %collective-permute-start.3 = (bf16[11,96,128]{2,1,0:T(8,128)(2,1)S(1)}, bf16[11,96,128]{2,1,0:T(8,128)(2,1)S(1)}, u32[]{:S(2)}, u32[]{:S(2)}) collective-permute-start(bf16[11,96,128]{2,1,0:T(8,128)(2,1)S(1)} %get-tuple-element.34), channel_id=1, source_target_pairs={{0,12},{4,8},{8,4},{12,0},{1,13},{5,9},{9,5},{13,1},{2,14},{6,10},... | collective-permute-start | bytes 811016 | tf_op jit(solution)/shard_map/ppermute | solution.py:472
  7.3 27.5 %collective-permute-start.11 = (bf16[1,192,768]{2,1,0:T(8,128)(2,1)}, bf16[1,192,768]{2,1,0:T(8,128)(2,1)S(1)}, u32[]{:S(2)}, u32[]{:S(2)}) collective-permute-start(bf16[1,192,768]{2,1,0:T(8,128)(2,1)} %param.13), channel_id=1, source_target_pairs={{0,1},{1,5},{2,9},{3,13},{4,0},{5,4},{6,8},{7,12},{8,3},{9,7},{10,... | collective-permute-start | bytes 884744 | tf_op jit(solution)/shard_map/ppermute | solution.py:460
  10.8 29.9 %collective-permute-start = (bf16[1,192,768]{2,1,0:T(8,128)(2,1)}, bf16[1,192,768]{2,1,0:T(8,128)(2,1)S(1)}, u32[]{:S(2)}, u32[]{:S(2)}) collective-permute-start(bf16[1,192,768]{2,1,0:T(8,128)(2,1)} %param.13), channel_id=1, source_target_pairs={{0,0},{1,4},{2,8},{3,12},{4,1},{5,5},{6,9},{7,13},{8,2},{9,6},{10,... | collective-permute-start | bytes 884744 | tf_op jit(solution)/shard_map/ppermute | solution.py:460
  13.2 27.6 %collective-permute-start.13 = (bf16[1,192,768]{2,1,0:T(8,128)(2,1)}, bf16[1,192,768]{2,1,0:T(8,128)(2,1)S(1)}, u32[]{:S(2)}, u32[]{:S(2)}) collective-permute-start(bf16[1,192,768]{2,1,0:T(8,128)(2,1)} %param.13), channel_id=1, source_target_pairs={{0,3},{1,7},{2,11},{3,15},{4,2},{5,6},{6,10},{7,14},{8,1},{9,5},{1... | collective-permute-start | bytes 884744 | tf_op jit(solution)/shard_map/ppermute | solution.py:460
  21.0 19.7 %collective-permute-start.12 = (bf16[1,192,768]{2,1,0:T(8,128)(2,1)}, bf16[1,192,768]{2,1,0:T(8,128)(2,1)S(1)}, u32[]{:S(2)}, u32[]{:S(2)}) collective-permute-start(bf16[1,192,768]{2,1,0:T(8,128)(2,1)} %param.13), channel_id=1, source_target_pairs={{0,2},{1,6},{2,10},{3,14},{4,3},{5,7},{6,11},{7,15},{8,0},{9,4},{1... | collective-permute-start | bytes 884744 | tf_op jit(solution)/shard_map/ppermute | solution.py:460
  23.7 24.1 %collective-permute-start.6 = (bf16[4,3,96,128]{3,2,1,0:T(8,128)(2,1)S(1)}, bf16[4,3,96,128]{3,2,1,0:T(8,128)(2,1)S(1)}, u32[]{:S(2)}, u32[]{:S(2)}) collective-permute-start(bf16[4,3,96,128]{3,2,1,0:T(8,128)(2,1)S(1)} %get-tuple-element.35.refs_0_.o_ref), channel_id=1, source_target_pairs={{0,12},{4,8},{8,4},{12,0},{1,13},{5,9},{9,5},{13,1},{2,14},{6,10},... | collective-permute-start | bytes 884744 | tf_op jit(solution)/shard_map/ppermute | solution.py:481
  34.8 14.0 %collective-permute-start.5 = (bf16[4,3,96,128]{3,2,1,0:T(8,128)(2,1)S(1)}, bf16[4,3,96,128]{3,2,1,0:T(8,128)(2,1)S(1)}, u32[]{:S(2)}, u32[]{:S(2)}) collective-permute-start(bf16[4,3,96,128]{3,2,1,0:T(8,128)(2,1)S(1)} %get-tuple-element.35.refs_0_.o_ref), channel_id=1, source_target_pairs={{0,8},{4,12},{8,0},{12,4},{1,9},{5,13},{9,1},{13,5},{2,10},{6,14},... | collective-permute-start | bytes 884744 | tf_op jit(solution)/shard_map/ppermute | solution.py:481
  40.7 10.9 %collective-permute-start.4 = (bf16[4,3,96,128]{3,2,1,0:T(8,128)(2,1)S(1)}, bf16[4,3,96,128]{3,2,1,0:T(8,128)(2,1)S(1)}, u32[]{:S(2)}, u32[]{:S(2)}) collective-permute-start(bf16[4,3,96,128]{3,2,1,0:T(8,128)(2,1)S(1)} %get-tuple-element.35.refs_0_.o_ref), channel_id=1, source_target_pairs={{0,4},{4,0},{8,12},{12,8},{1,5},{5,1},{9,13},{13,9},{2,6},{6,2},{1... | collective-permute-start | bytes 884744 | tf_op jit(solution)/shard_map/ppermute | solution.py:481
  54.5 68.1 %collective-permute-start.20 = (bf16[768,768]{1,0:T(8,128)(2,1)S(1)}, bf16[768,768]{1,0:T(8,128)(2,1)S(1)}, u32[]{:S(2)}, u32[]{:S(2)}) collective-permute-start(bf16[768,768]{1,0:T(8,128)(2,1)S(1)} %shard_map.125), channel_id=1, source_target_pairs={{0,16},{16,0},{1,17},{17,1},{2,18},{18,2},{3,19},{19,3},{4,20},{20... | collective-permute-start | bytes 3538952 | tf_op jit(solution)/shard_map/ppermute | solution.py:505
  54.6 10.4 %collective-permute-start.14 = (bf16[4,3,96,128]{3,2,1,0:T(8,128)(2,1)S(1)}, bf16[4,3,96,128]{3,2,1,0:T(8,128)(2,1)S(1)}, u32[]{:S(2)}, u32[]{:S(2)}) collective-permute-start(bf16[4,3,96,128]{3,2,1,0:T(8,128)(2,1)S(1)} %get-tuple-element.43), channel_id=1, source_target_pairs={{0,4},{4,0},{8,12},{12,8},{1,5},{5,1},{9,13},{13,9},{2,6},{6,2},{1... | collective-permute-start | bytes 884744 | tf_op jit(solution)/shard_map/ppermute | solution.py:489
  57.2 15.4 %collective-permute-start.15 = (bf16[4,3,96,128]{3,2,1,0:T(8,128)(2,1)S(1)}, bf16[4,3,96,128]{3,2,1,0:T(8,128)(2,1)S(1)}, u32[]{:S(2)}, u32[]{:S(2)}) collective-permute-start(bf16[4,3,96,128]{3,2,1,0:T(8,128)(2,1)S(1)} %get-tuple-element.44), channel_id=1, source_target_pairs={{0,8},{4,12},{8,0},{12,4},{1,9},{5,13},{9,1},{13,5},{2,10},{6,14},... | collective-permute-start | bytes 884744 | tf_op jit(solution)/shard_map/ppermute | solution.py:489
  57.2 15.4 %collective-permute-start.16 = (bf16[4,3,96,128]{3,2,1,0:T(8,128)(2,1)S(1)}, bf16[4,3,96,128]{3,2,1,0:T(8,128)(2,1)S(1)}, u32[]{:S(2)}, u32[]{:S(2)}) collective-permute-start(bf16[4,3,96,128]{3,2,1,0:T(8,128)(2,1)S(1)} %get-tuple-element.45), channel_id=1, source_target_pairs={{0,12},{4,8},{8,4},{12,0},{1,13},{5,9},{9,5},{13,1},{2,14},{6,10},... | collective-permute-start | bytes 884744 | tf_op jit(solution)/shard_map/ppermute | solution.py:489
  58.7 17.0 %collective-permute-start.7 = (bf16[192,768]{1,0:T(8,128)(2,1)S(1)}, bf16[192,768]{1,0:T(8,128)(2,1)S(1)}, u32[]{:S(2)}, u32[]{:S(2)}) collective-permute-start(bf16[192,768]{1,0:T(8,128)(2,1)S(1)} %get-tuple-element.37), channel_id=1, source_target_pairs={{0,1},{1,0},{2,3},{3,2},{4,5},{5,4},{6,7},{7,6},{8,9},{9,8},{10,11... | collective-permute-start | bytes 884744 | tf_op jit(solution)/shard_map/ppermute | solution.py:498
  65.0 23.5 %collective-permute-start.8 = (bf16[192,768]{1,0:T(8,128)(2,1)S(1)}, bf16[192,768]{1,0:T(8,128)(2,1)S(1)}, u32[]{:S(2)}, u32[]{:S(2)}) collective-permute-start(bf16[192,768]{1,0:T(8,128)(2,1)S(1)} %get-tuple-element.38), channel_id=1, source_target_pairs={{0,2},{1,3},{2,0},{3,1},{4,6},{5,7},{6,4},{7,5},{8,10},{9,11},{10,... | collective-permute-start | bytes 884744 | tf_op jit(solution)/shard_map/ppermute | solution.py:498
  72.6 16.8 %collective-permute-start.9 = (bf16[192,768]{1,0:T(8,128)(2,1)S(1)}, bf16[192,768]{1,0:T(8,128)(2,1)S(1)}, u32[]{:S(2)}, u32[]{:S(2)}) collective-permute-start(bf16[192,768]{1,0:T(8,128)(2,1)S(1)} %get-tuple-element.39), channel_id=1, source_target_pairs={{0,3},{1,2},{2,1},{3,0},{4,7},{5,6},{6,5},{7,4},{8,11},{9,10},{10,... | collective-permute-start | bytes 884744 | tf_op jit(solution)/shard_map/ppermute | solution.py:498
  75.4 20.3 %collective-permute-start.17 = (bf16[11,96,128]{2,1,0:T(8,128)(2,1)S(1)}, bf16[11,96,128]{2,1,0:T(8,128)(2,1)S(1)}, u32[]{:S(2)}, u32[]{:S(2)}) collective-permute-start(bf16[11,96,128]{2,1,0:T(8,128)(2,1)S(1)} %get-tuple-element.47), channel_id=1, source_target_pairs={{0,4},{4,0},{8,12},{12,8},{1,5},{5,1},{9,13},{13,9},{2,6},{6,2},{1... | collective-permute-start | bytes 811016 | tf_op jit(solution)/shard_map/ppermute | solution.py:514
  75.7 20.5 %collective-permute-start.18 = (bf16[11,96,128]{2,1,0:T(8,128)(2,1)S(1)}, bf16[11,96,128]{2,1,0:T(8,128)(2,1)S(1)}, u32[]{:S(2)}, u32[]{:S(2)}) collective-permute-start(bf16[11,96,128]{2,1,0:T(8,128)(2,1)S(1)} %get-tuple-element.48), channel_id=1, source_target_pairs={{0,8},{4,12},{8,0},{12,4},{1,9},{5,13},{9,1},{13,5},{2,10},{6,14},... | collective-permute-start | bytes 811016 | tf_op jit(solution)/shard_map/ppermute | solution.py:514
  88.5 11.5 %collective-permute-start.19 = (bf16[11,96,128]{2,1,0:T(8,128)(2,1)S(1)}, bf16[11,96,128]{2,1,0:T(8,128)(2,1)S(1)}, u32[]{:S(2)}, u32[]{:S(2)}) collective-permute-start(bf16[11,96,128]{2,1,0:T(8,128)(2,1)S(1)} %get-tuple-element.49), channel_id=1, source_target_pairs={{0,12},{4,8},{8,4},{12,0},{1,13},{5,9},{9,5},{13,1},{2,14},{6,10},... | collective-permute-start | bytes 811016 | tf_op jit(solution)/shard_map/ppermute | solution.py:514
  89.6 33.0 %collective-permute-start.10 = (bf16[1,192,768]{2,1,0:T(8,128)(2,1)S(1)}, bf16[1,192,768]{2,1,0:T(8,128)(2,1)S(1)}, u32[]{:S(2)}, u32[]{:S(2)}) collective-permute-start(bf16[1,192,768]{2,1,0:T(8,128)(2,1)S(1)} %get-tuple-element.40), channel_id=1, source_target_pairs={{0,0},{1,4},{2,8},{3,12},{4,1},{5,5},{6,9},{7,13},{8,2},{9,6},{10,... | collective-permute-start | bytes 884744 | tf_op jit(solution)/shard_map/ppermute | solution.py:520
  95.6 19.1 %collective-permute-start.24 = (f32[1,768]{1,0:T(1,128)S(1)}, f32[1,768]{1,0:T(1,128)S(1)}, u32[]{:S(2)}, u32[]{:S(2)}) collective-permute-start(f32[1,768]{1,0:T(1,128)S(1)} %get-tuple-element.55), channel_id=1, source_target_pairs={{0,12},{1,8},{2,4},{3,0},{4,13},{5,9},{6,5},{7,1},{8,14},{9,10},{1... | collective-permute-start | bytes 9224 | tf_op jit(solution)/shard_map/ppermute | solution.py:524
  96.2 21.5 %collective-permute-start.23 = (f32[1,768]{1,0:T(1,128)S(1)}, f32[1,768]{1,0:T(1,128)S(1)}, u32[]{:S(2)}, u32[]{:S(2)}) collective-permute-start(f32[1,768]{1,0:T(1,128)S(1)} %get-tuple-element.55), channel_id=1, source_target_pairs={{0,8},{1,12},{2,0},{3,4},{4,9},{5,13},{6,1},{7,5},{8,10},{9,14},{1... | collective-permute-start | bytes 9224 | tf_op jit(solution)/shard_map/ppermute | solution.py:524
  100.0 17.7 %collective-permute-start.22 = (f32[1,768]{1,0:T(1,128)S(1)}, f32[1,768]{1,0:T(1,128)S(1)}, u32[]{:S(2)}, u32[]{:S(2)}) collective-permute-start(f32[1,768]{1,0:T(1,128)S(1)} %get-tuple-element.55), channel_id=1, source_target_pairs={{0,4},{1,0},{2,12},{3,8},{4,5},{5,1},{6,13},{7,9},{8,6},{9,2},{10,... | collective-permute-start | bytes 9224 | tf_op jit(solution)/shard_map/ppermute | solution.py:524
  114.7 7.3 %collective-permute-start.21 = (f32[1,768]{1,0:T(1,128)S(1)}, f32[1,768]{1,0:T(1,128)S(1)}, u32[]{:S(2)}, u32[]{:S(2)}) collective-permute-start(f32[1,768]{1,0:T(1,128)S(1)} %get-tuple-element.55), channel_id=1, source_target_pairs={{0,0},{1,4},{2,8},{3,12},{4,1},{5,5},{6,9},{7,13},{8,2},{9,6},{10,... | collective-permute-start | bytes 9224 | tf_op jit(solution)/shard_map/ppermute | solution.py:524

commit v2 on v0

--- a/solution.py
+++ b/solution.py
@@ -1,8 +1,11 @@
+import functools
 import math
 
 import jax
 import jax.numpy as jnp
 from jax import lax
+from jax.experimental import pallas as pl
+from jax.experimental.pallas import tpu as pltpu
 from jax.sharding import PartitionSpec as P
 
 HD = 128
@@ -49,7 +52,7 @@
     return (key_part, value_part)
 
 
-def shards(query_rows, key_rows, value_rows, lengths, out_weight, gate_vector, cotangent):
+def general_shards(query_rows, key_rows, value_rows, lengths, out_weight, gate_vector, cotangent):
     tokens = query_rows.shape[1]
     local_width = query_rows.shape[2]
     head_count = local_width // HD
@@ -207,6 +210,391 @@
     )
 
 
+VMEM_LIMIT = 40 * 1024 * 1024
+NT = (((1,), (1,)), ((), ()))
+TN = (((0,), (0,)), ((), ()))
+NN = (((1,), (0,)), ((), ()))
+
+
+def mm(left, right, dims):
+    return lax.dot_general(left, right, dims, preferred_element_type=jnp.float32)
+
+
+def lane_block(index, width):
+    return pl.ds(pl.multiple_of(index * width, HD), width)
+
+
+def call(kernel, out_shape, args, flops=0, smem=(), scratch=(), space=pltpu.VMEM, out_space=pltpu.VMEM, limit=VMEM_LIMIT):
+    nbytes = sum(a.size * a.dtype.itemsize for a in args)
+    nbytes += sum(math.prod(o.shape) * o.dtype.itemsize for o in jax.tree.leaves(out_shape))
+    return pl.pallas_call(
+        kernel,
+        out_shape=out_shape,
+        in_specs=[
+            pl.BlockSpec(memory_space=pltpu.SMEM if i in smem else space)
+            for i in range(len(args))
+        ],
+        out_specs=jax.tree.map(lambda _: pl.BlockSpec(memory_space=out_space), out_shape),
+        scratch_shapes=list(scratch),
+        compiler_params=pltpu.CompilerParams(vmem_limit_bytes=limit),
+        cost_estimate=pl.CostEstimate(flops=flops, bytes_accessed=nbytes, transcendentals=0),
+    )(*args)
+
+
+def xor_pairs(count, k):
+    return [(i, i ^ k) for i in range(count)]
+
+
+def pack_kernel(q_ref, k_ref, v_ref, w_ref, kv_ref, q_own_ref, send_ref, near_ref, near2_ref, sems):
+    s, core = lax.axis_index("seq"), lax.axis_index("dp")
+    width, quarter = q_own_ref.shape[1], near_ref.shape[0]
+    own, other = lane_block(s % 2, width), lane_block(1 - s % 2, width)
+    pairs = [
+        (k_ref.at[0, :, other], send_ref.at[0]),
+        (v_ref.at[0, :, other], send_ref.at[1]),
+        (q_ref.at[0, :, other], send_ref.at[2]),
+        (k_ref.at[0, :, own], kv_ref.at[0]),
+        (v_ref.at[0, :, own], kv_ref.at[1]),
+        (q_ref.at[0, :, own], q_own_ref),
+    ]
+    for i, ref in enumerate((near_ref, near2_ref)):
+        at = pl.multiple_of((2 * core + i) * quarter, quarter)
+        pairs.append((w_ref.at[pl.ds(at, quarter), :], ref))
+    copies = [pltpu.make_async_copy(a, b, sems.at[i]) for i, (a, b) in enumerate(pairs)]
+    for copy in copies:
+        copy.start()
+    for copy in copies:
+        copy.wait()
+
+
+def head_rows(parts, head):
+    return jnp.concatenate([p[:, head * HD : (head + 1) * HD] for p in parts], axis=0)
+
+
+def live_bias(s, n, rows, length):
+    parts = []
+    for k in range(n):
+        place = (s ^ k) * rows + lax.broadcasted_iota(jnp.int32, (rows, 1), 0)
+        parts.append(jnp.where(place < length, 0.0, MASKED_SCORE))
+    return jnp.concatenate(parts, axis=0)
+
+
+def forward_kernel(n, scale, len_ref, *refs):
+    kvs, queries, (o_ref, lse_ref) = refs[:n], (refs[n], refs[1].at[2]), refs[n + 1 :]
+    s = lax.axis_index("seq")
+    rows = o_ref.shape[1]
+    bias = live_bias(s, n, rows, len_ref[0])
+    for head in range(o_ref.shape[2] // HD):
+        keys = head_rows([kv.at[0] for kv in kvs], head)
+        values = head_rows([kv.at[1] for kv in kvs], head)
+        scores = mm(keys, head_rows(queries, head), NT) * scale + bias
+        top = jnp.max(scores, axis=0, keepdims=True)
+        weights = jnp.exp(scores - top)
+        total = jnp.sum(weights, axis=0, keepdims=True)
+        summed = mm(values, weights.astype(jnp.bfloat16), TN)
+        attended = (summed / total).T.astype(jnp.bfloat16)
+        lse_ref[head : head + 1, :] = top + jnp.log(total)
+        for u in range(2):
+            o_ref[u, :, head * HD : (head + 1) * HD] = attended[u * rows : (u + 1) * rows]
+
+
+def join_quarters(core, own_refs, other_refs, out_ref):
+    rows = own_refs[0].shape[0]
+    for i in range(2):
+        at = pl.multiple_of((2 * core + i) * rows, rows)
+        out_ref[pl.ds(at, rows), :] = own_refs[i][...]
+        at = pl.multiple_of((2 * (1 - core) + i) * rows, rows)
+        out_ref[pl.ds(at, rows), :] = other_refs[i][...]
+
+
+def grad_attended_kernel(n, gate_ref, w_ref, *refs):
+    quarters, cots, (own_ref, send_ref, cot_ref, w2_ref, share_ref) = refs[:4], refs[4 : 4 + n], refs[4 + n :]
+    s = lax.axis_index("seq")
+    rows, heads_width = own_ref.shape[1:]
+    size = w_ref.shape[0]
+    t = lax.axis_index("tensor")
+    join_quarters(lax.axis_index("dp"), quarters[:2], quarters[2:], w2_ref)
+    for k in range(n):
+        cot_ref[s ^ t ^ k] = cots[k][0]
+    total = None
+    for b, weight_ref in ((0, w_ref), (1, w2_ref)):
+        gate = gate_ref[:, lane_block(s ^ (2 * b), size)]
+        cot = jnp.concatenate([cot_ref[2 * b], cot_ref[2 * b + 1]], axis=0)
+        grad_proj = (gate * cot.astype(jnp.float32)).astype(jnp.bfloat16)
+        part = mm(grad_proj, weight_ref[...], NN)
+        total = part if total is None else total + part
+    share_ref[...] = total
+    own, other = lane_block(s % 2, heads_width), lane_block(1 - s % 2, heads_width)
+    for u in range(2):
+        own_ref[u] = share_ref[u * rows : (u + 1) * rows, own]
+        send_ref[1 - u] = share_ref[u * rows : (u + 1) * rows, other].astype(jnp.bfloat16)
+
+
+def backward_kernel(n, scale, len_ref, lse_ref, o_ref, own_ref, other_ref, *refs):
+    kvs, queries = refs[:n], (refs[n], refs[1].at[2])
+    dq_refs, dkv_refs = refs[n + 1 : n + 3], refs[n + 3 :]
+    s = lax.axis_index("seq")
+    rows = o_ref.shape[1]
+    bias = live_bias(s, n, rows, len_ref[0])
+    for head in range(o_ref.shape[2] // HD):
+        lanes = slice(head * HD, (head + 1) * HD)
+        keys = head_rows([kv.at[0] for kv in kvs], head)
+        values = head_rows([kv.at[1] for kv in kvs], head)
+        query = head_rows(queries, head)
+        grad = jnp.concatenate(
+            [own_ref[u, :, lanes] + other_ref[u, :, lanes].astype(jnp.float32) for u in range(2)],
+            axis=0,
+        ).astype(jnp.bfloat16)
+        attended = jnp.concatenate([o_ref[u, :, lanes] for u in range(2)], axis=0)
+        product = grad.astype(jnp.float32) * attended.astype(jnp.float32)
+        delta = jnp.sum(product.T, axis=0, keepdims=True)
+        scores = mm(keys, query, NT) * scale + bias
+        probs = jnp.exp(scores - lse_ref[head : head + 1, :])
+        grad_probs = mm(values, grad, NT)
+        dscores = (probs * (grad_probs - delta) * scale).astype(jnp.bfloat16)
+        grad_values = mm(probs.astype(jnp.bfloat16), grad, NN)
+        grad_keys = mm(dscores, query, NN)
+        grad_query = mm(keys, dscores, TN).T.astype(jnp.bfloat16)
+        for u in range(2):
+            dq_refs[u][:, lanes] = grad_query[u * rows : (u + 1) * rows]
+        for k in range(n):
+            out = dkv_refs[k]
+            out[0, :, lanes] = grad_keys[k * rows : (k + 1) * rows].astype(out.dtype)
+            out[1, :, lanes] = grad_values[k * rows : (k + 1) * rows].astype(out.dtype)
+
+
+def forward_sum_kernel(own_ref, other_ref, out_ref):
+    out_ref[...] = (own_ref[...] + other_ref[...].astype(jnp.float32)).astype(jnp.bfloat16)
+
+
+def unpack_kernel(dq_ref, dq_other_ref, own_ref, part_ref, other_ref, *outs):
+    s = lax.axis_index("seq")
+    own, other = lane_block(s % 2, dq_ref.shape[1]), lane_block(1 - s % 2, dq_ref.shape[1])
+    outs[0][0, :, own] = dq_ref[...]
+    outs[0][0, :, other] = dq_other_ref[...]
+    for i in range(2):
+        total = own_ref[i] + part_ref[i].astype(jnp.float32)
+        outs[1 + i][0, :, own] = total.astype(jnp.bfloat16)
+        outs[1 + i][0, :, other] = other_ref[i]
+
+
+def project_kernel(n, w_ref, w2_ref, o_ref, other_ref, *refs):
+    (own_ref, *send_refs), (all_ref, parts_ref) = refs[:n], refs[n:]
+    s, t = lax.axis_index("seq"), lax.axis_index("tensor")
+    rows, heads_width = o_ref.shape[1:]
+    own, other = lane_block(s % 2, heads_width), lane_block(1 - s % 2, heads_width)
+    for u in range(2):
+        all_ref[u * rows : (u + 1) * rows, own] = o_ref[u]
+        all_ref[u * rows : (u + 1) * rows, other] = other_ref[1 - u]
+    for b, weight_ref in ((0, w_ref), (1, w2_ref)):
+        part = mm(all_ref[...], weight_ref[...], NT)
+        for u in range(2):
+            parts_ref[2 * b + u] = part[u * rows : (u + 1) * rows]
+    own_ref[...] = parts_ref[s ^ t]
+    for k in range(1, n):
+        send_refs[k - 1][...] = parts_ref[s ^ t ^ k].astype(jnp.bfloat16)
+
+
+def grad_weight_kernel(gate_ref, all_ref, cot_ref, keep_ref, send_ref, outer_ref):
+    core, s = lax.axis_index("dp"), lax.axis_index("seq")
+    size = all_ref.shape[1]
+    half = size // 2
+    for b in range(2):
+        gate = gate_ref[:, lane_block(s ^ (2 * b), size)]
+        cot = jnp.concatenate([cot_ref[2 * b], cot_ref[2 * b + 1]], axis=0)
+        grad_proj = (gate * cot.astype(jnp.float32)).astype(jnp.bfloat16)
+        outer_ref[...] = mm(grad_proj, all_ref[...], TN)
+        keep_ref[b] = outer_ref[pl.ds(pl.multiple_of(core * half, half), half), :]
+        send_ref[b] = outer_ref[pl.ds(pl.multiple_of((1 - core) * half, half), half), :].astype(
+            jnp.bfloat16
+        )
+
+
+def weight_clips_kernel(keep_ref, other_ref, own_ref, send_ref):
+    own_ref[...] = keep_ref[0] + other_ref[0].astype(jnp.float32)
+    send_ref[...] = (keep_ref[1] + other_ref[1].astype(jnp.float32)).astype(jnp.bfloat16)
+
+
+def weight_halves_kernel(own_ref, other_ref, out_ref):
+    out_ref[...] = (own_ref[...] + other_ref[...].astype(jnp.float32)).astype(jnp.bfloat16)
+
+
+def weight_join_kernel(own_ref, other_ref, out_ref):
+    core = lax.axis_index("dp")
+    half = own_ref.shape[0]
+    own = pl.ds(pl.multiple_of(core * half, half), half)
+    out_ref[own, :] = own_ref[...].astype(jnp.float32)
+    other = pl.ds(pl.multiple_of((1 - core) * half, half), half)
+    out_ref[other, :] = other_ref[...].astype(jnp.float32)
+
+
+def projected_kernel(n, own_ref, *refs):
+    parts, out_ref = refs[: n - 1], refs[n - 1]
+    projected = own_ref[...]
+    for part in parts:
+        projected = projected + part[...].astype(jnp.float32)
+    out_ref[...] = projected.astype(jnp.bfloat16)
+
+
+def branch_kernel(gate_ref, cot_ref, projected_ref, branch_ref, gate_grad_ref):
+    projected = projected_ref[...].astype(jnp.float32)
+    gate = gate_ref[:, lane_block(lax.axis_index("tensor"), projected.shape[1])]
+    branch_ref[0] = (gate * projected).astype(jnp.bfloat16)
+    cot = cot_ref[0].astype(jnp.float32)
+    gate_grad_ref[...] = jnp.sum(cot * projected, axis=0, keepdims=True)
+
+
+def square_shards(
+    n, query_rows, key_rows, value_rows, lengths, out_weight, gate_vector, cotangent
+):
+    tokens, width = query_rows.shape[1:]
+    scale = 1.0 / math.sqrt(HD)
+    bf16, f32 = jnp.bfloat16, jnp.float32
+    shape = jax.ShapeDtypeStruct
+    both = ("seq", "tensor")
+    both_pairs = [(a, b) for a in range(n) for b in range(n)]
+
+    def permute(value, axes, k):
+        return lax.ppermute(value, axes, xor_pairs(n, k))
+
+    def swap(value):
+        return lax.ppermute(value, "dp", xor_pairs(2, 1))
+
+    width_half = width // 2
+    rows_kv, rows_q = (2, tokens, width_half), (tokens, width_half)
+    kv, query, send, near_a, near_b = call(
+        pack_kernel,
+        [
+            shape(rows_kv, bf16),
+            shape(rows_q, bf16),
+            shape((3, tokens, width_half), bf16),
+            *[shape((width_half // 2, width), bf16)] * 2,
+        ],
+        (query_rows, key_rows, value_rows, out_weight),
+        scratch=[pltpu.SemaphoreType.DMA((8,))],
+        space=pl.ANY,
+        limit=60 * 1024 * 1024,
+    )
+
+    def turn(value, k):
+        return lax.ppermute(
+            value,
+            both,
+            [
+                (a * n + b, ((a & 2) | (b & 1)) * n + (b ^ k ^ ((a ^ b) & 1)))
+                for a, b in both_pairs
+            ],
+        )
+
+    qkv_x, kv_y, near_a, cot_1, cot_2, near_b, cot_late = lax.optimization_barrier(
+        (
+            permute(send, "seq", 1),
+            permute(kv, "seq", 2),
+            permute(near_a, "seq", 2),
+            turn(cotangent, 1),
+            turn(cotangent, 2),
+            near_b,
+            cotangent,
+        )
+    )
+    kv_xy, near_b, cot_0, cot_3, far_a, qkv_x, kv_y, query = lax.optimization_barrier(
+        (
+            permute(qkv_x[:2], "seq", 2),
+            permute(near_b, "seq", 2),
+            turn(cot_late, 0),
+            turn(cot_late, 3),
+            swap(near_a),
+            qkv_x,
+            kv_y,
+            query,
+        )
+    )
+    cots = (cot_0, cot_1, cot_2, cot_3)
+    kvs = (kv, qkv_x, kv_y, kv_xy)
+    block = 2 * tokens
+    unit_flops = 2 * n * tokens * block * HD
+    wide_flops = 4 * block * width * width
+    attended, lse = call(
+        functools.partial(forward_kernel, n, scale),
+        [shape(rows_kv, bf16), shape((width_half // HD, block), f32)],
+        (lengths, *kvs, query),
+        flops=6 * unit_flops,
+        smem=(0,),
+    )
+    heads = (attended, permute(attended, "seq", 1))
+    grad_own, grad_send, cot_all, weight_y = call(
+        functools.partial(grad_attended_kernel, n),
+        [
+            shape(rows_kv, f32),
+            shape(rows_kv, bf16),
+            shape((n, tokens, width), bf16),
+            shape((width, width), bf16),
+        ],
+        (gate_vector, out_weight, near_a, near_b, far_a, swap(near_b), *cots),
+        flops=wide_flops,
+        scratch=[pltpu.VMEM((block, width), f32)],
+    )
+    grad_other = permute(grad_send, "seq", 1)
+    *parts, attended_all = call(
+        functools.partial(project_kernel, n),
+        [
+            shape((tokens, width), f32),
+            *[shape((tokens, width), bf16)] * (n - 1),
+            shape((block, width), bf16),
+        ],
+        (out_weight, weight_y, *heads),
+        flops=wide_flops,
+        scratch=[pltpu.VMEM((n, tokens, width), f32)],
+    )
+    dq, dq_send, dkv, dkv_x, dkv_y, dkv_xy = call(
+        functools.partial(backward_kernel, n, scale),
+        [shape(rows_q, bf16)] * 2 + [shape(rows_kv, f32)] * 2 + [shape(rows_kv, bf16)] * 2,
+        (lengths, lse, attended, grad_own, grad_other, *kvs, query),
+        flops=15 * unit_flops,
+        smem=(0,),
+    )
+    keep, send = call(
+        grad_weight_kernel,
+        [shape((2, width_half, width), f32), shape((2, width_half, width), bf16)],
+        (gate_vector, attended_all, cot_all),
+        flops=wide_flops,
+        scratch=[pltpu.VMEM((width, width), f32)],
+    )
+    parts = [parts[0]] + [permute(parts[k], "tensor", k) for k in range(1, n)]
+    own, send = call(
+        weight_clips_kernel,
+        [shape((width_half, width), f32), shape((width_half, width), bf16)],
+        (keep, swap(send)),
+    )
+    fin = call(
+        weight_halves_kernel, shape((width_half, width), bf16), (own, permute(send, "seq", 2))
+    )
+    grad_weight = call(weight_join_kernel, shape((width, width), f32), (fin, swap(fin)))
+    dq_other, dkv_xy = permute(dq_send, "seq", 1), permute(dkv_xy, "seq", 2)
+    dkv_y = permute(dkv_y, "seq", 2)
+    dkv_xy, dq_other = lax.optimization_barrier((dkv_xy, dq_other))
+    dkv_x = call(forward_sum_kernel, shape(rows_kv, bf16), (dkv_x, dkv_xy))
+    dkv_other = permute(dkv_x, "seq", 1)
+    projected = call(
+        functools.partial(projected_kernel, n), shape((tokens, width), bf16), tuple(parts)
+    )
+    home = [(a * n + b, (a ^ 1) * n + (b ^ 1) if (a ^ b) & 1 else a * n + b) for a, b in both_pairs]
+    projected = lax.ppermute(projected, both, home)
+    branch, grad_gate = call(
+        branch_kernel,
+        [shape((1, tokens, width), bf16), shape((1, width), f32)],
+        (gate_vector, cotangent, projected),
+    )
+    for k in (1, 2):
+        grad_gate = grad_gate + permute(grad_gate, "seq", k)
+    grad_query, grad_key, grad_value = call(
+        unpack_kernel,
+        [shape((1, tokens, width), bf16)] * 3,
+        (dq, dq_other, dkv, dkv_y, dkv_other),
+    )
+    return (branch, grad_query, grad_key, grad_value, grad_weight, grad_gate)
+
+
 def solution(mesh):
     placed = (
         P("dp", "seq", "tensor"),
@@ -217,8 +605,23 @@
         P("dp", None),
         P("dp", "seq", "tensor"),
     )
+    n = mesh.shape["seq"]
+
+    def body(query_rows, *rest):
+        tokens, width = query_rows.shape[1:]
+        square = (
+            n == 4
+            and mesh.shape["tensor"] == n
+            and mesh.shape["dp"] == 2
+            and width % (2 * HD) == 0
+            and tokens % 32 == 0
+        )
+        if square:
+            return square_shards(n, query_rows, *rest)
+        return general_shards(query_rows, *rest)
+
     return jax.shard_map(
-        shards,
+        body,
         mesh=mesh,
         in_specs=placed,
         out_specs=(

time: 352 us -> 116 us (0.33)
  waiting for transfers between devices: 220 us -> 55.3 us
  starting transfers between devices: 0.35 us -> 40.2 us
  matrix products: 35.1 us -> 0 us
  local copies, waits for them, and re-layouts: 35.3 us -> 1.92 us
  blocking collectives: 26.4 us -> 0 us
  other arithmetic: 19.6 us -> 0.59 us
  Pallas kernels: 0 us -> 16.1 us
  between operations: 14.1 us -> 1.48 us
    all_gather x6 -> x0, waiting for transfers between devices: 194 us -> none  [the longest x1 57.9 us: shards(): weight_whole = lax.all_gather(out_weight, 'seq', axis=0, tiled=True)]
    ppermute x0 -> x26, waiting for transfers between devices: none -> 55.3 us  [the longest x17 44.2 us: permute(): return lax.ppermute(value, axes, xor_pairs(n, k))]
    ppermute x0 -> x26, starting transfers between devices: none -> 40.2 us  [the longest x17 29.3 us: permute(): return lax.ppermute(value, axes, xor_pairs(n, k))]
    dot_general x24 -> x0, matrix products: 35.1 us -> none  [the longest x3 8.54 us: query_terms(): jnp.einsum('ths,shd->thd', dscores, key_block, preferred_element_type=jnp...]
    dynamic_slice x19 -> x0, local copies, waits for them, and re-layouts: 17.4 us -> none  [the longest x3 5.56 us: query_block_step(): lax.dynamic_slice_in_dim(query_value_piece, offset, query_step_rows, 0)]
    pallas_call x0 -> x13, Pallas kernels: none -> 16.1 us  [call(): pl.pallas_call(kernel, out_shape=out_shape, in_specs=[pl.BlockSpec(memory...]
    all_gather x2 -> x0, blocking collectives: 16 us -> none  [the longest x1 8.3 us: shards(): lax.all_gather(row_lse, 'seq', axis=0, tiled=True)]
    reduce_scatter x2 -> x0, waiting for transfers between devices: 14.4 us -> none  [the longest x1 8.15 us: shards(): lax.psum_scatter(partial_value.astype(jnp.bfloat16), 'tensor', scatter_di...]
  transfers between devices with their start and end apart: 9 -> 26, of which waited for: 9 -> 14; matrix products, arithmetic and copies ran while one was open for 22% -> 1% of each run, Pallas kernels for 0% -> 7%
where the time goes in v2:
time: 116 us
  waiting for transfers between devices  55.3 us (48%)
  starting transfers between devices  40.2 us (35%)
  Pallas kernels  16.1 us (14%)
  local copies, waits for them, and re-layouts  1.92 us (2%)
  between operations  1.48 us (1%)
    ppermute x17, waiting for transfers between devices, permute(): return lax.ppermute(value, axes, xor_pairs(n, k))  44.2 us
    ppermute x17, starting transfers between devices, permute(): return lax.ppermute(value, axes, xor_pairs(n, k))  29.3 us
    pallas_call x13, Pallas kernels, call(): pl.pallas_call(kernel, out_shape=out_shape, in_specs=[pl.BlockSpec(memory...  16.1 us
    ppermute x4, starting transfers between devices, turn(): lax.ppermute(value, both, [(a * n + b, (a & 2 | b & 1) * n + (b ^ k ^ (a...  10.1 us
    ppermute x4, waiting for transfers between devices, turn(): lax.ppermute(value, both, [(a * n + b, (a & 2 | b & 1) * n + (b ^ k ^ (a...  8.21 us
    ppermute x4, waiting for transfers between devices, swap(): return lax.ppermute(value, 'dp', xor_pairs(2, 1))  2.84 us
  transfers between devices with their start and end apart: 26, of which 14 were waited for; matrix products, arithmetic and copies ran while one was open for 1% of the time, Pallas kernels for 7%

profile of v2, /device:TPU:0, one launch (start us, length us, event | category | flops | bytes accessed | tf_op | source)
XLA Modules:
  0.0 115.6 jit_solution(1566960096475067139)
XLA Ops:
  0.6 2.7 %shard_map.118 = (bf16[2,192,384]{2,1,0:T(8,128)(2,1)}, bf16[192,384]{1,0:T(8,128)(2,1)}, bf16[3,192,384]{2,1,0:T(8,128)(2,1)}, bf16[192,768]{1,0:T(8,128)(2,1)}, bf16[192,768]{1,0:T(8,128)(2,1)}) custom-call(bf16[1,192,768]{2,1,0:T(8,128)(2,1)} %q_ref.1, bf16[1,192,768]{2,1,0:T(8,128)(2,1)} %k_ref.1, bf16[1,192,768]{2,1,0:T(8,128)(2,1)} %v_ref.1, ...), custom_call_target="tpu_custom_call" | custom-call | bytes 3538944 | tf_op jit(solution)/shard_map/pallas_call | solution.py:230
  3.3 0.0 copy-start
  3.3 0.0 copy-start.2
  3.3 3.0 %collective-permute-start = (bf16[3,192,384]{2,1,0:T(8,128)(2,1)}, bf16[3,192,384]{2,1,0:T(8,128)(2,1)S(1)}, u32[]{:S(2)}, u32[]{:S(2)}) collective-permute-start(bf16[3,192,384]{2,1,0:T(8,128)(2,1)} %get-tuple-element.54), channel_id=1, source_target_pairs={{0,4},{4,0},{8,12},{12,8},{1,5},{5,1},{9,13},{13,9},{2,6},{6,2},{1... | collective-permute-start | bytes 1327112 | tf_op jit(solution)/shard_map/ppermute | solution.py:458
  6.3 1.5 %collective-permute-start.1 = (bf16[2,192,384]{2,1,0:T(8,128)(2,1)}, bf16[2,192,384]{2,1,0:T(8,128)(2,1)S(1)}, u32[]{:S(2)}, u32[]{:S(2)}) collective-permute-start(bf16[2,192,384]{2,1,0:T(8,128)(2,1)} %get-tuple-element.55.refs_0_), channel_id=1, source_target_pairs={{0,8},{4,12},{8,0},{12,4},{1,9},{5,13},{9,1},{13,5},{2,10},{6,14},... | collective-permute-start | bytes 884744 | tf_op jit(solution)/shard_map/ppermute | solution.py:458
  7.9 0.5 collective-permute-start.2
  8.4 1.6 %collective-permute-start.3 = (bf16[1,192,768]{2,1,0:T(8,128)(2,1)S(1)}, bf16[1,192,768]{2,1,0:T(8,128)(2,1)S(1)}, u32[]{:S(2)}, u32[]{:S(2)}) collective-permute-start(bf16[1,192,768]{2,1,0:T(8,128)(2,1)S(1)} %copy-done.1), channel_id=1, source_target_pairs={{0,1},{1,5},{2,3},{3,7},{4,0},{5,4},{6,2},{7,6},{8,9},{9,13},{10,1... | collective-permute-start | bytes 884744 | tf_op jit(solution)/shard_map/ppermute | solution.py:480
  9.9 2.6 %collective-permute-start.4 = (bf16[1,192,768]{2,1,0:T(8,128)(2,1)S(1)}, bf16[1,192,768]{2,1,0:T(8,128)(2,1)S(1)}, u32[]{:S(2)}, u32[]{:S(2)}) collective-permute-start(bf16[1,192,768]{2,1,0:T(8,128)(2,1)S(1)} %copy-done.1), channel_id=1, source_target_pairs={{0,2},{1,6},{2,0},{3,4},{4,3},{5,7},{6,1},{7,5},{8,10},{9,14},{10,... | collective-permute-start | bytes 884744 | tf_op jit(solution)/shard_map/ppermute | solution.py:480
  12.5 3.9 %collective-permute-done.1.refs_2_ = bf16[2,192,384]{2,1,0:T(8,128)(2,1)S(1)} collective-permute-done((bf16[2,192,384]{2,1,0:T(8,128)(2,1)}, bf16[2,192,384]{2,1,0:T(8,128)(2,1)S(1)}, u32[]{:S(2)}, u32[]{:S(2)}) %collective-permute-start.1) | collective-permute-done | bytes 294944 | tf_op jit(solution)/shard_map/ppermute | solution.py:458
  16.5 4.9 %collective-permute-done.2.refs_0_ = bf16[192,768]{1,0:T(8,128)(2,1)S(1)} collective-permute-done((bf16[192,768]{1,0:T(8,128)(2,1)}, bf16[192,768]{1,0:T(8,128)(2,1)S(1)}, u32[]{:S(2)}, u32[]{:S(2)}) %collective-permute-start.2) | collective-permute-done | bytes 294944 | tf_op jit(solution)/shard_map/ppermute | solution.py:458
  21.3 1.7 %collective-permute-done.3.refs_5_ = bf16[1,192,768]{2,1,0:T(8,128)(2,1)S(1)} collective-permute-done((bf16[1,192,768]{2,1,0:T(8,128)(2,1)S(1)}, bf16[1,192,768]{2,1,0:T(8,128)(2,1)S(1)}, u32[]{:S(2)}, u32[]{:S(2)}) %collective-permute-start.3) | collective-permute-done | bytes 294944 | tf_op jit(solution)/shard_map/ppermute | solution.py:480
  23.0 1.8 %collective-permute-done.4.refs_6_ = bf16[1,192,768]{2,1,0:T(8,128)(2,1)S(1)} collective-permute-done((bf16[1,192,768]{2,1,0:T(8,128)(2,1)S(1)}, bf16[1,192,768]{2,1,0:T(8,128)(2,1)S(1)}, u32[]{:S(2)}, u32[]{:S(2)}) %collective-permute-start.4) | collective-permute-done | bytes 294944 | tf_op jit(solution)/shard_map/ppermute | solution.py:480
  24.8 0.0 collective-permute-done.refs_1_
  24.8 1.6 %collective-permute-start.5 = (bf16[2,192,384]{2,1,0:T(8,128)(2,1)S(1)}, bf16[2,192,384]{2,1,0:T(8,128)(2,1)S(1)}, u32[]{:S(2)}, u32[]{:S(2)}) collective-permute-start(bf16[2,192,384]{2,1,0:T(8,128)(2,1)S(1)} %slice.3), channel_id=1, source_target_pairs={{0,8},{4,12},{8,0},{12,4},{1,9},{5,13},{9,1},{13,5},{2,10},{6,14},... | collective-permute-start | bytes 884744 | tf_op jit(solution)/shard_map/ppermute | solution.py:458
  26.4 0.5 collective-permute-start.6
  26.9 0.7 collective-permute-start.7
  27.6 5.3 %collective-permute-start.8 = (bf16[1,192,768]{2,1,0:T(8,128)(2,1)S(1)}, bf16[1,192,768]{2,1,0:T(8,128)(2,1)S(1)}, u32[]{:S(2)}, u32[]{:S(2)}) collective-permute-start(bf16[1,192,768]{2,1,0:T(8,128)(2,1)S(1)} %copy-done.1), channel_id=1, source_target_pairs={{0,3},{1,7},{2,1},{3,5},{4,2},{5,6},{6,0},{7,4},{8,11},{9,15},{10,... | collective-permute-start | bytes 884744 | tf_op jit(solution)/shard_map/ppermute | solution.py:480
  32.9 0.0 collective-permute-start.9
  32.9 2.0 %collective-permute-done.5.refs_3_ = bf16[2,192,384]{2,1,0:T(8,128)(2,1)S(1)} collective-permute-done((bf16[2,192,384]{2,1,0:T(8,128)(2,1)S(1)}, bf16[2,192,384]{2,1,0:T(8,128)(2,1)S(1)}, u32[]{:S(2)}, u32[]{:S(2)}) %collective-permute-start.5) | collective-permute-done | bytes 294944 | tf_op jit(solution)/shard_map/ppermute | solution.py:458
  34.8 4.4 %collective-permute-done.6.refs_1_ = bf16[192,768]{1,0:T(8,128)(2,1)S(1)} collective-permute-done((bf16[192,768]{1,0:T(8,128)(2,1)}, bf16[192,768]{1,0:T(8,128)(2,1)S(1)}, u32[]{:S(2)}, u32[]{:S(2)}) %collective-permute-start.6) | collective-permute-done | bytes 294944 | tf_op jit(solution)/shard_map/ppermute | solution.py:458
  39.3 0.0 collective-permute-done.7.refs_4_
  39.3 4.8 %collective-permute-done.8.refs_7_ = bf16[1,192,768]{2,1,0:T(8,128)(2,1)S(1)} collective-permute-done((bf16[1,192,768]{2,1,0:T(8,128)(2,1)S(1)}, bf16[1,192,768]{2,1,0:T(8,128)(2,1)S(1)}, u32[]{:S(2)}, u32[]{:S(2)}) %collective-permute-start.8) | collective-permute-done | bytes 294944 | tf_op jit(solution)/shard_map/ppermute | solution.py:480
  44.0 0.0 collective-permute-done.9.refs_2_
  44.0 0.0 collective-permute-start.10
  44.7 0.0 copy-start.3
  44.7 1.0 copy-done.3
  45.7 0.9 copy-done.5
  46.6 2.0 %shard_map.120 = (bf16[2,192,384]{2,1,0:T(8,128)(2,1)S(1)}, f32[3,384]{1,0:T(4,128)S(1)}) custom-call(s32[1]{0:T(128)S(6)} %copy.13.len_ref, bf16[2,192,384]{2,1,0:T(8,128)(2,1)S(1)} %copy-done.3, bf16[3,192,384]{2,1,0:T(8,128)(2,1)S(1)} %collective-permute-done.refs_1_, bf16[2,192,384]{2,1,0:T(8,128)(2,1)S(1)} %collective-permute-done.1.refs_2_, ...), custom_call_target="tpu_custom_call" | custom-call | flops 452984832 | bytes 1774084 | tf_op jit(solution)/shard_map/pallas_call | solution.py:230
  48.6 0.1 collective-permute-start.11
  48.7 0.0 collective-permute-done.10.refs_3_
  48.7 1.4 %shard_map.119 = (f32[2,192,384]{2,1,0:T(8,128)S(1)}, bf16[2,192,384]{2,1,0:T(8,128)(2,1)S(1)}, bf16[4,192,768]{2,1,0:T(8,128)(2,1)S(1)}, bf16[768,768]{1,0:T(8,128)(2,1)S(1)}) custom-call(f32[1,3072]{1,0:T(1,128)S(1)} %copy-done.2, bf16[768,768]{1,0:T(8,128)(2,1)S(1)} %copy-done, bf16[192,768]{1,0:T(8,128)(2,1)S(1)} %collective-permute-done.2.refs_0_, ...), custom_call_target="tpu_custom_call" | custom-call | flops 905969664 | bytes 6795264 | tf_op jit(solution)/shard_map/pallas_call | solution.py:230
  50.1 8.0 %collective-permute-done.11.other_ref = bf16[2,192,384]{2,1,0:T(8,128)(2,1)S(1)} collective-permute-done((bf16[2,192,384]{2,1,0:T(8,128)(2,1)S(1)}, bf16[2,192,384]{2,1,0:T(8,128)(2,1)S(1)}, u32[]{:S(2)}, u32[]{:S(2)}) %collective-permute-start.11) | collective-permute-done | bytes 294944 | tf_op jit(solution)/shard_map/ppermute | solution.py:458
  58.1 1.3 %shard_map.121 = (f32[192,768]{1,0:T(8,128)S(1)}, bf16[192,768]{1,0:T(8,128)(2,1)S(1)}, bf16[192,768]{1,0:T(8,128)(2,1)S(1)}, bf16[192,768]{1,0:T(8,128)(2,1)S(1)}, bf16[384,768]{1,0:T(8,128)(2,1)S(1)}) custom-call(bf16[768,768]{1,0:T(8,128)(2,1)S(1)} %copy-done, bf16[768,768]{1,0:T(8,128)(2,1)S(1)} %get-tuple-element.70.w2_ref, ...), custom_call_target="tpu_custom_call" | custom-call | flops 905969664 | bytes 5013504 | tf_op jit(solution)/shard_map/pallas_call | solution.py:230
  59.4 2.0 %shard_map.127 = (f32[2,384,768]{2,1,0:T(8,128)S(1)}, bf16[2,384,768]{2,1,0:T(8,128)(2,1)S(1)}) custom-call(f32[1,3072]{1,0:T(1,128)S(1)} %copy-done.2, bf16[384,768]{1,0:T(8,128)(2,1)S(1)} %get-tuple-element.95.all_ref, bf16[4,192,768]{2,1,0:T(8,128)(2,1)S(1)} %get-tuple-element.96.cot_ref), custom_call_target="tpu_custom_call" | custom-call | flops 905969664 | bytes 5320704 | tf_op jit(solution)/shard_map/pallas_call | solution.py:230
  61.4 0.1 collective-permute-start.21
  61.5 2.8 %collective-permute-done.21.other_ref = bf16[2,384,768]{2,1,0:T(8,128)(2,1)S(1)} collective-permute-done((bf16[2,384,768]{2,1,0:T(8,128)(2,1)S(1)}, bf16[2,384,768]{2,1,0:T(8,128)(2,1)S(1)}, u32[]{:S(2)}, u32[]{:S(2)}) %collective-permute-start.21) | collective-permute-done | bytes 1179680 | tf_op jit(solution)/shard_map/ppermute | solution.py:461
  64.3 0.3 shard_map.128
  64.6 1.6 %collective-permute-start.22 = (bf16[384,768]{1,0:T(8,128)(2,1)S(1)}, bf16[384,768]{1,0:T(8,128)(2,1)S(1)}, u32[]{:S(2)}, u32[]{:S(2)}) collective-permute-start(bf16[384,768]{1,0:T(8,128)(2,1)S(1)} %get-tuple-element.100), channel_id=1, source_target_pairs={{0,8},{4,12},{8,0},{12,4},{1,9},{5,13},{9,1},{13,5},{2,10},{6,14},... | collective-permute-start | bytes 1769480 | tf_op jit(solution)/shard_map/ppermute | solution.py:458
  66.1 0.3 collective-permute-start.16
  66.4 0.6 collective-permute-start.12
  67.1 2.3 %collective-permute-start.13 = (bf16[192,768]{1,0:T(8,128)(2,1)S(1)}, bf16[192,768]{1,0:T(8,128)(2,1)S(1)}, u32[]{:S(2)}, u32[]{:S(2)}) collective-permute-start(bf16[192,768]{1,0:T(8,128)(2,1)S(1)} %get-tuple-element.78), channel_id=1, source_target_pairs={{0,2},{1,3},{2,0},{3,1},{4,6},{5,7},{6,4},{7,5},{8,10},{9,11},{10,... | collective-permute-start | bytes 884744 | tf_op jit(solution)/shard_map/ppermute | solution.py:458
  69.3 1.5 %collective-permute-start.14 = (bf16[192,768]{1,0:T(8,128)(2,1)S(1)}, bf16[192,768]{1,0:T(8,128)(2,1)S(1)}, u32[]{:S(2)}, u32[]{:S(2)}) collective-permute-start(bf16[192,768]{1,0:T(8,128)(2,1)S(1)} %get-tuple-element.79), channel_id=1, source_target_pairs={{0,3},{1,2},{2,1},{3,0},{4,7},{5,6},{6,5},{7,4},{8,11},{9,10},{10,... | collective-permute-start | bytes 884744 | tf_op jit(solution)/shard_map/ppermute | solution.py:458
  70.8 4.1 %collective-permute-done.16.other_ref = bf16[2,192,384]{2,1,0:T(8,128)(2,1)S(1)} collective-permute-done((bf16[2,192,384]{2,1,0:T(8,128)(2,1)S(1)}, bf16[2,192,384]{2,1,0:T(8,128)(2,1)S(1)}, u32[]{:S(2)}, u32[]{:S(2)}) %collective-permute-start.16) | collective-permute-done | bytes 294944 | tf_op jit(solution)/shard_map/ppermute | solution.py:458
  74.9 2.8 %shard_map.124 = (bf16[192,384]{1,0:T(8,128)(2,1)S(1)}, bf16[192,384]{1,0:T(8,128)(2,1)S(1)}, f32[2,192,384]{2,1,0:T(8,128)S(1)}, f32[2,192,384]{2,1,0:T(8,128)S...) custom-call(s32[1]{0:T(128)S(6)} %copy.13.len_ref, f32[3,384]{1,0:T(4,128)S(1)} %get-tuple-element.81.lse_ref, ...), custom_call_target="tpu_custom_call" | custom-call | flops 1132462080 | bytes 4723204 | tf_op jit(solution)/shard_map/pallas_call | solution.py:230
  77.7 0.6 collective-permute-start.17
  78.3 2.3 %collective-permute-done.22.other_ref = bf16[384,768]{1,0:T(8,128)(2,1)S(1)} collective-permute-done((bf16[384,768]{1,0:T(8,128)(2,1)S(1)}, bf16[384,768]{1,0:T(8,128)(2,1)S(1)}, u32[]{:S(2)}, u32[]{:S(2)}) %collective-permute-start.22) | collective-permute-done | bytes 589856 | tf_op jit(solution)/shard_map/ppermute | solution.py:458
  80.6 0.1 shard_map.129.own_ref
  80.7 0.1 collective-permute-start.23
  80.8 0.0 collective-permute-done.12.refs_0_
  80.8 1.3 %collective-permute-start.18 = (bf16[192,384]{1,0:T(8,128)(2,1)S(1)}, bf16[192,384]{1,0:T(8,128)(2,1)S(1)}, u32[]{:S(2)}, u32[]{:S(2)}) collective-permute-start(bf16[192,384]{1,0:T(8,128)(2,1)S(1)} %get-tuple-element.86), channel_id=1, source_target_pairs={{0,4},{4,0},{8,12},{12,8},{1,5},{5,1},{9,13},{13,9},{2,6},{6,2},{1... | collective-permute-start | bytes 442376 | tf_op jit(solution)/shard_map/ppermute | solution.py:458
  82.1 8.5 %collective-permute-done.13.refs_1_ = bf16[192,768]{1,0:T(8,128)(2,1)S(1)} collective-permute-done((bf16[192,768]{1,0:T(8,128)(2,1)S(1)}, bf16[192,768]{1,0:T(8,128)(2,1)S(1)}, u32[]{:S(2)}, u32[]{:S(2)}) %collective-permute-start.13) | collective-permute-done | bytes 294944 | tf_op jit(solution)/shard_map/ppermute | solution.py:458
  90.6 0.2 shard_map.122
  90.7 0.7 collective-permute-start.15
  91.4 0.6 collective-permute-start.19
  92.0 0.1 shard_map.125
  92.1 7.9 %collective-permute-start.20 = (bf16[2,192,384]{2,1,0:T(8,128)(2,1)S(1)}, bf16[2,192,384]{2,1,0:T(8,128)(2,1)S(1)}, u32[]{:S(2)}, u32[]{:S(2)}) collective-permute-start(bf16[2,192,384]{2,1,0:T(8,128)(2,1)S(1)} %shard_map.125), channel_id=1, source_target_pairs={{0,4},{4,0},{8,12},{12,8},{1,5},{5,1},{9,13},{13,9},{2,6},{6,2},{1... | collective-permute-start | bytes 884744 | tf_op jit(solution)/shard_map/ppermute | solution.py:458
  100.0 0.8 shard_map.123
  100.8 5.0 %collective-permute-start.24 = (f32[1,768]{1,0:T(1,128)S(1)}, f32[1,768]{1,0:T(1,128)S(1)}, u32[]{:S(2)}, u32[]{:S(2)}) collective-permute-start(f32[1,768]{1,0:T(1,128)S(1)} %get-tuple-element.101), channel_id=1, source_target_pairs={{0,4},{4,0},{8,12},{12,8},{1,5},{5,1},{9,13},{13,9},{2,6},{6,2},{1... | collective-permute-start | bytes 9224 | tf_op jit(solution)/shard_map/ppermute | solution.py:458
  105.8 3.0 %collective-permute-done.24 = f32[1,768]{1,0:T(1,128)S(1)} collective-permute-done((f32[1,768]{1,0:T(1,128)S(1)}, f32[1,768]{1,0:T(1,128)S(1)}, u32[]{:S(2)}, u32[]{:S(2)}) %collective-permute-start.24) | collective-permute-done | bytes 3104 | tf_op jit(solution)/shard_map/ppermute | solution.py:458
  108.8 0.5 collective-permute-start.25
  109.3 3.1 %collective-permute-done.25 = f32[1,768]{1,0:T(1,128)S(1)} collective-permute-done((f32[1,768]{1,0:T(1,128)S(1)}, f32[1,768]{1,0:T(1,128)S(1)}, u32[]{:S(2)}, u32[]{:S(2)}) %collective-permute-start.25) | collective-permute-done | bytes 3104 | tf_op jit(solution)/shard_map/ppermute | solution.py:458
  112.4 0.6 add.7
  113.0 1.0 shard_map.126
  114.0 1.6 %shard_map.130 = f32[768,768]{1,0:T(8,128)} custom-call(bf16[384,768]{1,0:T(8,128)(2,1)S(1)} %shard_map.129.own_ref, bf16[384,768]{1,0:T(8,128)(2,1)S(1)} %collective-permute-done.23.other_ref), custom_call_target="tpu_custom_call" | custom-call | bytes 3538944 | tf_op jit(solution)/shard_map/pallas_call | solution.py:230
  (18 shorter events, 0.1 us)
Async XLA Ops:
  0.6 7.7 %copy-start.1 = (bf16[1,192,768]{2,1,0:T(8,128)(2,1)S(1)}, bf16[1,192,768]{2,1,0:T(8,128)(2,1)}, u32[]{:S(2)}) copy-start(bf16[1,192,768]{2,1,0:T(8,128)(2,1)} %cot_ref.1) | copy-start | bytes 884740
  3.3 45.4 %copy-start = (bf16[768,768]{1,0:T(8,128)(2,1)S(1)}, bf16[768,768]{1,0:T(8,128)(2,1)}, u32[]{:S(2)}) copy-start(bf16[768,768]{1,0:T(8,128)(2,1)} %w_ref.5) | copy-start | bytes 3538948
  3.3 45.4 %copy-start.2 = (f32[1,3072]{1,0:T(1,128)S(1)}, f32[1,3072]{1,0:T(1,128)}, u32[]{:S(2)}) copy-start(f32[1,3072]{1,0:T(1,128)} %gate_ref.5) | copy-start | bytes 36868
  3.3 21.5 %collective-permute-start = (bf16[3,192,384]{2,1,0:T(8,128)(2,1)}, bf16[3,192,384]{2,1,0:T(8,128)(2,1)S(1)}, u32[]{:S(2)}, u32[]{:S(2)}) collective-permute-start(bf16[3,192,384]{2,1,0:T(8,128)(2,1)} %get-tuple-element.54), channel_id=1, source_target_pairs={{0,4},{4,0},{8,12},{12,8},{1,5},{5,1},{9,13},{13,9},{2,6},{6,2},{1... | collective-permute-start | bytes 1327112 | tf_op jit(solution)/shard_map/ppermute | solution.py:458
  6.3 10.1 %collective-permute-start.1 = (bf16[2,192,384]{2,1,0:T(8,128)(2,1)}, bf16[2,192,384]{2,1,0:T(8,128)(2,1)S(1)}, u32[]{:S(2)}, u32[]{:S(2)}) collective-permute-start(bf16[2,192,384]{2,1,0:T(8,128)(2,1)} %get-tuple-element.55.refs_0_), channel_id=1, source_target_pairs={{0,8},{4,12},{8,0},{12,4},{1,9},{5,13},{9,1},{13,5},{2,10},{6,14},... | collective-permute-start | bytes 884744 | tf_op jit(solution)/shard_map/ppermute | solution.py:458
  7.9 13.5 %collective-permute-start.2 = (bf16[192,768]{1,0:T(8,128)(2,1)}, bf16[192,768]{1,0:T(8,128)(2,1)S(1)}, u32[]{:S(2)}, u32[]{:S(2)}) collective-permute-start(bf16[192,768]{1,0:T(8,128)(2,1)} %get-tuple-element.56), channel_id=1, source_target_pairs={{0,8},{4,12},{8,0},{12,4},{1,9},{5,13},{9,1},{13,5},{2,10},{6,14},... | collective-permute-start | bytes 884744 | tf_op jit(solution)/shard_map/ppermute | solution.py:458
  8.4 14.7 %collective-permute-start.3 = (bf16[1,192,768]{2,1,0:T(8,128)(2,1)S(1)}, bf16[1,192,768]{2,1,0:T(8,128)(2,1)S(1)}, u32[]{:S(2)}, u32[]{:S(2)}) collective-permute-start(bf16[1,192,768]{2,1,0:T(8,128)(2,1)S(1)} %copy-done.1), channel_id=1, source_target_pairs={{0,1},{1,5},{2,3},{3,7},{4,0},{5,4},{6,2},{7,6},{8,9},{9,13},{10,1... | collective-permute-start | bytes 884744 | tf_op jit(solution)/shard_map/ppermute | solution.py:480
  9.9 14.8 %collective-permute-start.4 = (bf16[1,192,768]{2,1,0:T(8,128)(2,1)S(1)}, bf16[1,192,768]{2,1,0:T(8,128)(2,1)S(1)}, u32[]{:S(2)}, u32[]{:S(2)}) collective-permute-start(bf16[1,192,768]{2,1,0:T(8,128)(2,1)S(1)} %copy-done.1), channel_id=1, source_target_pairs={{0,2},{1,6},{2,0},{3,4},{4,3},{5,7},{6,1},{7,5},{8,10},{9,14},{10,... | collective-permute-start | bytes 884744 | tf_op jit(solution)/shard_map/ppermute | solution.py:480
  24.8 10.0 %collective-permute-start.5 = (bf16[2,192,384]{2,1,0:T(8,128)(2,1)S(1)}, bf16[2,192,384]{2,1,0:T(8,128)(2,1)S(1)}, u32[]{:S(2)}, u32[]{:S(2)}) collective-permute-start(bf16[2,192,384]{2,1,0:T(8,128)(2,1)S(1)} %slice.3), channel_id=1, source_target_pairs={{0,8},{4,12},{8,0},{12,4},{1,9},{5,13},{9,1},{13,5},{2,10},{6,14},... | collective-permute-start | bytes 884744 | tf_op jit(solution)/shard_map/ppermute | solution.py:458
  26.4 12.9 %collective-permute-start.6 = (bf16[192,768]{1,0:T(8,128)(2,1)}, bf16[192,768]{1,0:T(8,128)(2,1)S(1)}, u32[]{:S(2)}, u32[]{:S(2)}) collective-permute-start(bf16[192,768]{1,0:T(8,128)(2,1)} %get-tuple-element.60), channel_id=1, source_target_pairs={{0,8},{4,12},{8,0},{12,4},{1,9},{5,13},{9,1},{13,5},{2,10},{6,14},... | collective-permute-start | bytes 884744 | tf_op jit(solution)/shard_map/ppermute | solution.py:458
  26.9 12.4 %collective-permute-start.7 = (bf16[1,192,768]{2,1,0:T(8,128)(2,1)S(1)}, bf16[1,192,768]{2,1,0:T(8,128)(2,1)S(1)}, u32[]{:S(2)}, u32[]{:S(2)}) collective-permute-start(bf16[1,192,768]{2,1,0:T(8,128)(2,1)S(1)} %copy-done.1), channel_id=1, source_target_pairs={{0,0},{1,4},{2,2},{3,6},{4,1},{5,5},{6,3},{7,7},{8,8},{9,12},{10,1... | collective-permute-start | bytes 884744 | tf_op jit(solution)/shard_map/ppermute | solution.py:480
  27.6 16.5 %collective-permute-start.8 = (bf16[1,192,768]{2,1,0:T(8,128)(2,1)S(1)}, bf16[1,192,768]{2,1,0:T(8,128)(2,1)S(1)}, u32[]{:S(2)}, u32[]{:S(2)}) collective-permute-start(bf16[1,192,768]{2,1,0:T(8,128)(2,1)S(1)} %copy-done.1), channel_id=1, source_target_pairs={{0,3},{1,7},{2,1},{3,5},{4,2},{5,6},{6,0},{7,4},{8,11},{9,15},{10,... | collective-permute-start | bytes 884744 | tf_op jit(solution)/shard_map/ppermute | solution.py:480
  32.9 11.2 %collective-permute-start.9 = (bf16[192,768]{1,0:T(8,128)(2,1)S(1)}, bf16[192,768]{1,0:T(8,128)(2,1)S(1)}, u32[]{:S(2)}, u32[]{:S(2)}) collective-permute-start(bf16[192,768]{1,0:T(8,128)(2,1)S(1)} %collective-permute-done.2.refs_0_), channel_id=1, source_target_pairs={{0,16},{16,0},{1,17},{17,1},{2,18},{18,2},{3,19},{19,3},{4,20},{20... | collective-permute-start | bytes 884744 | tf_op jit(solution)/shard_map/ppermute | solution.py:461
  44.0 4.6 %collective-permute-start.10 = (bf16[192,768]{1,0:T(8,128)(2,1)S(1)}, bf16[192,768]{1,0:T(8,128)(2,1)S(1)}, u32[]{:S(2)}, u32[]{:S(2)}) collective-permute-start(bf16[192,768]{1,0:T(8,128)(2,1)S(1)} %collective-permute-done.6.refs_1_), channel_id=1, source_target_pairs={{0,16},{16,0},{1,17},{17,1},{2,18},{18,2},{3,19},{19,3},{4,20},{20... | collective-permute-start | bytes 884744 | tf_op jit(solution)/shard_map/ppermute | solution.py:461
  44.7 1.0 copy-start.3
  45.7 0.9 copy-start.5
  48.6 9.5 %collective-permute-start.11 = (bf16[2,192,384]{2,1,0:T(8,128)(2,1)S(1)}, bf16[2,192,384]{2,1,0:T(8,128)(2,1)S(1)}, u32[]{:S(2)}, u32[]{:S(2)}) collective-permute-start(bf16[2,192,384]{2,1,0:T(8,128)(2,1)S(1)} %get-tuple-element.75.o_ref), channel_id=1, source_target_pairs={{0,4},{4,0},{8,12},{12,8},{1,5},{5,1},{9,13},{13,9},{2,6},{6,2},{1... | collective-permute-start | bytes 884744 | tf_op jit(solution)/shard_map/ppermute | solution.py:458
  61.4 2.9 %collective-permute-start.21 = (bf16[2,384,768]{2,1,0:T(8,128)(2,1)S(1)}, bf16[2,384,768]{2,1,0:T(8,128)(2,1)S(1)}, u32[]{:S(2)}, u32[]{:S(2)}) collective-permute-start(bf16[2,384,768]{2,1,0:T(8,128)(2,1)S(1)} %get-tuple-element.98), channel_id=1, source_target_pairs={{0,16},{16,0},{1,17},{17,1},{2,18},{18,2},{3,19},{19,3},{4,20},{20... | collective-permute-start | bytes 3538952 | tf_op jit(solution)/shard_map/ppermute | solution.py:461
  64.3 10.6 %copy-start.4 = (bf16[2,192,384]{2,1,0:T(8,128)(2,1)S(1)}, bf16[2,192,384]{2,1,0:T(8,128)(2,1)}, u32[]{:S(2)}) copy-start(bf16[2,192,384]{2,1,0:T(8,128)(2,1)} %get-tuple-element.55.refs_0_) | copy-start | bytes 884740
  64.3 10.6 %copy-start.6 = (bf16[192,384]{1,0:T(8,128)(2,1)S(1)}, bf16[192,384]{1,0:T(8,128)(2,1)}, u32[]{:S(2)}) copy-start(bf16[192,384]{1,0:T(8,128)(2,1)} %get-tuple-element.74.refs_4_) | copy-start | bytes 442372
  64.6 16.0 %collective-permute-start.22 = (bf16[384,768]{1,0:T(8,128)(2,1)S(1)}, bf16[384,768]{1,0:T(8,128)(2,1)S(1)}, u32[]{:S(2)}, u32[]{:S(2)}) collective-permute-start(bf16[384,768]{1,0:T(8,128)(2,1)S(1)} %get-tuple-element.100), channel_id=1, source_target_pairs={{0,8},{4,12},{8,0},{12,4},{1,9},{5,13},{9,1},{13,5},{2,10},{6,14},... | collective-permute-start | bytes 1769480 | tf_op jit(solution)/shard_map/ppermute | solution.py:458
  66.1 8.8 %collective-permute-start.16 = (bf16[2,192,384]{2,1,0:T(8,128)(2,1)S(1)}, bf16[2,192,384]{2,1,0:T(8,128)(2,1)S(1)}, u32[]{:S(2)}, u32[]{:S(2)}) collective-permute-start(bf16[2,192,384]{2,1,0:T(8,128)(2,1)S(1)} %get-tuple-element.83), channel_id=1, source_target_pairs={{0,4},{4,0},{8,12},{12,8},{1,5},{5,1},{9,13},{13,9},{2,6},{6,2},{1... | collective-permute-start | bytes 884744 | tf_op jit(solution)/shard_map/ppermute | solution.py:458
  66.4 14.3 %collective-permute-start.12 = (bf16[192,768]{1,0:T(8,128)(2,1)S(1)}, bf16[192,768]{1,0:T(8,128)(2,1)S(1)}, u32[]{:S(2)}, u32[]{:S(2)}) collective-permute-start(bf16[192,768]{1,0:T(8,128)(2,1)S(1)} %get-tuple-element.77), channel_id=1, source_target_pairs={{0,1},{1,0},{2,3},{3,2},{4,5},{5,4},{6,7},{7,6},{8,9},{9,8},{10,11... | collective-permute-start | bytes 884744 | tf_op jit(solution)/shard_map/ppermute | solution.py:458
  67.1 23.5 %collective-permute-start.13 = (bf16[192,768]{1,0:T(8,128)(2,1)S(1)}, bf16[192,768]{1,0:T(8,128)(2,1)S(1)}, u32[]{:S(2)}, u32[]{:S(2)}) collective-permute-start(bf16[192,768]{1,0:T(8,128)(2,1)S(1)} %get-tuple-element.78), channel_id=1, source_target_pairs={{0,2},{1,3},{2,0},{3,1},{4,6},{5,7},{6,4},{7,5},{8,10},{9,11},{10,... | collective-permute-start | bytes 884744 | tf_op jit(solution)/shard_map/ppermute | solution.py:458
  69.3 21.2 %collective-permute-start.14 = (bf16[192,768]{1,0:T(8,128)(2,1)S(1)}, bf16[192,768]{1,0:T(8,128)(2,1)S(1)}, u32[]{:S(2)}, u32[]{:S(2)}) collective-permute-start(bf16[192,768]{1,0:T(8,128)(2,1)S(1)} %get-tuple-element.79), channel_id=1, source_target_pairs={{0,3},{1,2},{2,1},{3,0},{4,7},{5,6},{6,5},{7,4},{8,11},{9,10},{10,... | collective-permute-start | bytes 884744 | tf_op jit(solution)/shard_map/ppermute | solution.py:458
  77.7 14.3 %collective-permute-start.17 = (bf16[2,192,384]{2,1,0:T(8,128)(2,1)S(1)}, bf16[2,192,384]{2,1,0:T(8,128)(2,1)S(1)}, u32[]{:S(2)}, u32[]{:S(2)}) collective-permute-start(bf16[2,192,384]{2,1,0:T(8,128)(2,1)S(1)} %get-tuple-element.85), channel_id=1, source_target_pairs={{0,8},{4,12},{8,0},{12,4},{1,9},{5,13},{9,1},{13,5},{2,10},{6,14},... | collective-permute-start | bytes 884744 | tf_op jit(solution)/shard_map/ppermute | solution.py:458
  80.7 33.3 %collective-permute-start.23 = (bf16[384,768]{1,0:T(8,128)(2,1)S(1)}, bf16[384,768]{1,0:T(8,128)(2,1)S(1)}, u32[]{:S(2)}, u32[]{:S(2)}) collective-permute-start(bf16[384,768]{1,0:T(8,128)(2,1)S(1)} %shard_map.129.own_ref), channel_id=1, source_target_pairs={{0,16},{16,0},{1,17},{17,1},{2,18},{18,2},{3,19},{19,3},{4,20},{20... | collective-permute-start | bytes 1769480 | tf_op jit(solution)/shard_map/ppermute | solution.py:461
  80.8 11.2 %collective-permute-start.18 = (bf16[192,384]{1,0:T(8,128)(2,1)S(1)}, bf16[192,384]{1,0:T(8,128)(2,1)S(1)}, u32[]{:S(2)}, u32[]{:S(2)}) collective-permute-start(bf16[192,384]{1,0:T(8,128)(2,1)S(1)} %get-tuple-element.86), channel_id=1, source_target_pairs={{0,4},{4,0},{8,12},{12,8},{1,5},{5,1},{9,13},{13,9},{2,6},{6,2},{1... | collective-permute-start | bytes 442376 | tf_op jit(solution)/shard_map/ppermute | solution.py:458
  90.7 9.3 %collective-permute-start.15 = (bf16[192,768]{1,0:T(8,128)(2,1)S(1)}, bf16[192,768]{1,0:T(8,128)(2,1)S(1)}, u32[]{:S(2)}, u32[]{:S(2)}) collective-permute-start(bf16[192,768]{1,0:T(8,128)(2,1)S(1)} %shard_map.122), channel_id=1, source_target_pairs={{0,0},{1,4},{2,2},{3,6},{4,1},{5,5},{6,3},{7,7},{8,8},{9,12},{10,1... | collective-permute-start | bytes 884744 | tf_op jit(solution)/shard_map/ppermute | solution.py:582
  91.4 21.6 %collective-permute-start.19 = (bf16[2,192,384]{2,1,0:T(8,128)(2,1)S(1)}, bf16[2,192,384]{2,1,0:T(8,128)(2,1)S(1)}, u32[]{:S(2)}, u32[]{:S(2)}) collective-permute-start(bf16[2,192,384]{2,1,0:T(8,128)(2,1)S(1)} %get-tuple-element.89), channel_id=1, source_target_pairs={{0,8},{4,12},{8,0},{12,4},{1,9},{5,13},{9,1},{13,5},{2,10},{6,14},... | collective-permute-start | bytes 884744 | tf_op jit(solution)/shard_map/ppermute | solution.py:458
  92.1 20.9 %collective-permute-start.20 = (bf16[2,192,384]{2,1,0:T(8,128)(2,1)S(1)}, bf16[2,192,384]{2,1,0:T(8,128)(2,1)S(1)}, u32[]{:S(2)}, u32[]{:S(2)}) collective-permute-start(bf16[2,192,384]{2,1,0:T(8,128)(2,1)S(1)} %shard_map.125), channel_id=1, source_target_pairs={{0,4},{4,0},{8,12},{12,8},{1,5},{5,1},{9,13},{13,9},{2,6},{6,2},{1... | collective-permute-start | bytes 884744 | tf_op jit(solution)/shard_map/ppermute | solution.py:458
  100.8 8.0 %collective-permute-start.24 = (f32[1,768]{1,0:T(1,128)S(1)}, f32[1,768]{1,0:T(1,128)S(1)}, u32[]{:S(2)}, u32[]{:S(2)}) collective-permute-start(f32[1,768]{1,0:T(1,128)S(1)} %get-tuple-element.101), channel_id=1, source_target_pairs={{0,4},{4,0},{8,12},{12,8},{1,5},{5,1},{9,13},{13,9},{2,6},{6,2},{1... | collective-permute-start | bytes 9224 | tf_op jit(solution)/shard_map/ppermute | solution.py:458
  108.8 3.6 %collective-permute-start.25 = (f32[1,768]{1,0:T(1,128)S(1)}, f32[1,768]{1,0:T(1,128)S(1)}, u32[]{:S(2)}, u32[]{:S(2)}) collective-permute-start(f32[1,768]{1,0:T(1,128)S(1)} %add.6), channel_id=1, source_target_pairs={{0,8},{4,12},{8,0},{12,4},{1,9},{5,13},{9,1},{13,5},{2,10},{6,14},... | collective-permute-start | bytes 9224 | tf_op jit(solution)/shard_map/ppermute | solution.py:458

commit v3 on v2

--- a/solution.py
+++ b/solution.py
@@ -441,7 +441,9 @@
     gate = gate_ref[:, lane_block(lax.axis_index("tensor"), projected.shape[1])]
     branch_ref[0] = (gate * projected).astype(jnp.bfloat16)
     cot = cot_ref[0].astype(jnp.float32)
-    gate_grad_ref[...] = jnp.sum(cot * projected, axis=0, keepdims=True)
+    gate_grad = jnp.sum(cot * projected, axis=0, keepdims=True)
+    for i in range(gate_grad_ref.shape[0]):
+        gate_grad_ref[i] = gate_grad
 
 
 def square_shards(
@@ -497,19 +499,7 @@
             cotangent,
         )
     )
-    kv_xy, near_b, cot_0, cot_3, far_a, qkv_x, kv_y, query = lax.optimization_barrier(
-        (
-            permute(qkv_x[:2], "seq", 2),
-            permute(near_b, "seq", 2),
-            turn(cot_late, 0),
-            turn(cot_late, 3),
-            swap(near_a),
-            qkv_x,
-            kv_y,
-            query,
-        )
-    )
-    cots = (cot_0, cot_1, cot_2, cot_3)
+    kv_xy = permute(qkv_x[:2], "seq", 2)
     kvs = (kv, qkv_x, kv_y, kv_xy)
     block = 2 * tokens
     unit_flops = 2 * n * tokens * block * HD
@@ -521,6 +511,16 @@
         flops=6 * unit_flops,
         smem=(0,),
     )
+    near_b, cot_0, cot_3, far_a, attended = lax.optimization_barrier(
+        (
+            permute(near_b, "seq", 2),
+            turn(cot_late, 0),
+            turn(cot_late, 3),
+            swap(near_a),
+            attended,
+        )
+    )
+    cots = (cot_0, cot_1, cot_2, cot_3)
     heads = (attended, permute(attended, "seq", 1))
     grad_own, grad_send, cot_all, weight_y = call(
         functools.partial(grad_attended_kernel, n),
@@ -582,11 +582,10 @@
     projected = lax.ppermute(projected, both, home)
     branch, grad_gate = call(
         branch_kernel,
-        [shape((1, tokens, width), bf16), shape((1, width), f32)],
+        [shape((1, tokens, width), bf16), shape((n, 1, width), f32)],
         (gate_vector, cotangent, projected),
     )
-    for k in (1, 2):
-        grad_gate = grad_gate + permute(grad_gate, "seq", k)
+    grad_gate = jnp.sum(lax.all_to_all(grad_gate, "seq", 0, 0, tiled=True), axis=0)
     grad_query, grad_key, grad_value = call(
         unpack_kernel,
         [shape((1, tokens, width), bf16)] * 3,

time: 116 us -> 110 us (0.948)
  blocking collectives: 0 us -> 10.7 us
  waiting for transfers between devices: 55.3 us -> 44.8 us
  starting transfers between devices: 40.2 us -> 34.6 us
    ppermute x17 -> x15, waiting for transfers between devices: 44.2 us -> 32.2 us  [permute(): return lax.ppermute(value, axes, xor_pairs(n, k))]
    all_to_all x0 -> x1, blocking collectives: none -> 10.7 us  [square_shards(): lax.all_to_all(grad_gate, 'seq', 0, 0, tiled=True)]
    ppermute x17 -> x15, starting transfers between devices: 29.3 us -> 23.7 us  [permute(): return lax.ppermute(value, axes, xor_pairs(n, k))]
    ppermute x4, waiting for transfers between devices: 2.84 us -> 4.41 us  [swap(): return lax.ppermute(value, 'dp', xor_pairs(2, 1))]
  transfers between devices with their start and end apart: 26 -> 24, of which waited for: 14 -> 13; matrix products, arithmetic and copies ran while one was open for 1% -> 1% of each run, Pallas kernels for 7% -> 7%
where the time goes in v3:
time: 110 us
  waiting for transfers between devices  44.8 us (41%)
  starting transfers between devices  34.6 us (31%)
  Pallas kernels  16 us (15%)
  blocking collectives  10.7 us (10%)
  local copies, waits for them, and re-layouts  2.51 us (2%)
  between operations  1.45 us (1%)
    ppermute x15, waiting for transfers between devices, permute(): return lax.ppermute(value, axes, xor_pairs(n, k))  32.2 us
    ppermute x15, starting transfers between devices, permute(): return lax.ppermute(value, axes, xor_pairs(n, k))  23.7 us
    pallas_call x13, Pallas kernels, call(): pl.pallas_call(kernel, out_shape=out_shape, in_specs=[pl.BlockSpec(memory...  16 us
    all_to_all x1, blocking collectives, square_shards(): lax.all_to_all(grad_gate, 'seq', 0, 0, tiled=True)  10.7 us
    ppermute x4, starting transfers between devices, turn(): lax.ppermute(value, both, [(a * n + b, (a & 2 | b & 1) * n + (b ^ k ^ (a...  10.1 us
    ppermute x4, waiting for transfers between devices, turn(): lax.ppermute(value, both, [(a * n + b, (a & 2 | b & 1) * n + (b ^ k ^ (a...  8.21 us
    ppermute x4, waiting for transfers between devices, swap(): return lax.ppermute(value, 'dp', xor_pairs(2, 1))  4.41 us
  transfers between devices with their start and end apart: 24, of which 13 were waited for; matrix products, arithmetic and copies ran while one was open for 1% of the time, Pallas kernels for 7%

profile of v3, /device:TPU:0, one launch (start us, length us, event | category | flops | bytes accessed | tf_op | source)
XLA Modules:
  0.0 110.1 jit_solution(15062292332100930667)
XLA Ops:
  0.6 2.7 %shard_map.118 = (bf16[2,192,384]{2,1,0:T(8,128)(2,1)}, bf16[192,384]{1,0:T(8,128)(2,1)}, bf16[3,192,384]{2,1,0:T(8,128)(2,1)}, bf16[192,768]{1,0:T(8,128)(2,1)}, bf16[192,768]{1,0:T(8,128)(2,1)}) custom-call(bf16[1,192,768]{2,1,0:T(8,128)(2,1)} %q_ref.1, bf16[1,192,768]{2,1,0:T(8,128)(2,1)} %k_ref.1, bf16[1,192,768]{2,1,0:T(8,128)(2,1)} %v_ref.1, ...), custom_call_target="tpu_custom_call" | custom-call | bytes 3538944 | tf_op jit(solution)/shard_map/pallas_call | solution.py:230
  3.3 0.0 copy-start
  3.3 0.0 copy-start.2
  3.3 3.0 %collective-permute-start = (bf16[3,192,384]{2,1,0:T(8,128)(2,1)}, bf16[3,192,384]{2,1,0:T(8,128)(2,1)S(1)}, u32[]{:S(2)}, u32[]{:S(2)}) collective-permute-start(bf16[3,192,384]{2,1,0:T(8,128)(2,1)} %get-tuple-element.51), channel_id=1, source_target_pairs={{0,4},{4,0},{8,12},{12,8},{1,5},{5,1},{9,13},{13,9},{2,6},{6,2},{1... | collective-permute-start | bytes 1327112 | tf_op jit(solution)/shard_map/ppermute | solution.py:460
  6.3 1.5 %collective-permute-start.1 = (bf16[2,192,384]{2,1,0:T(8,128)(2,1)}, bf16[2,192,384]{2,1,0:T(8,128)(2,1)S(1)}, u32[]{:S(2)}, u32[]{:S(2)}) collective-permute-start(bf16[2,192,384]{2,1,0:T(8,128)(2,1)} %get-tuple-element.52.refs_0_), channel_id=1, source_target_pairs={{0,8},{4,12},{8,0},{12,4},{1,9},{5,13},{9,1},{13,5},{2,10},{6,14},... | collective-permute-start | bytes 884744 | tf_op jit(solution)/shard_map/ppermute | solution.py:460
  7.9 0.5 collective-permute-start.2
  8.4 1.6 %collective-permute-start.3 = (bf16[1,192,768]{2,1,0:T(8,128)(2,1)S(1)}, bf16[1,192,768]{2,1,0:T(8,128)(2,1)S(1)}, u32[]{:S(2)}, u32[]{:S(2)}) collective-permute-start(bf16[1,192,768]{2,1,0:T(8,128)(2,1)S(1)} %copy-done.1), channel_id=1, source_target_pairs={{0,1},{1,5},{2,3},{3,7},{4,0},{5,4},{6,2},{7,6},{8,9},{9,13},{10,1... | collective-permute-start | bytes 884744 | tf_op jit(solution)/shard_map/ppermute | solution.py:482
  9.9 2.6 %collective-permute-start.4 = (bf16[1,192,768]{2,1,0:T(8,128)(2,1)S(1)}, bf16[1,192,768]{2,1,0:T(8,128)(2,1)S(1)}, u32[]{:S(2)}, u32[]{:S(2)}) collective-permute-start(bf16[1,192,768]{2,1,0:T(8,128)(2,1)S(1)} %copy-done.1), channel_id=1, source_target_pairs={{0,2},{1,6},{2,0},{3,4},{4,3},{5,7},{6,1},{7,5},{8,10},{9,14},{10,... | collective-permute-start | bytes 884744 | tf_op jit(solution)/shard_map/ppermute | solution.py:482
  12.5 3.9 %collective-permute-done.1.refs_2_ = bf16[2,192,384]{2,1,0:T(8,128)(2,1)S(1)} collective-permute-done((bf16[2,192,384]{2,1,0:T(8,128)(2,1)}, bf16[2,192,384]{2,1,0:T(8,128)(2,1)S(1)}, u32[]{:S(2)}, u32[]{:S(2)}) %collective-permute-start.1) | collective-permute-done | bytes 294944 | tf_op jit(solution)/shard_map/ppermute | solution.py:460
  16.5 4.9 %collective-permute-done.2.refs_0_ = bf16[192,768]{1,0:T(8,128)(2,1)S(1)} collective-permute-done((bf16[192,768]{1,0:T(8,128)(2,1)}, bf16[192,768]{1,0:T(8,128)(2,1)S(1)}, u32[]{:S(2)}, u32[]{:S(2)}) %collective-permute-start.2) | collective-permute-done | bytes 294944 | tf_op jit(solution)/shard_map/ppermute | solution.py:460
  21.3 1.7 %collective-permute-done.3.refs_5_ = bf16[1,192,768]{2,1,0:T(8,128)(2,1)S(1)} collective-permute-done((bf16[1,192,768]{2,1,0:T(8,128)(2,1)S(1)}, bf16[1,192,768]{2,1,0:T(8,128)(2,1)S(1)}, u32[]{:S(2)}, u32[]{:S(2)}) %collective-permute-start.3) | collective-permute-done | bytes 294944 | tf_op jit(solution)/shard_map/ppermute | solution.py:482
  23.0 1.8 %collective-permute-done.4.refs_6_ = bf16[1,192,768]{2,1,0:T(8,128)(2,1)S(1)} collective-permute-done((bf16[1,192,768]{2,1,0:T(8,128)(2,1)S(1)}, bf16[1,192,768]{2,1,0:T(8,128)(2,1)S(1)}, u32[]{:S(2)}, u32[]{:S(2)}) %collective-permute-start.4) | collective-permute-done | bytes 294944 | tf_op jit(solution)/shard_map/ppermute | solution.py:482
  24.8 0.0 collective-permute-done.refs_1_
  24.8 1.6 %collective-permute-start.9 = (bf16[2,192,384]{2,1,0:T(8,128)(2,1)S(1)}, bf16[2,192,384]{2,1,0:T(8,128)(2,1)S(1)}, u32[]{:S(2)}, u32[]{:S(2)}) collective-permute-start(bf16[2,192,384]{2,1,0:T(8,128)(2,1)S(1)} %slice.3), channel_id=1, source_target_pairs={{0,8},{4,12},{8,0},{12,4},{1,9},{5,13},{9,1},{13,5},{2,10},{6,14},... | collective-permute-start | bytes 884744 | tf_op jit(solution)/shard_map/ppermute | solution.py:460
  26.4 0.5 collective-permute-start.5
  26.9 0.7 collective-permute-start.6
  27.6 5.3 %collective-permute-start.7 = (bf16[1,192,768]{2,1,0:T(8,128)(2,1)S(1)}, bf16[1,192,768]{2,1,0:T(8,128)(2,1)S(1)}, u32[]{:S(2)}, u32[]{:S(2)}) collective-permute-start(bf16[1,192,768]{2,1,0:T(8,128)(2,1)S(1)} %copy-done.1), channel_id=1, source_target_pairs={{0,3},{1,7},{2,1},{3,5},{4,2},{5,6},{6,0},{7,4},{8,11},{9,15},{10,... | collective-permute-start | bytes 884744 | tf_op jit(solution)/shard_map/ppermute | solution.py:482
  32.9 0.0 collective-permute-start.8
  33.5 1.3 %collective-permute-done.9.refs_3_ = bf16[2,192,384]{2,1,0:T(8,128)(2,1)S(1)} collective-permute-done((bf16[2,192,384]{2,1,0:T(8,128)(2,1)S(1)}, bf16[2,192,384]{2,1,0:T(8,128)(2,1)S(1)}, u32[]{:S(2)}, u32[]{:S(2)}) %collective-permute-start.9) | collective-permute-done | bytes 294944 | tf_op jit(solution)/shard_map/ppermute | solution.py:460
  34.8 1.0 copy-done.3
  35.8 0.9 copy-done.5
  36.7 2.0 %shard_map.119 = (bf16[2,192,384]{2,1,0:T(8,128)(2,1)S(1)}, f32[3,384]{1,0:T(4,128)S(1)}) custom-call(s32[1]{0:T(128)S(6)} %copy.13.len_ref, bf16[2,192,384]{2,1,0:T(8,128)(2,1)S(1)} %copy-done.3, bf16[3,192,384]{2,1,0:T(8,128)(2,1)S(1)} %collective-permute-done.refs_1_, bf16[2,192,384]{2,1,0:T(8,128)(2,1)S(1)} %collective-permute-done.1.refs_2_, ...), custom_call_target="tpu_custom_call" | custom-call | flops 452984832 | bytes 1774084 | tf_op jit(solution)/shard_map/pallas_call | solution.py:230
  38.7 0.6 collective-permute-done.5.refs_1_
  39.3 0.0 collective-permute-done.6.refs_4_
  39.3 4.8 %collective-permute-done.7.refs_7_ = bf16[1,192,768]{2,1,0:T(8,128)(2,1)S(1)} collective-permute-done((bf16[1,192,768]{2,1,0:T(8,128)(2,1)S(1)}, bf16[1,192,768]{2,1,0:T(8,128)(2,1)S(1)}, u32[]{:S(2)}, u32[]{:S(2)}) %collective-permute-start.7) | collective-permute-done | bytes 294944 | tf_op jit(solution)/shard_map/ppermute | solution.py:482
  44.0 0.0 collective-permute-done.8.refs_2_
  44.0 0.0 collective-permute-start.10
  44.1 0.0 collective-permute-start.11
  44.1 1.6 %collective-permute-done.10.refs_3_ = bf16[192,768]{1,0:T(8,128)(2,1)S(1)} collective-permute-done((bf16[192,768]{1,0:T(8,128)(2,1)S(1)}, bf16[192,768]{1,0:T(8,128)(2,1)S(1)}, u32[]{:S(2)}, u32[]{:S(2)}) %collective-permute-start.10) | collective-permute-done | bytes 294944 | tf_op jit(solution)/shard_map/ppermute | solution.py:463
  45.6 1.4 %shard_map.120 = (f32[2,192,384]{2,1,0:T(8,128)S(1)}, bf16[2,192,384]{2,1,0:T(8,128)(2,1)S(1)}, bf16[4,192,768]{2,1,0:T(8,128)(2,1)S(1)}, bf16[768,768]{1,0:T(8,128)(2,1)S(1)}) custom-call(f32[1,3072]{1,0:T(1,128)S(1)} %copy-done.2, bf16[768,768]{1,0:T(8,128)(2,1)S(1)} %copy-done, bf16[192,768]{1,0:T(8,128)(2,1)S(1)} %collective-permute-done.2.refs_0_, ...), custom_call_target="tpu_custom_call" | custom-call | flops 905969664 | bytes 6795264 | tf_op jit(solution)/shard_map/pallas_call | solution.py:230
  47.0 6.5 %collective-permute-done.11.other_ref = bf16[2,192,384]{2,1,0:T(8,128)(2,1)S(1)} collective-permute-done((bf16[2,192,384]{2,1,0:T(8,128)(2,1)S(1)}, bf16[2,192,384]{2,1,0:T(8,128)(2,1)S(1)}, u32[]{:S(2)}, u32[]{:S(2)}) %collective-permute-start.11) | collective-permute-done | bytes 294944 | tf_op jit(solution)/shard_map/ppermute | solution.py:460
  53.5 1.3 %shard_map.121 = (f32[192,768]{1,0:T(8,128)S(1)}, bf16[192,768]{1,0:T(8,128)(2,1)S(1)}, bf16[192,768]{1,0:T(8,128)(2,1)S(1)}, bf16[192,768]{1,0:T(8,128)(2,1)S(1)}, bf16[384,768]{1,0:T(8,128)(2,1)S(1)}) custom-call(bf16[768,768]{1,0:T(8,128)(2,1)S(1)} %copy-done, bf16[768,768]{1,0:T(8,128)(2,1)S(1)} %get-tuple-element.68.w2_ref, ...), custom_call_target="tpu_custom_call" | custom-call | flops 905969664 | bytes 5013504 | tf_op jit(solution)/shard_map/pallas_call | solution.py:230
  54.7 2.0 %shard_map.127 = (f32[2,384,768]{2,1,0:T(8,128)S(1)}, bf16[2,384,768]{2,1,0:T(8,128)(2,1)S(1)}) custom-call(f32[1,3072]{1,0:T(1,128)S(1)} %copy-done.2, bf16[384,768]{1,0:T(8,128)(2,1)S(1)} %get-tuple-element.89.all_ref, bf16[4,192,768]{2,1,0:T(8,128)(2,1)S(1)} %get-tuple-element.90.cot_ref), custom_call_target="tpu_custom_call" | custom-call | flops 905969664 | bytes 5320704 | tf_op jit(solution)/shard_map/pallas_call | solution.py:230
  56.8 0.1 collective-permute-start.21
  56.8 2.8 %collective-permute-done.21.other_ref = bf16[2,384,768]{2,1,0:T(8,128)(2,1)S(1)} collective-permute-done((bf16[2,384,768]{2,1,0:T(8,128)(2,1)S(1)}, bf16[2,384,768]{2,1,0:T(8,128)(2,1)S(1)}, u32[]{:S(2)}, u32[]{:S(2)}) %collective-permute-start.21) | collective-permute-done | bytes 1179680 | tf_op jit(solution)/shard_map/ppermute | solution.py:463
  59.7 0.3 shard_map.128
  59.9 1.6 %collective-permute-start.22 = (bf16[384,768]{1,0:T(8,128)(2,1)S(1)}, bf16[384,768]{1,0:T(8,128)(2,1)S(1)}, u32[]{:S(2)}, u32[]{:S(2)}) collective-permute-start(bf16[384,768]{1,0:T(8,128)(2,1)S(1)} %get-tuple-element.94), channel_id=1, source_target_pairs={{0,8},{4,12},{8,0},{12,4},{1,9},{5,13},{9,1},{13,5},{2,10},{6,14},... | collective-permute-start | bytes 1769480 | tf_op jit(solution)/shard_map/ppermute | solution.py:460
  61.5 0.3 collective-permute-start.16
  61.8 0.6 collective-permute-start.12
  62.5 2.3 %collective-permute-start.13 = (bf16[192,768]{1,0:T(8,128)(2,1)S(1)}, bf16[192,768]{1,0:T(8,128)(2,1)S(1)}, u32[]{:S(2)}, u32[]{:S(2)}) collective-permute-start(bf16[192,768]{1,0:T(8,128)(2,1)S(1)} %get-tuple-element.72), channel_id=1, source_target_pairs={{0,2},{1,3},{2,0},{3,1},{4,6},{5,7},{6,4},{7,5},{8,10},{9,11},{10,... | collective-permute-start | bytes 884744 | tf_op jit(solution)/shard_map/ppermute | solution.py:460
  64.7 1.5 %collective-permute-start.14 = (bf16[192,768]{1,0:T(8,128)(2,1)S(1)}, bf16[192,768]{1,0:T(8,128)(2,1)S(1)}, u32[]{:S(2)}, u32[]{:S(2)}) collective-permute-start(bf16[192,768]{1,0:T(8,128)(2,1)S(1)} %get-tuple-element.73), channel_id=1, source_target_pairs={{0,3},{1,2},{2,1},{3,0},{4,7},{5,6},{6,5},{7,4},{8,11},{9,10},{10,... | collective-permute-start | bytes 884744 | tf_op jit(solution)/shard_map/ppermute | solution.py:460
  66.2 4.1 %collective-permute-done.16.other_ref = bf16[2,192,384]{2,1,0:T(8,128)(2,1)S(1)} collective-permute-done((bf16[2,192,384]{2,1,0:T(8,128)(2,1)S(1)}, bf16[2,192,384]{2,1,0:T(8,128)(2,1)S(1)}, u32[]{:S(2)}, u32[]{:S(2)}) %collective-permute-start.16) | collective-permute-done | bytes 294944 | tf_op jit(solution)/shard_map/ppermute | solution.py:460
  70.3 2.7 %shard_map.124 = (bf16[192,384]{1,0:T(8,128)(2,1)S(1)}, bf16[192,384]{1,0:T(8,128)(2,1)S(1)}, f32[2,192,384]{2,1,0:T(8,128)S(1)}, f32[2,192,384]{2,1,0:T(8,128)S...) custom-call(s32[1]{0:T(128)S(6)} %copy.13.len_ref, f32[3,384]{1,0:T(4,128)S(1)} %get-tuple-element.75.lse_ref, ...), custom_call_target="tpu_custom_call" | custom-call | flops 1132462080 | bytes 4723204 | tf_op jit(solution)/shard_map/pallas_call | solution.py:230
  73.0 0.6 collective-permute-start.17
  73.6 2.4 %collective-permute-done.22.other_ref = bf16[384,768]{1,0:T(8,128)(2,1)S(1)} collective-permute-done((bf16[384,768]{1,0:T(8,128)(2,1)S(1)}, bf16[384,768]{1,0:T(8,128)(2,1)S(1)}, u32[]{:S(2)}, u32[]{:S(2)}) %collective-permute-start.22) | collective-permute-done | bytes 589856 | tf_op jit(solution)/shard_map/ppermute | solution.py:460
  76.0 0.1 shard_map.129.own_ref
  76.1 0.1 collective-permute-start.23
  76.2 1.2 %collective-permute-start.18 = (bf16[192,384]{1,0:T(8,128)(2,1)S(1)}, bf16[192,384]{1,0:T(8,128)(2,1)S(1)}, u32[]{:S(2)}, u32[]{:S(2)}) collective-permute-start(bf16[192,384]{1,0:T(8,128)(2,1)S(1)} %get-tuple-element.80), channel_id=1, source_target_pairs={{0,4},{4,0},{8,12},{12,8},{1,5},{5,1},{9,13},{13,9},{2,6},{6,2},{1... | collective-permute-start | bytes 442376 | tf_op jit(solution)/shard_map/ppermute | solution.py:460
  77.5 8.5 %collective-permute-done.13.refs_1_ = bf16[192,768]{1,0:T(8,128)(2,1)S(1)} collective-permute-done((bf16[192,768]{1,0:T(8,128)(2,1)S(1)}, bf16[192,768]{1,0:T(8,128)(2,1)S(1)}, u32[]{:S(2)}, u32[]{:S(2)}) %collective-permute-start.13) | collective-permute-done | bytes 294944 | tf_op jit(solution)/shard_map/ppermute | solution.py:460
  85.9 0.0 collective-permute-done.14.refs_2_
  85.9 0.2 shard_map.122
  86.1 0.7 collective-permute-start.15
  86.8 0.6 collective-permute-start.19
  87.4 0.0 collective-permute-done.18.dq_other_ref
  87.4 0.0 collective-permute-done.17.other_ref
  87.4 0.1 shard_map.125
  87.5 7.9 %collective-permute-start.20 = (bf16[2,192,384]{2,1,0:T(8,128)(2,1)S(1)}, bf16[2,192,384]{2,1,0:T(8,128)(2,1)S(1)}, u32[]{:S(2)}, u32[]{:S(2)}) collective-permute-start(bf16[2,192,384]{2,1,0:T(8,128)(2,1)S(1)} %shard_map.125), channel_id=1, source_target_pairs={{0,4},{4,0},{8,12},{12,8},{1,5},{5,1},{9,13},{13,9},{2,6},{6,2},{1... | collective-permute-start | bytes 884744 | tf_op jit(solution)/shard_map/ppermute | solution.py:460
  95.4 0.0 collective-permute-done.15.projected_ref
  95.4 0.8 shard_map.123
  96.2 10.7 %all_to_all.5 = f32[4,1,768]{2,1,0:T(1,128)S(1)} all-to-all(f32[4,1,768]{2,1,0:T(1,128)S(1)} %get-tuple-element.95), channel_id=1, replica_groups=mesh['dp'=2,'seq'=4,'tensor'=4] {'seq'}, dimensions={0} | all-to-all | bytes 24576 | tf_op jit(solution)/shard_map/all_to_all | solution.py:588
  106.9 0.6 reduce_sum.12
  107.5 0.0 collective-permute-done.19.part_ref
  107.5 1.0 shard_map.126
  108.5 1.6 %shard_map.130 = f32[768,768]{1,0:T(8,128)} custom-call(bf16[384,768]{1,0:T(8,128)(2,1)S(1)} %shard_map.129.own_ref, bf16[384,768]{1,0:T(8,128)(2,1)S(1)} %collective-permute-done.23.other_ref), custom_call_target="tpu_custom_call" | custom-call | bytes 3538944 | tf_op jit(solution)/shard_map/pallas_call | solution.py:230
  (15 shorter events, 0.1 us)
Async XLA Ops:
  0.6 7.7 %copy-start.1 = (bf16[1,192,768]{2,1,0:T(8,128)(2,1)S(1)}, bf16[1,192,768]{2,1,0:T(8,128)(2,1)}, u32[]{:S(2)}) copy-start(bf16[1,192,768]{2,1,0:T(8,128)(2,1)} %cot_ref.1) | copy-start | bytes 884740
  3.3 42.3 %copy-start = (bf16[768,768]{1,0:T(8,128)(2,1)S(1)}, bf16[768,768]{1,0:T(8,128)(2,1)}, u32[]{:S(2)}) copy-start(bf16[768,768]{1,0:T(8,128)(2,1)} %w_ref.5) | copy-start | bytes 3538948
  3.3 42.3 %copy-start.2 = (f32[1,3072]{1,0:T(1,128)S(1)}, f32[1,3072]{1,0:T(1,128)}, u32[]{:S(2)}) copy-start(f32[1,3072]{1,0:T(1,128)} %gate_ref.5) | copy-start | bytes 36868
  3.3 21.5 %collective-permute-start = (bf16[3,192,384]{2,1,0:T(8,128)(2,1)}, bf16[3,192,384]{2,1,0:T(8,128)(2,1)S(1)}, u32[]{:S(2)}, u32[]{:S(2)}) collective-permute-start(bf16[3,192,384]{2,1,0:T(8,128)(2,1)} %get-tuple-element.51), channel_id=1, source_target_pairs={{0,4},{4,0},{8,12},{12,8},{1,5},{5,1},{9,13},{13,9},{2,6},{6,2},{1... | collective-permute-start | bytes 1327112 | tf_op jit(solution)/shard_map/ppermute | solution.py:460
  6.3 10.1 %collective-permute-start.1 = (bf16[2,192,384]{2,1,0:T(8,128)(2,1)}, bf16[2,192,384]{2,1,0:T(8,128)(2,1)S(1)}, u32[]{:S(2)}, u32[]{:S(2)}) collective-permute-start(bf16[2,192,384]{2,1,0:T(8,128)(2,1)} %get-tuple-element.52.refs_0_), channel_id=1, source_target_pairs={{0,8},{4,12},{8,0},{12,4},{1,9},{5,13},{9,1},{13,5},{2,10},{6,14},... | collective-permute-start | bytes 884744 | tf_op jit(solution)/shard_map/ppermute | solution.py:460
  7.9 13.5 %collective-permute-start.2 = (bf16[192,768]{1,0:T(8,128)(2,1)}, bf16[192,768]{1,0:T(8,128)(2,1)S(1)}, u32[]{:S(2)}, u32[]{:S(2)}) collective-permute-start(bf16[192,768]{1,0:T(8,128)(2,1)} %get-tuple-element.53), channel_id=1, source_target_pairs={{0,8},{4,12},{8,0},{12,4},{1,9},{5,13},{9,1},{13,5},{2,10},{6,14},... | collective-permute-start | bytes 884744 | tf_op jit(solution)/shard_map/ppermute | solution.py:460
  8.4 14.7 %collective-permute-start.3 = (bf16[1,192,768]{2,1,0:T(8,128)(2,1)S(1)}, bf16[1,192,768]{2,1,0:T(8,128)(2,1)S(1)}, u32[]{:S(2)}, u32[]{:S(2)}) collective-permute-start(bf16[1,192,768]{2,1,0:T(8,128)(2,1)S(1)} %copy-done.1), channel_id=1, source_target_pairs={{0,1},{1,5},{2,3},{3,7},{4,0},{5,4},{6,2},{7,6},{8,9},{9,13},{10,1... | collective-permute-start | bytes 884744 | tf_op jit(solution)/shard_map/ppermute | solution.py:482
  9.9 14.8 %collective-permute-start.4 = (bf16[1,192,768]{2,1,0:T(8,128)(2,1)S(1)}, bf16[1,192,768]{2,1,0:T(8,128)(2,1)S(1)}, u32[]{:S(2)}, u32[]{:S(2)}) collective-permute-start(bf16[1,192,768]{2,1,0:T(8,128)(2,1)S(1)} %copy-done.1), channel_id=1, source_target_pairs={{0,2},{1,6},{2,0},{3,4},{4,3},{5,7},{6,1},{7,5},{8,10},{9,14},{10,... | collective-permute-start | bytes 884744 | tf_op jit(solution)/shard_map/ppermute | solution.py:482
  24.8 10.0 %collective-permute-start.9 = (bf16[2,192,384]{2,1,0:T(8,128)(2,1)S(1)}, bf16[2,192,384]{2,1,0:T(8,128)(2,1)S(1)}, u32[]{:S(2)}, u32[]{:S(2)}) collective-permute-start(bf16[2,192,384]{2,1,0:T(8,128)(2,1)S(1)} %slice.3), channel_id=1, source_target_pairs={{0,8},{4,12},{8,0},{12,4},{1,9},{5,13},{9,1},{13,5},{2,10},{6,14},... | collective-permute-start | bytes 884744 | tf_op jit(solution)/shard_map/ppermute | solution.py:460
  26.4 12.9 %collective-permute-start.5 = (bf16[192,768]{1,0:T(8,128)(2,1)}, bf16[192,768]{1,0:T(8,128)(2,1)S(1)}, u32[]{:S(2)}, u32[]{:S(2)}) collective-permute-start(bf16[192,768]{1,0:T(8,128)(2,1)} %get-tuple-element.56), channel_id=1, source_target_pairs={{0,8},{4,12},{8,0},{12,4},{1,9},{5,13},{9,1},{13,5},{2,10},{6,14},... | collective-permute-start | bytes 884744 | tf_op jit(solution)/shard_map/ppermute | solution.py:460
  26.9 12.4 %collective-permute-start.6 = (bf16[1,192,768]{2,1,0:T(8,128)(2,1)S(1)}, bf16[1,192,768]{2,1,0:T(8,128)(2,1)S(1)}, u32[]{:S(2)}, u32[]{:S(2)}) collective-permute-start(bf16[1,192,768]{2,1,0:T(8,128)(2,1)S(1)} %copy-done.1), channel_id=1, source_target_pairs={{0,0},{1,4},{2,2},{3,6},{4,1},{5,5},{6,3},{7,7},{8,8},{9,12},{10,1... | collective-permute-start | bytes 884744 | tf_op jit(solution)/shard_map/ppermute | solution.py:482
  27.6 16.5 %collective-permute-start.7 = (bf16[1,192,768]{2,1,0:T(8,128)(2,1)S(1)}, bf16[1,192,768]{2,1,0:T(8,128)(2,1)S(1)}, u32[]{:S(2)}, u32[]{:S(2)}) collective-permute-start(bf16[1,192,768]{2,1,0:T(8,128)(2,1)S(1)} %copy-done.1), channel_id=1, source_target_pairs={{0,3},{1,7},{2,1},{3,5},{4,2},{5,6},{6,0},{7,4},{8,11},{9,15},{10,... | collective-permute-start | bytes 884744 | tf_op jit(solution)/shard_map/ppermute | solution.py:482
  32.9 11.2 %collective-permute-start.8 = (bf16[192,768]{1,0:T(8,128)(2,1)S(1)}, bf16[192,768]{1,0:T(8,128)(2,1)S(1)}, u32[]{:S(2)}, u32[]{:S(2)}) collective-permute-start(bf16[192,768]{1,0:T(8,128)(2,1)S(1)} %collective-permute-done.2.refs_0_), channel_id=1, source_target_pairs={{0,16},{16,0},{1,17},{17,1},{2,18},{18,2},{3,19},{19,3},{4,20},{20... | collective-permute-start | bytes 884744 | tf_op jit(solution)/shard_map/ppermute | solution.py:463
  34.8 1.0 copy-start.3
  35.8 0.9 copy-start.5
  44.0 1.6 %collective-permute-start.10 = (bf16[192,768]{1,0:T(8,128)(2,1)S(1)}, bf16[192,768]{1,0:T(8,128)(2,1)S(1)}, u32[]{:S(2)}, u32[]{:S(2)}) collective-permute-start(bf16[192,768]{1,0:T(8,128)(2,1)S(1)} %collective-permute-done.5.refs_1_), channel_id=1, source_target_pairs={{0,16},{16,0},{1,17},{17,1},{2,18},{18,2},{3,19},{19,3},{4,20},{20... | collective-permute-start | bytes 884744 | tf_op jit(solution)/shard_map/ppermute | solution.py:463
  44.1 9.4 %collective-permute-start.11 = (bf16[2,192,384]{2,1,0:T(8,128)(2,1)S(1)}, bf16[2,192,384]{2,1,0:T(8,128)(2,1)S(1)}, u32[]{:S(2)}, u32[]{:S(2)}) collective-permute-start(bf16[2,192,384]{2,1,0:T(8,128)(2,1)S(1)} %get-tuple-element.69.o_ref), channel_id=1, source_target_pairs={{0,4},{4,0},{8,12},{12,8},{1,5},{5,1},{9,13},{13,9},{2,6},{6,2},{1... | collective-permute-start | bytes 884744 | tf_op jit(solution)/shard_map/ppermute | solution.py:460
  56.8 2.9 %collective-permute-start.21 = (bf16[2,384,768]{2,1,0:T(8,128)(2,1)S(1)}, bf16[2,384,768]{2,1,0:T(8,128)(2,1)S(1)}, u32[]{:S(2)}, u32[]{:S(2)}) collective-permute-start(bf16[2,384,768]{2,1,0:T(8,128)(2,1)S(1)} %get-tuple-element.92), channel_id=1, source_target_pairs={{0,16},{16,0},{1,17},{17,1},{2,18},{18,2},{3,19},{19,3},{4,20},{20... | collective-permute-start | bytes 3538952 | tf_op jit(solution)/shard_map/ppermute | solution.py:463
  59.7 10.6 %copy-start.4 = (bf16[2,192,384]{2,1,0:T(8,128)(2,1)S(1)}, bf16[2,192,384]{2,1,0:T(8,128)(2,1)}, u32[]{:S(2)}) copy-start(bf16[2,192,384]{2,1,0:T(8,128)(2,1)} %get-tuple-element.52.refs_0_) | copy-start | bytes 884740
  59.7 10.6 %copy-start.6 = (bf16[192,384]{1,0:T(8,128)(2,1)S(1)}, bf16[192,384]{1,0:T(8,128)(2,1)}, u32[]{:S(2)}) copy-start(bf16[192,384]{1,0:T(8,128)(2,1)} %get-tuple-element.60.refs_4_) | copy-start | bytes 442372
  59.9 16.1 %collective-permute-start.22 = (bf16[384,768]{1,0:T(8,128)(2,1)S(1)}, bf16[384,768]{1,0:T(8,128)(2,1)S(1)}, u32[]{:S(2)}, u32[]{:S(2)}) collective-permute-start(bf16[384,768]{1,0:T(8,128)(2,1)S(1)} %get-tuple-element.94), channel_id=1, source_target_pairs={{0,8},{4,12},{8,0},{12,4},{1,9},{5,13},{9,1},{13,5},{2,10},{6,14},... | collective-permute-start | bytes 1769480 | tf_op jit(solution)/shard_map/ppermute | solution.py:460
  61.5 8.8 %collective-permute-start.16 = (bf16[2,192,384]{2,1,0:T(8,128)(2,1)S(1)}, bf16[2,192,384]{2,1,0:T(8,128)(2,1)S(1)}, u32[]{:S(2)}, u32[]{:S(2)}) collective-permute-start(bf16[2,192,384]{2,1,0:T(8,128)(2,1)S(1)} %get-tuple-element.77), channel_id=1, source_target_pairs={{0,4},{4,0},{8,12},{12,8},{1,5},{5,1},{9,13},{13,9},{2,6},{6,2},{1... | collective-permute-start | bytes 884744 | tf_op jit(solution)/shard_map/ppermute | solution.py:460
  61.8 14.4 %collective-permute-start.12 = (bf16[192,768]{1,0:T(8,128)(2,1)S(1)}, bf16[192,768]{1,0:T(8,128)(2,1)S(1)}, u32[]{:S(2)}, u32[]{:S(2)}) collective-permute-start(bf16[192,768]{1,0:T(8,128)(2,1)S(1)} %get-tuple-element.71), channel_id=1, source_target_pairs={{0,1},{1,0},{2,3},{3,2},{4,5},{5,4},{6,7},{7,6},{8,9},{9,8},{10,11... | collective-permute-start | bytes 884744 | tf_op jit(solution)/shard_map/ppermute | solution.py:460
  62.5 23.5 %collective-permute-start.13 = (bf16[192,768]{1,0:T(8,128)(2,1)S(1)}, bf16[192,768]{1,0:T(8,128)(2,1)S(1)}, u32[]{:S(2)}, u32[]{:S(2)}) collective-permute-start(bf16[192,768]{1,0:T(8,128)(2,1)S(1)} %get-tuple-element.72), channel_id=1, source_target_pairs={{0,2},{1,3},{2,0},{3,1},{4,6},{5,7},{6,4},{7,5},{8,10},{9,11},{10,... | collective-permute-start | bytes 884744 | tf_op jit(solution)/shard_map/ppermute | solution.py:460
  64.7 21.2 %collective-permute-start.14 = (bf16[192,768]{1,0:T(8,128)(2,1)S(1)}, bf16[192,768]{1,0:T(8,128)(2,1)S(1)}, u32[]{:S(2)}, u32[]{:S(2)}) collective-permute-start(bf16[192,768]{1,0:T(8,128)(2,1)S(1)} %get-tuple-element.73), channel_id=1, source_target_pairs={{0,3},{1,2},{2,1},{3,0},{4,7},{5,6},{6,5},{7,4},{8,11},{9,10},{10,... | collective-permute-start | bytes 884744 | tf_op jit(solution)/shard_map/ppermute | solution.py:460
  73.0 14.3 %collective-permute-start.17 = (bf16[2,192,384]{2,1,0:T(8,128)(2,1)S(1)}, bf16[2,192,384]{2,1,0:T(8,128)(2,1)S(1)}, u32[]{:S(2)}, u32[]{:S(2)}) collective-permute-start(bf16[2,192,384]{2,1,0:T(8,128)(2,1)S(1)} %get-tuple-element.79), channel_id=1, source_target_pairs={{0,8},{4,12},{8,0},{12,4},{1,9},{5,13},{9,1},{13,5},{2,10},{6,14},... | collective-permute-start | bytes 884744 | tf_op jit(solution)/shard_map/ppermute | solution.py:460
  76.1 32.4 %collective-permute-start.23 = (bf16[384,768]{1,0:T(8,128)(2,1)S(1)}, bf16[384,768]{1,0:T(8,128)(2,1)S(1)}, u32[]{:S(2)}, u32[]{:S(2)}) collective-permute-start(bf16[384,768]{1,0:T(8,128)(2,1)S(1)} %shard_map.129.own_ref), channel_id=1, source_target_pairs={{0,16},{16,0},{1,17},{17,1},{2,18},{18,2},{3,19},{19,3},{4,20},{20... | collective-permute-start | bytes 1769480 | tf_op jit(solution)/shard_map/ppermute | solution.py:463
  76.2 11.1 %collective-permute-start.18 = (bf16[192,384]{1,0:T(8,128)(2,1)S(1)}, bf16[192,384]{1,0:T(8,128)(2,1)S(1)}, u32[]{:S(2)}, u32[]{:S(2)}) collective-permute-start(bf16[192,384]{1,0:T(8,128)(2,1)S(1)} %get-tuple-element.80), channel_id=1, source_target_pairs={{0,4},{4,0},{8,12},{12,8},{1,5},{5,1},{9,13},{13,9},{2,6},{6,2},{1... | collective-permute-start | bytes 442376 | tf_op jit(solution)/shard_map/ppermute | solution.py:460
  86.1 9.3 %collective-permute-start.15 = (bf16[192,768]{1,0:T(8,128)(2,1)S(1)}, bf16[192,768]{1,0:T(8,128)(2,1)S(1)}, u32[]{:S(2)}, u32[]{:S(2)}) collective-permute-start(bf16[192,768]{1,0:T(8,128)(2,1)S(1)} %shard_map.122), channel_id=1, source_target_pairs={{0,0},{1,4},{2,2},{3,6},{4,1},{5,5},{6,3},{7,7},{8,8},{9,12},{10,1... | collective-permute-start | bytes 884744 | tf_op jit(solution)/shard_map/ppermute | solution.py:582
  86.8 20.7 %collective-permute-start.19 = (bf16[2,192,384]{2,1,0:T(8,128)(2,1)S(1)}, bf16[2,192,384]{2,1,0:T(8,128)(2,1)S(1)}, u32[]{:S(2)}, u32[]{:S(2)}) collective-permute-start(bf16[2,192,384]{2,1,0:T(8,128)(2,1)S(1)} %get-tuple-element.83), channel_id=1, source_target_pairs={{0,8},{4,12},{8,0},{12,4},{1,9},{5,13},{9,1},{13,5},{2,10},{6,14},... | collective-permute-start | bytes 884744 | tf_op jit(solution)/shard_map/ppermute | solution.py:460
  87.5 20.1 %collective-permute-start.20 = (bf16[2,192,384]{2,1,0:T(8,128)(2,1)S(1)}, bf16[2,192,384]{2,1,0:T(8,128)(2,1)S(1)}, u32[]{:S(2)}, u32[]{:S(2)}) collective-permute-start(bf16[2,192,384]{2,1,0:T(8,128)(2,1)S(1)} %shard_map.125), channel_id=1, source_target_pairs={{0,4},{4,0},{8,12},{12,8},{1,5},{5,1},{9,13},{13,9},{2,6},{6,2},{1... | collective-permute-start | bytes 884744 | tf_op jit(solution)/shard_map/ppermute | solution.py:460

commit v4 on v3

--- a/solution.py
+++ b/solution.py
@@ -580,6 +580,7 @@
     )
     home = [(a * n + b, (a ^ 1) * n + (b ^ 1) if (a ^ b) & 1 else a * n + b) for a, b in both_pairs]
     projected = lax.ppermute(projected, both, home)
+    projected, grad_weight = lax.optimization_barrier((projected, grad_weight))
     branch, grad_gate = call(
         branch_kernel,
         [shape((1, tokens, width), bf16), shape((n, 1, width), f32)],

time: 110 us -> 108 us (0.982)
  blocking collectives: 10.7 us -> 0 us
  waiting for transfers between devices: 44.8 us -> 50 us
  starting transfers between devices: 34.6 us -> 36.5 us
    all_to_all x1 -> x0, blocking collectives: 10.7 us -> none  [square_shards(): lax.all_to_all(grad_gate, 'seq', 0, 0, tiled=True)]
    all_to_all x0 -> x1, starting transfers between devices: none -> 4.59 us  [square_shards(): lax.all_to_all(grad_gate, 'seq', 0, 0, tiled=True)]
    all_to_all x0 -> x1, waiting for transfers between devices: none -> 2.87 us  [square_shards(): lax.all_to_all(grad_gate, 'seq', 0, 0, tiled=True)]
    ppermute x15, starting transfers between devices: 23.7 us -> 21 us  [permute(): return lax.ppermute(value, axes, xor_pairs(n, k))]
    ppermute x4, waiting for transfers between devices: 8.21 us -> 9.84 us  [turn(): lax.ppermute(value, both, [(a * n + b, (a & 2 | b & 1) * n + (b ^ k ^ (a...]
  transfers between devices with their start and end apart: 24 -> 25, of which waited for: 13 -> 13; matrix products, arithmetic and copies ran while one was open for 1% -> 0% of each run, Pallas kernels for 7% -> 9%
where the time goes in v4:
time: 108 us; the launch traced here: 107 us
  waiting for transfers between devices  50 us (46%)
  starting transfers between devices  36.5 us (34%)
  Pallas kernels  16 us (15%)
  local copies, waits for them, and re-layouts  3.3 us (3%)
  between operations  1.48 us (1%)
    ppermute x15, waiting for transfers between devices, permute(): return lax.ppermute(value, axes, xor_pairs(n, k))  33 us
    ppermute x15, starting transfers between devices, permute(): return lax.ppermute(value, axes, xor_pairs(n, k))  21 us
    pallas_call x13, Pallas kernels, call(): pl.pallas_call(kernel, out_shape=out_shape, in_specs=[pl.BlockSpec(memory...  16 us
    ppermute x4, starting transfers between devices, turn(): lax.ppermute(value, both, [(a * n + b, (a & 2 | b & 1) * n + (b ^ k ^ (a...  10.1 us
    ppermute x4, waiting for transfers between devices, turn(): lax.ppermute(value, both, [(a * n + b, (a & 2 | b & 1) * n + (b ^ k ^ (a...  9.84 us
    all_to_all x1, starting transfers between devices, square_shards(): lax.all_to_all(grad_gate, 'seq', 0, 0, tiled=True)  4.59 us
    ppermute x4, waiting for transfers between devices, swap(): return lax.ppermute(value, 'dp', xor_pairs(2, 1))  4.34 us
    all_to_all x1, waiting for transfers between devices, square_shards(): lax.all_to_all(grad_gate, 'seq', 0, 0, tiled=True)  2.87 us
  transfers between devices with their start and end apart: 25, of which 13 were waited for; matrix products, arithmetic and copies ran while one was open for 0% of the time, Pallas kernels for 9%

profile of v4, /device:TPU:0, one launch (start us, length us, event | category | flops | bytes accessed | tf_op | source)
XLA Modules:
  0.0 107.4 jit_solution(14689952142814065909)
XLA Ops:
  0.6 2.7 %shard_map.118 = (bf16[2,192,384]{2,1,0:T(8,128)(2,1)}, bf16[192,384]{1,0:T(8,128)(2,1)}, bf16[3,192,384]{2,1,0:T(8,128)(2,1)}, bf16[192,768]{1,0:T(8,128)(2,1)}, bf16[192,768]{1,0:T(8,128)(2,1)}) custom-call(bf16[1,192,768]{2,1,0:T(8,128)(2,1)} %q_ref.1, bf16[1,192,768]{2,1,0:T(8,128)(2,1)} %k_ref.1, bf16[1,192,768]{2,1,0:T(8,128)(2,1)} %v_ref.1, ...), custom_call_target="tpu_custom_call" | custom-call | bytes 3538944 | tf_op jit(solution)/shard_map/pallas_call | solution.py:230
  3.3 0.0 copy-start
  3.3 0.0 copy-start.2
  3.3 3.0 %collective-permute-start = (bf16[3,192,384]{2,1,0:T(8,128)(2,1)}, bf16[3,192,384]{2,1,0:T(8,128)(2,1)S(1)}, u32[]{:S(2)}, u32[]{:S(2)}) collective-permute-start(bf16[3,192,384]{2,1,0:T(8,128)(2,1)} %get-tuple-element.53), channel_id=1, source_target_pairs={{0,4},{4,0},{8,12},{12,8},{1,5},{5,1},{9,13},{13,9},{2,6},{6,2},{1... | collective-permute-start | bytes 1327112 | tf_op jit(solution)/shard_map/ppermute | solution.py:460
  6.3 1.5 %collective-permute-start.1 = (bf16[2,192,384]{2,1,0:T(8,128)(2,1)}, bf16[2,192,384]{2,1,0:T(8,128)(2,1)S(1)}, u32[]{:S(2)}, u32[]{:S(2)}) collective-permute-start(bf16[2,192,384]{2,1,0:T(8,128)(2,1)} %get-tuple-element.54.refs_0_), channel_id=1, source_target_pairs={{0,8},{4,12},{8,0},{12,4},{1,9},{5,13},{9,1},{13,5},{2,10},{6,14},... | collective-permute-start | bytes 884744 | tf_op jit(solution)/shard_map/ppermute | solution.py:460
  7.9 0.5 collective-permute-start.2
  8.4 1.6 %collective-permute-start.3 = (bf16[1,192,768]{2,1,0:T(8,128)(2,1)S(1)}, bf16[1,192,768]{2,1,0:T(8,128)(2,1)S(1)}, u32[]{:S(2)}, u32[]{:S(2)}) collective-permute-start(bf16[1,192,768]{2,1,0:T(8,128)(2,1)S(1)} %copy-done.1), channel_id=1, source_target_pairs={{0,1},{1,5},{2,3},{3,7},{4,0},{5,4},{6,2},{7,6},{8,9},{9,13},{10,1... | collective-permute-start | bytes 884744 | tf_op jit(solution)/shard_map/ppermute | solution.py:482
  9.9 2.6 %collective-permute-start.4 = (bf16[1,192,768]{2,1,0:T(8,128)(2,1)S(1)}, bf16[1,192,768]{2,1,0:T(8,128)(2,1)S(1)}, u32[]{:S(2)}, u32[]{:S(2)}) collective-permute-start(bf16[1,192,768]{2,1,0:T(8,128)(2,1)S(1)} %copy-done.1), channel_id=1, source_target_pairs={{0,2},{1,6},{2,0},{3,4},{4,3},{5,7},{6,1},{7,5},{8,10},{9,14},{10,... | collective-permute-start | bytes 884744 | tf_op jit(solution)/shard_map/ppermute | solution.py:482
  12.5 3.9 %collective-permute-done.1.refs_2_ = bf16[2,192,384]{2,1,0:T(8,128)(2,1)S(1)} collective-permute-done((bf16[2,192,384]{2,1,0:T(8,128)(2,1)}, bf16[2,192,384]{2,1,0:T(8,128)(2,1)S(1)}, u32[]{:S(2)}, u32[]{:S(2)}) %collective-permute-start.1) | collective-permute-done | bytes 294944 | tf_op jit(solution)/shard_map/ppermute | solution.py:460
  16.5 4.9 %collective-permute-done.2.refs_0_ = bf16[192,768]{1,0:T(8,128)(2,1)S(1)} collective-permute-done((bf16[192,768]{1,0:T(8,128)(2,1)}, bf16[192,768]{1,0:T(8,128)(2,1)S(1)}, u32[]{:S(2)}, u32[]{:S(2)}) %collective-permute-start.2) | collective-permute-done | bytes 294944 | tf_op jit(solution)/shard_map/ppermute | solution.py:460
  21.3 1.7 %collective-permute-done.3.refs_5_ = bf16[1,192,768]{2,1,0:T(8,128)(2,1)S(1)} collective-permute-done((bf16[1,192,768]{2,1,0:T(8,128)(2,1)S(1)}, bf16[1,192,768]{2,1,0:T(8,128)(2,1)S(1)}, u32[]{:S(2)}, u32[]{:S(2)}) %collective-permute-start.3) | collective-permute-done | bytes 294944 | tf_op jit(solution)/shard_map/ppermute | solution.py:482
  23.0 1.8 %collective-permute-done.4.refs_6_ = bf16[1,192,768]{2,1,0:T(8,128)(2,1)S(1)} collective-permute-done((bf16[1,192,768]{2,1,0:T(8,128)(2,1)S(1)}, bf16[1,192,768]{2,1,0:T(8,128)(2,1)S(1)}, u32[]{:S(2)}, u32[]{:S(2)}) %collective-permute-start.4) | collective-permute-done | bytes 294944 | tf_op jit(solution)/shard_map/ppermute | solution.py:482
  24.8 0.0 collective-permute-done.refs_1_
  24.8 1.6 %collective-permute-start.9 = (bf16[2,192,384]{2,1,0:T(8,128)(2,1)S(1)}, bf16[2,192,384]{2,1,0:T(8,128)(2,1)S(1)}, u32[]{:S(2)}, u32[]{:S(2)}) collective-permute-start(bf16[2,192,384]{2,1,0:T(8,128)(2,1)S(1)} %slice.3), channel_id=1, source_target_pairs={{0,8},{4,12},{8,0},{12,4},{1,9},{5,13},{9,1},{13,5},{2,10},{6,14},... | collective-permute-start | bytes 884744 | tf_op jit(solution)/shard_map/ppermute | solution.py:460
  26.4 0.7 collective-permute-start.6
  27.1 5.3 %collective-permute-start.7 = (bf16[1,192,768]{2,1,0:T(8,128)(2,1)S(1)}, bf16[1,192,768]{2,1,0:T(8,128)(2,1)S(1)}, u32[]{:S(2)}, u32[]{:S(2)}) collective-permute-start(bf16[1,192,768]{2,1,0:T(8,128)(2,1)S(1)} %copy-done.1), channel_id=1, source_target_pairs={{0,3},{1,7},{2,1},{3,5},{4,2},{5,6},{6,0},{7,4},{8,11},{9,15},{10,... | collective-permute-start | bytes 884744 | tf_op jit(solution)/shard_map/ppermute | solution.py:482
  32.4 0.5 collective-permute-start.5
  33.5 0.0 copy-start.3
  33.5 1.0 copy-done.3
  34.5 0.9 copy-done.5
  35.4 2.0 %shard_map.119 = (bf16[2,192,384]{2,1,0:T(8,128)(2,1)S(1)}, f32[3,384]{1,0:T(4,128)S(1)}) custom-call(s32[1]{0:T(128)S(6)} %copy.13.len_ref, bf16[2,192,384]{2,1,0:T(8,128)(2,1)S(1)} %copy-done.3, bf16[3,192,384]{2,1,0:T(8,128)(2,1)S(1)} %collective-permute-done.refs_1_, bf16[2,192,384]{2,1,0:T(8,128)(2,1)S(1)} %collective-permute-done.1.refs_2_, ...), custom_call_target="tpu_custom_call" | custom-call | flops 452984832 | bytes 1774084 | tf_op jit(solution)/shard_map/pallas_call | solution.py:230
  37.4 6.4 %collective-permute-done.7.refs_7_ = bf16[1,192,768]{2,1,0:T(8,128)(2,1)S(1)} collective-permute-done((bf16[1,192,768]{2,1,0:T(8,128)(2,1)S(1)}, bf16[1,192,768]{2,1,0:T(8,128)(2,1)S(1)}, u32[]{:S(2)}, u32[]{:S(2)}) %collective-permute-start.7) | collective-permute-done | bytes 294944 | tf_op jit(solution)/shard_map/ppermute | solution.py:482
  43.8 0.0 collective-permute-start.10
  43.8 0.1 collective-permute-start.11
  43.9 1.5 %collective-permute-done.10.refs_3_ = bf16[192,768]{1,0:T(8,128)(2,1)S(1)} collective-permute-done((bf16[192,768]{1,0:T(8,128)(2,1)S(1)}, bf16[192,768]{1,0:T(8,128)(2,1)S(1)}, u32[]{:S(2)}, u32[]{:S(2)}) %collective-permute-start.10) | collective-permute-done | bytes 294944 | tf_op jit(solution)/shard_map/ppermute | solution.py:463
  45.4 1.4 %shard_map.120 = (f32[2,192,384]{2,1,0:T(8,128)S(1)}, bf16[2,192,384]{2,1,0:T(8,128)(2,1)S(1)}, bf16[4,192,768]{2,1,0:T(8,128)(2,1)S(1)}, bf16[768,768]{1,0:T(8,128)(2,1)S(1)}) custom-call(f32[1,3072]{1,0:T(1,128)S(1)} %copy-done.2, bf16[768,768]{1,0:T(8,128)(2,1)S(1)} %copy-done, bf16[192,768]{1,0:T(8,128)(2,1)S(1)} %collective-permute-done.2.refs_0_, ...), custom_call_target="tpu_custom_call" | custom-call | flops 905969664 | bytes 6795264 | tf_op jit(solution)/shard_map/pallas_call | solution.py:230
  46.8 6.5 %collective-permute-done.11.other_ref = bf16[2,192,384]{2,1,0:T(8,128)(2,1)S(1)} collective-permute-done((bf16[2,192,384]{2,1,0:T(8,128)(2,1)S(1)}, bf16[2,192,384]{2,1,0:T(8,128)(2,1)S(1)}, u32[]{:S(2)}, u32[]{:S(2)}) %collective-permute-start.11) | collective-permute-done | bytes 294944 | tf_op jit(solution)/shard_map/ppermute | solution.py:460
  53.2 1.2 %shard_map.121 = (f32[192,768]{1,0:T(8,128)S(1)}, bf16[192,768]{1,0:T(8,128)(2,1)S(1)}, bf16[192,768]{1,0:T(8,128)(2,1)S(1)}, bf16[192,768]{1,0:T(8,128)(2,1)S(1)}, bf16[384,768]{1,0:T(8,128)(2,1)S(1)}) custom-call(bf16[768,768]{1,0:T(8,128)(2,1)S(1)} %copy-done, bf16[768,768]{1,0:T(8,128)(2,1)S(1)} %get-tuple-element.70.w2_ref, ...), custom_call_target="tpu_custom_call" | custom-call | flops 905969664 | bytes 5013504 | tf_op jit(solution)/shard_map/pallas_call | solution.py:230
  54.5 2.0 %shard_map.123 = (f32[2,384,768]{2,1,0:T(8,128)S(1)}, bf16[2,384,768]{2,1,0:T(8,128)(2,1)S(1)}) custom-call(f32[1,3072]{1,0:T(1,128)S(1)} %copy-done.2, bf16[384,768]{1,0:T(8,128)(2,1)S(1)} %get-tuple-element.76.all_ref, bf16[4,192,768]{2,1,0:T(8,128)(2,1)S(1)} %get-tuple-element.77.cot_ref), custom_call_target="tpu_custom_call" | custom-call | flops 905969664 | bytes 5320704 | tf_op jit(solution)/shard_map/pallas_call | solution.py:230
  56.5 0.1 collective-permute-start.16
  56.6 2.8 %collective-permute-done.16.other_ref = bf16[2,384,768]{2,1,0:T(8,128)(2,1)S(1)} collective-permute-done((bf16[2,384,768]{2,1,0:T(8,128)(2,1)S(1)}, bf16[2,384,768]{2,1,0:T(8,128)(2,1)S(1)}, u32[]{:S(2)}, u32[]{:S(2)}) %collective-permute-start.16) | collective-permute-done | bytes 1179680 | tf_op jit(solution)/shard_map/ppermute | solution.py:463
  59.4 0.3 shard_map.124
  59.7 0.6 collective-permute-start.17
  60.3 0.3 collective-permute-start.19
  60.6 0.6 collective-permute-start.12
  61.2 2.3 %collective-permute-start.13 = (bf16[192,768]{1,0:T(8,128)(2,1)S(1)}, bf16[192,768]{1,0:T(8,128)(2,1)S(1)}, u32[]{:S(2)}, u32[]{:S(2)}) collective-permute-start(bf16[192,768]{1,0:T(8,128)(2,1)S(1)} %get-tuple-element.74), channel_id=1, source_target_pairs={{0,2},{1,3},{2,0},{3,1},{4,6},{5,7},{6,4},{7,5},{8,10},{9,11},{10,... | collective-permute-start | bytes 884744 | tf_op jit(solution)/shard_map/ppermute | solution.py:460
  63.5 1.5 %collective-permute-start.14 = (bf16[192,768]{1,0:T(8,128)(2,1)S(1)}, bf16[192,768]{1,0:T(8,128)(2,1)S(1)}, u32[]{:S(2)}, u32[]{:S(2)}) collective-permute-start(bf16[192,768]{1,0:T(8,128)(2,1)S(1)} %get-tuple-element.75), channel_id=1, source_target_pairs={{0,3},{1,2},{2,1},{3,0},{4,7},{5,6},{6,5},{7,4},{8,11},{9,10},{10,... | collective-permute-start | bytes 884744 | tf_op jit(solution)/shard_map/ppermute | solution.py:460
  65.0 10.2 %collective-permute-done.17.other_ref = bf16[384,768]{1,0:T(8,128)(2,1)S(1)} collective-permute-done((bf16[384,768]{1,0:T(8,128)(2,1)S(1)}, bf16[384,768]{1,0:T(8,128)(2,1)S(1)}, u32[]{:S(2)}, u32[]{:S(2)}) %collective-permute-start.17) | collective-permute-done | bytes 589856 | tf_op jit(solution)/shard_map/ppermute | solution.py:460
  75.2 0.1 shard_map.125.own_ref
  75.3 0.1 collective-permute-start.18
  75.3 0.0 collective-permute-done.19.other_ref
  75.3 0.8 copy-done.4
  76.1 0.0 copy-done.6
  76.1 2.8 %shard_map.128 = (bf16[192,384]{1,0:T(8,128)(2,1)S(1)}, bf16[192,384]{1,0:T(8,128)(2,1)S(1)}, f32[2,192,384]{2,1,0:T(8,128)S(1)}, f32[2,192,384]{2,1,0:T(8,128)S...) custom-call(s32[1]{0:T(128)S(6)} %copy.13.len_ref, f32[3,384]{1,0:T(4,128)S(1)} %get-tuple-element.84.lse_ref, ...), custom_call_target="tpu_custom_call" | custom-call | flops 1132462080 | bytes 4723204 | tf_op jit(solution)/shard_map/pallas_call | solution.py:230
  78.9 0.6 collective-permute-start.20
  79.5 0.0 collective-permute-done.12.refs_0_
  79.5 0.3 collective-permute-start.21
  79.8 4.9 %collective-permute-done.13.refs_1_ = bf16[192,768]{1,0:T(8,128)(2,1)S(1)} collective-permute-done((bf16[192,768]{1,0:T(8,128)(2,1)S(1)}, bf16[192,768]{1,0:T(8,128)(2,1)S(1)}, u32[]{:S(2)}, u32[]{:S(2)}) %collective-permute-start.13) | collective-permute-done | bytes 294944 | tf_op jit(solution)/shard_map/ppermute | solution.py:460
  84.7 0.0 collective-permute-done.14.refs_2_
  84.7 0.2 shard_map.122
  84.8 0.7 collective-permute-start.15
  85.5 1.6 %collective-permute-start.22 = (bf16[2,192,384]{2,1,0:T(8,128)(2,1)S(1)}, bf16[2,192,384]{2,1,0:T(8,128)(2,1)S(1)}, u32[]{:S(2)}, u32[]{:S(2)}) collective-permute-start(bf16[2,192,384]{2,1,0:T(8,128)(2,1)S(1)} %get-tuple-element.92), channel_id=1, source_target_pairs={{0,8},{4,12},{8,0},{12,4},{1,9},{5,13},{9,1},{13,5},{2,10},{6,14},... | collective-permute-start | bytes 884744 | tf_op jit(solution)/shard_map/ppermute | solution.py:460
  87.1 0.0 collective-permute-done.21.dq_other_ref
  87.1 1.8 %collective-permute-done.20.other_ref = bf16[2,192,384]{2,1,0:T(8,128)(2,1)S(1)} collective-permute-done((bf16[2,192,384]{2,1,0:T(8,128)(2,1)S(1)}, bf16[2,192,384]{2,1,0:T(8,128)(2,1)S(1)}, u32[]{:S(2)}, u32[]{:S(2)}) %collective-permute-start.20) | collective-permute-done | bytes 294944 | tf_op jit(solution)/shard_map/ppermute | solution.py:460
  88.9 0.1 shard_map.129
  89.0 6.1 %collective-permute-start.23 = (bf16[2,192,384]{2,1,0:T(8,128)(2,1)S(1)}, bf16[2,192,384]{2,1,0:T(8,128)(2,1)S(1)}, u32[]{:S(2)}, u32[]{:S(2)}) collective-permute-start(bf16[2,192,384]{2,1,0:T(8,128)(2,1)S(1)} %shard_map.129), channel_id=1, source_target_pairs={{0,4},{4,0},{8,12},{12,8},{1,5},{5,1},{9,13},{13,9},{2,6},{6,2},{1... | collective-permute-start | bytes 884744 | tf_op jit(solution)/shard_map/ppermute | solution.py:460
  95.1 0.0 collective-permute-done.18.other_ref
  95.1 1.6 %shard_map.126 = f32[768,768]{1,0:T(8,128)} custom-call(bf16[384,768]{1,0:T(8,128)(2,1)S(1)} %shard_map.125.own_ref, bf16[384,768]{1,0:T(8,128)(2,1)S(1)} %collective-permute-done.18.other_ref), custom_call_target="tpu_custom_call" | custom-call | bytes 3538944 | tf_op jit(solution)/shard_map/pallas_call | solution.py:230
  96.7 0.8 shard_map.127
  97.5 4.6 %all-to-all-start = ((f32[4,1,768]{2,1,0:T(1,128)}), f32[4,1,768]{2,1,0:T(1,128)S(1)}, u32[]{:S(2)}, u32[]{:S(2)}) async-start(f32[4,1,768]{2,1,0:T(1,128)} %get-tuple-element.99), calls=%async_computation | async-start | bytes 24576 | tf_op jit(solution)/shard_map/all_to_all | solution.py:589
  102.1 0.8 collective-permute-done.23.other_ref
  102.9 1.0 shard_map.130
  103.9 2.9 %all-to-all-done = f32[4,1,768]{2,1,0:T(1,128)S(1)} async-done(((f32[4,1,768]{2,1,0:T(1,128)}), f32[4,1,768]{2,1,0:T(1,128)S(1)}, u32[]{:S(2)}, u32[]{:S(2)}) %all-to-all-start) | async-done | bytes 12320 | tf_op jit(solution)/shard_map/all_to_all | solution.py:589
  106.8 0.6 reduce_sum.12
  (16 shorter events, 0.1 us)
Async XLA Ops:
  0.6 7.7 %copy-start.1 = (bf16[1,192,768]{2,1,0:T(8,128)(2,1)S(1)}, bf16[1,192,768]{2,1,0:T(8,128)(2,1)}, u32[]{:S(2)}) copy-start(bf16[1,192,768]{2,1,0:T(8,128)(2,1)} %cot_ref.1) | copy-start | bytes 884740
  3.3 42.1 %copy-start = (bf16[768,768]{1,0:T(8,128)(2,1)S(1)}, bf16[768,768]{1,0:T(8,128)(2,1)}, u32[]{:S(2)}) copy-start(bf16[768,768]{1,0:T(8,128)(2,1)} %w_ref.5) | copy-start | bytes 3538948
  3.3 42.1 %copy-start.2 = (f32[1,3072]{1,0:T(1,128)S(1)}, f32[1,3072]{1,0:T(1,128)}, u32[]{:S(2)}) copy-start(f32[1,3072]{1,0:T(1,128)} %gate_ref.5) | copy-start | bytes 36868
  3.3 21.5 %collective-permute-start = (bf16[3,192,384]{2,1,0:T(8,128)(2,1)}, bf16[3,192,384]{2,1,0:T(8,128)(2,1)S(1)}, u32[]{:S(2)}, u32[]{:S(2)}) collective-permute-start(bf16[3,192,384]{2,1,0:T(8,128)(2,1)} %get-tuple-element.53), channel_id=1, source_target_pairs={{0,4},{4,0},{8,12},{12,8},{1,5},{5,1},{9,13},{13,9},{2,6},{6,2},{1... | collective-permute-start | bytes 1327112 | tf_op jit(solution)/shard_map/ppermute | solution.py:460
  6.3 10.1 %collective-permute-start.1 = (bf16[2,192,384]{2,1,0:T(8,128)(2,1)}, bf16[2,192,384]{2,1,0:T(8,128)(2,1)S(1)}, u32[]{:S(2)}, u32[]{:S(2)}) collective-permute-start(bf16[2,192,384]{2,1,0:T(8,128)(2,1)} %get-tuple-element.54.refs_0_), channel_id=1, source_target_pairs={{0,8},{4,12},{8,0},{12,4},{1,9},{5,13},{9,1},{13,5},{2,10},{6,14},... | collective-permute-start | bytes 884744 | tf_op jit(solution)/shard_map/ppermute | solution.py:460
  7.9 13.5 %collective-permute-start.2 = (bf16[192,768]{1,0:T(8,128)(2,1)}, bf16[192,768]{1,0:T(8,128)(2,1)S(1)}, u32[]{:S(2)}, u32[]{:S(2)}) collective-permute-start(bf16[192,768]{1,0:T(8,128)(2,1)} %get-tuple-element.55), channel_id=1, source_target_pairs={{0,8},{4,12},{8,0},{12,4},{1,9},{5,13},{9,1},{13,5},{2,10},{6,14},... | collective-permute-start | bytes 884744 | tf_op jit(solution)/shard_map/ppermute | solution.py:460
  8.4 14.7 %collective-permute-start.3 = (bf16[1,192,768]{2,1,0:T(8,128)(2,1)S(1)}, bf16[1,192,768]{2,1,0:T(8,128)(2,1)S(1)}, u32[]{:S(2)}, u32[]{:S(2)}) collective-permute-start(bf16[1,192,768]{2,1,0:T(8,128)(2,1)S(1)} %copy-done.1), channel_id=1, source_target_pairs={{0,1},{1,5},{2,3},{3,7},{4,0},{5,4},{6,2},{7,6},{8,9},{9,13},{10,1... | collective-permute-start | bytes 884744 | tf_op jit(solution)/shard_map/ppermute | solution.py:482
  9.9 14.8 %collective-permute-start.4 = (bf16[1,192,768]{2,1,0:T(8,128)(2,1)S(1)}, bf16[1,192,768]{2,1,0:T(8,128)(2,1)S(1)}, u32[]{:S(2)}, u32[]{:S(2)}) collective-permute-start(bf16[1,192,768]{2,1,0:T(8,128)(2,1)S(1)} %copy-done.1), channel_id=1, source_target_pairs={{0,2},{1,6},{2,0},{3,4},{4,3},{5,7},{6,1},{7,5},{8,10},{9,14},{10,... | collective-permute-start | bytes 884744 | tf_op jit(solution)/shard_map/ppermute | solution.py:482
  24.8 8.7 %collective-permute-start.9 = (bf16[2,192,384]{2,1,0:T(8,128)(2,1)S(1)}, bf16[2,192,384]{2,1,0:T(8,128)(2,1)S(1)}, u32[]{:S(2)}, u32[]{:S(2)}) collective-permute-start(bf16[2,192,384]{2,1,0:T(8,128)(2,1)S(1)} %slice.3), channel_id=1, source_target_pairs={{0,8},{4,12},{8,0},{12,4},{1,9},{5,13},{9,1},{13,5},{2,10},{6,14},... | collective-permute-start | bytes 884744 | tf_op jit(solution)/shard_map/ppermute | solution.py:460
  26.4 11.0 %collective-permute-start.6 = (bf16[1,192,768]{2,1,0:T(8,128)(2,1)S(1)}, bf16[1,192,768]{2,1,0:T(8,128)(2,1)S(1)}, u32[]{:S(2)}, u32[]{:S(2)}) collective-permute-start(bf16[1,192,768]{2,1,0:T(8,128)(2,1)S(1)} %copy-done.1), channel_id=1, source_target_pairs={{0,0},{1,4},{2,2},{3,6},{4,1},{5,5},{6,3},{7,7},{8,8},{9,12},{10,1... | collective-permute-start | bytes 884744 | tf_op jit(solution)/shard_map/ppermute | solution.py:482
  27.1 16.7 %collective-permute-start.7 = (bf16[1,192,768]{2,1,0:T(8,128)(2,1)S(1)}, bf16[1,192,768]{2,1,0:T(8,128)(2,1)S(1)}, u32[]{:S(2)}, u32[]{:S(2)}) collective-permute-start(bf16[1,192,768]{2,1,0:T(8,128)(2,1)S(1)} %copy-done.1), channel_id=1, source_target_pairs={{0,3},{1,7},{2,1},{3,5},{4,2},{5,6},{6,0},{7,4},{8,11},{9,15},{10,... | collective-permute-start | bytes 884744 | tf_op jit(solution)/shard_map/ppermute | solution.py:482
  32.3 11.5 %collective-permute-start.8 = (bf16[192,768]{1,0:T(8,128)(2,1)S(1)}, bf16[192,768]{1,0:T(8,128)(2,1)S(1)}, u32[]{:S(2)}, u32[]{:S(2)}) collective-permute-start(bf16[192,768]{1,0:T(8,128)(2,1)S(1)} %collective-permute-done.2.refs_0_), channel_id=1, source_target_pairs={{0,16},{16,0},{1,17},{17,1},{2,18},{18,2},{3,19},{19,3},{4,20},{20... | collective-permute-start | bytes 884744 | tf_op jit(solution)/shard_map/ppermute | solution.py:463
  32.4 11.5 %collective-permute-start.5 = (bf16[192,768]{1,0:T(8,128)(2,1)}, bf16[192,768]{1,0:T(8,128)(2,1)S(1)}, u32[]{:S(2)}, u32[]{:S(2)}) collective-permute-start(bf16[192,768]{1,0:T(8,128)(2,1)} %get-tuple-element.58), channel_id=1, source_target_pairs={{0,8},{4,12},{8,0},{12,4},{1,9},{5,13},{9,1},{13,5},{2,10},{6,14},... | collective-permute-start | bytes 884744 | tf_op jit(solution)/shard_map/ppermute | solution.py:460
  33.5 1.0 copy-start.3
  34.5 0.9 copy-start.5
  43.8 1.6 %collective-permute-start.10 = (bf16[192,768]{1,0:T(8,128)(2,1)S(1)}, bf16[192,768]{1,0:T(8,128)(2,1)S(1)}, u32[]{:S(2)}, u32[]{:S(2)}) collective-permute-start(bf16[192,768]{1,0:T(8,128)(2,1)S(1)} %collective-permute-done.5.refs_1_), channel_id=1, source_target_pairs={{0,16},{16,0},{1,17},{17,1},{2,18},{18,2},{3,19},{19,3},{4,20},{20... | collective-permute-start | bytes 884744 | tf_op jit(solution)/shard_map/ppermute | solution.py:463
  43.8 9.4 %collective-permute-start.11 = (bf16[2,192,384]{2,1,0:T(8,128)(2,1)S(1)}, bf16[2,192,384]{2,1,0:T(8,128)(2,1)S(1)}, u32[]{:S(2)}, u32[]{:S(2)}) collective-permute-start(bf16[2,192,384]{2,1,0:T(8,128)(2,1)S(1)} %get-tuple-element.71.o_ref), channel_id=1, source_target_pairs={{0,4},{4,0},{8,12},{12,8},{1,5},{5,1},{9,13},{13,9},{2,6},{6,2},{1... | collective-permute-start | bytes 884744 | tf_op jit(solution)/shard_map/ppermute | solution.py:460
  56.5 2.9 %collective-permute-start.16 = (bf16[2,384,768]{2,1,0:T(8,128)(2,1)S(1)}, bf16[2,384,768]{2,1,0:T(8,128)(2,1)S(1)}, u32[]{:S(2)}, u32[]{:S(2)}) collective-permute-start(bf16[2,384,768]{2,1,0:T(8,128)(2,1)S(1)} %get-tuple-element.79), channel_id=1, source_target_pairs={{0,16},{16,0},{1,17},{17,1},{2,18},{18,2},{3,19},{19,3},{4,20},{20... | collective-permute-start | bytes 3538952 | tf_op jit(solution)/shard_map/ppermute | solution.py:463
  59.7 15.4 %collective-permute-start.17 = (bf16[384,768]{1,0:T(8,128)(2,1)S(1)}, bf16[384,768]{1,0:T(8,128)(2,1)S(1)}, u32[]{:S(2)}, u32[]{:S(2)}) collective-permute-start(bf16[384,768]{1,0:T(8,128)(2,1)S(1)} %get-tuple-element.81), channel_id=1, source_target_pairs={{0,8},{4,12},{8,0},{12,4},{1,9},{5,13},{9,1},{13,5},{2,10},{6,14},... | collective-permute-start | bytes 1769480 | tf_op jit(solution)/shard_map/ppermute | solution.py:460
  60.3 15.0 %collective-permute-start.19 = (bf16[2,192,384]{2,1,0:T(8,128)(2,1)S(1)}, bf16[2,192,384]{2,1,0:T(8,128)(2,1)S(1)}, u32[]{:S(2)}, u32[]{:S(2)}) collective-permute-start(bf16[2,192,384]{2,1,0:T(8,128)(2,1)S(1)} %get-tuple-element.86), channel_id=1, source_target_pairs={{0,4},{4,0},{8,12},{12,8},{1,5},{5,1},{9,13},{13,9},{2,6},{6,2},{1... | collective-permute-start | bytes 884744 | tf_op jit(solution)/shard_map/ppermute | solution.py:460
  60.6 18.9 %collective-permute-start.12 = (bf16[192,768]{1,0:T(8,128)(2,1)S(1)}, bf16[192,768]{1,0:T(8,128)(2,1)S(1)}, u32[]{:S(2)}, u32[]{:S(2)}) collective-permute-start(bf16[192,768]{1,0:T(8,128)(2,1)S(1)} %get-tuple-element.73), channel_id=1, source_target_pairs={{0,1},{1,0},{2,3},{3,2},{4,5},{5,4},{6,7},{7,6},{8,9},{9,8},{10,11... | collective-permute-start | bytes 884744 | tf_op jit(solution)/shard_map/ppermute | solution.py:460
  61.2 23.5 %collective-permute-start.13 = (bf16[192,768]{1,0:T(8,128)(2,1)S(1)}, bf16[192,768]{1,0:T(8,128)(2,1)S(1)}, u32[]{:S(2)}, u32[]{:S(2)}) collective-permute-start(bf16[192,768]{1,0:T(8,128)(2,1)S(1)} %get-tuple-element.74), channel_id=1, source_target_pairs={{0,2},{1,3},{2,0},{3,1},{4,6},{5,7},{6,4},{7,5},{8,10},{9,11},{10,... | collective-permute-start | bytes 884744 | tf_op jit(solution)/shard_map/ppermute | solution.py:460
  63.5 21.2 %collective-permute-start.14 = (bf16[192,768]{1,0:T(8,128)(2,1)S(1)}, bf16[192,768]{1,0:T(8,128)(2,1)S(1)}, u32[]{:S(2)}, u32[]{:S(2)}) collective-permute-start(bf16[192,768]{1,0:T(8,128)(2,1)S(1)} %get-tuple-element.75), channel_id=1, source_target_pairs={{0,3},{1,2},{2,1},{3,0},{4,7},{5,6},{6,5},{7,4},{8,11},{9,10},{10,... | collective-permute-start | bytes 884744 | tf_op jit(solution)/shard_map/ppermute | solution.py:460
  75.1 1.0 copy-start.4
  75.1 1.0 copy-start.6
  75.3 19.9 %collective-permute-start.18 = (bf16[384,768]{1,0:T(8,128)(2,1)S(1)}, bf16[384,768]{1,0:T(8,128)(2,1)S(1)}, u32[]{:S(2)}, u32[]{:S(2)}) collective-permute-start(bf16[384,768]{1,0:T(8,128)(2,1)S(1)} %shard_map.125.own_ref), channel_id=1, source_target_pairs={{0,16},{16,0},{1,17},{17,1},{2,18},{18,2},{3,19},{19,3},{4,20},{20... | collective-permute-start | bytes 1769480 | tf_op jit(solution)/shard_map/ppermute | solution.py:463
  78.9 10.0 %collective-permute-start.20 = (bf16[2,192,384]{2,1,0:T(8,128)(2,1)S(1)}, bf16[2,192,384]{2,1,0:T(8,128)(2,1)S(1)}, u32[]{:S(2)}, u32[]{:S(2)}) collective-permute-start(bf16[2,192,384]{2,1,0:T(8,128)(2,1)S(1)} %get-tuple-element.88), channel_id=1, source_target_pairs={{0,8},{4,12},{8,0},{12,4},{1,9},{5,13},{9,1},{13,5},{2,10},{6,14},... | collective-permute-start | bytes 884744 | tf_op jit(solution)/shard_map/ppermute | solution.py:460
  79.5 7.6 %collective-permute-start.21 = (bf16[192,384]{1,0:T(8,128)(2,1)S(1)}, bf16[192,384]{1,0:T(8,128)(2,1)S(1)}, u32[]{:S(2)}, u32[]{:S(2)}) collective-permute-start(bf16[192,384]{1,0:T(8,128)(2,1)S(1)} %get-tuple-element.89), channel_id=1, source_target_pairs={{0,4},{4,0},{8,12},{12,8},{1,5},{5,1},{9,13},{13,9},{2,6},{6,2},{1... | collective-permute-start | bytes 442376 | tf_op jit(solution)/shard_map/ppermute | solution.py:460
  84.8 11.9 %collective-permute-start.15 = (bf16[192,768]{1,0:T(8,128)(2,1)S(1)}, bf16[192,768]{1,0:T(8,128)(2,1)S(1)}, u32[]{:S(2)}, u32[]{:S(2)}) collective-permute-start(bf16[192,768]{1,0:T(8,128)(2,1)S(1)} %shard_map.122), channel_id=1, source_target_pairs={{0,0},{1,4},{2,2},{3,6},{4,1},{5,5},{6,3},{7,7},{8,8},{9,12},{10,1... | collective-permute-start | bytes 884744 | tf_op jit(solution)/shard_map/ppermute | solution.py:582
  85.5 16.6 %collective-permute-start.22 = (bf16[2,192,384]{2,1,0:T(8,128)(2,1)S(1)}, bf16[2,192,384]{2,1,0:T(8,128)(2,1)S(1)}, u32[]{:S(2)}, u32[]{:S(2)}) collective-permute-start(bf16[2,192,384]{2,1,0:T(8,128)(2,1)S(1)} %get-tuple-element.92), channel_id=1, source_target_pairs={{0,8},{4,12},{8,0},{12,4},{1,9},{5,13},{9,1},{13,5},{2,10},{6,14},... | collective-permute-start | bytes 884744 | tf_op jit(solution)/shard_map/ppermute | solution.py:460
  89.0 13.9 %collective-permute-start.23 = (bf16[2,192,384]{2,1,0:T(8,128)(2,1)S(1)}, bf16[2,192,384]{2,1,0:T(8,128)(2,1)S(1)}, u32[]{:S(2)}, u32[]{:S(2)}) collective-permute-start(bf16[2,192,384]{2,1,0:T(8,128)(2,1)S(1)} %shard_map.129), channel_id=1, source_target_pairs={{0,4},{4,0},{8,12},{12,8},{1,5},{5,1},{9,13},{13,9},{2,6},{6,2},{1... | collective-permute-start | bytes 884744 | tf_op jit(solution)/shard_map/ppermute | solution.py:460
  97.5 9.3 %all-to-all-start = ((f32[4,1,768]{2,1,0:T(1,128)}), f32[4,1,768]{2,1,0:T(1,128)S(1)}, u32[]{:S(2)}, u32[]{:S(2)}) async-start(f32[4,1,768]{2,1,0:T(1,128)} %get-tuple-element.99), calls=%async_computation | async-start | bytes 24576 | tf_op jit(solution)/shard_map/all_to_all | solution.py:589

commit v5 on v4

--- a/solution.py
+++ b/solution.py
@@ -511,16 +511,10 @@
         flops=6 * unit_flops,
         smem=(0,),
     )
-    near_b, cot_0, cot_3, far_a, attended = lax.optimization_barrier(
-        (
-            permute(near_b, "seq", 2),
-            turn(cot_late, 0),
-            turn(cot_late, 3),
-            swap(near_a),
-            attended,
-        )
-    )
-    cots = (cot_0, cot_1, cot_2, cot_3)
+    near_b, far_a, attended = lax.optimization_barrier(
+        (permute(near_b, "seq", 2), swap(near_a), attended)
+    )
+    cots = (turn(cot_late, 0), cot_1, cot_2, turn(cot_late, 3))
     heads = (attended, permute(attended, "seq", 1))
     grad_own, grad_send, cot_all, weight_y = call(
         functools.partial(grad_attended_kernel, n),

time: 108 us -> 107 us (level)
    ppermute x4, starting transfers between devices: 10.1 us -> 6.98 us  [turn(): lax.ppermute(value, both, [(a * n + b, (a & 2 | b & 1) * n + (b ^ k ^ (a...]
    ppermute x15, starting transfers between devices: 21 us -> 23.7 us  [permute(): return lax.ppermute(value, axes, xor_pairs(n, k))]
    ppermute x15, waiting for transfers between devices: 33 us -> 35.6 us  [permute(): return lax.ppermute(value, axes, xor_pairs(n, k))]
    ppermute x4, waiting for transfers between devices: 4.34 us -> 2.8 us  [swap(): return lax.ppermute(value, 'dp', xor_pairs(2, 1))]
    ppermute x4, waiting for transfers between devices: 9.84 us -> 8.64 us  [turn(): lax.ppermute(value, both, [(a * n + b, (a & 2 | b & 1) * n + (b ^ k ^ (a...]
  transfers between devices with their start and end apart: 25 -> 25, of which waited for: 13 -> 14; matrix products, arithmetic and copies ran while one was open for 0% -> 0% of each run, Pallas kernels for 9% -> 9%
where the time goes in v5:
time: 107 us; the launch traced here: 106 us
  waiting for transfers between devices  49 us (46%)
  starting transfers between devices  36.5 us (34%)
  Pallas kernels  16 us (15%)
  local copies, waits for them, and re-layouts  3.3 us (3%)
  between operations  1.45 us (1%)
    ppermute x15, waiting for transfers between devices, permute(): return lax.ppermute(value, axes, xor_pairs(n, k))  35.6 us
    ppermute x15, starting transfers between devices, permute(): return lax.ppermute(value, axes, xor_pairs(n, k))  23.7 us
    pallas_call x13, Pallas kernels, call(): pl.pallas_call(kernel, out_shape=out_shape, in_specs=[pl.BlockSpec(memory...  16 us
    ppermute x4, waiting for transfers between devices, turn(): lax.ppermute(value, both, [(a * n + b, (a & 2 | b & 1) * n + (b ^ k ^ (a...  8.64 us
    ppermute x4, starting transfers between devices, turn(): lax.ppermute(value, both, [(a * n + b, (a & 2 | b & 1) * n + (b ^ k ^ (a...  6.98 us
    all_to_all x1, starting transfers between devices, square_shards(): lax.all_to_all(grad_gate, 'seq', 0, 0, tiled=True)  4.94 us
    ppermute x4, waiting for transfers between devices, swap(): return lax.ppermute(value, 'dp', xor_pairs(2, 1))  2.8 us
    unnamed x14, local copies, waits for them, and re-layouts  2.69 us
  transfers between devices with their start and end apart: 25, of which 14 were waited for; matrix products, arithmetic and copies ran while one was open for 0% of the time, Pallas kernels for 9%

profile of v5, /device:TPU:0, one launch (start us, length us, event | category | flops | bytes accessed | tf_op | source)
XLA Modules:
  0.0 106.3 jit_solution(17267004221012331084)
XLA Ops:
  0.6 2.7 %shard_map.118 = (bf16[2,192,384]{2,1,0:T(8,128)(2,1)}, bf16[192,384]{1,0:T(8,128)(2,1)}, bf16[3,192,384]{2,1,0:T(8,128)(2,1)}, bf16[192,768]{1,0:T(8,128)(2,1)}, bf16[192,768]{1,0:T(8,128)(2,1)}) custom-call(bf16[1,192,768]{2,1,0:T(8,128)(2,1)} %q_ref.1, bf16[1,192,768]{2,1,0:T(8,128)(2,1)} %k_ref.1, bf16[1,192,768]{2,1,0:T(8,128)(2,1)} %v_ref.1, ...), custom_call_target="tpu_custom_call" | custom-call | bytes 3538944 | tf_op jit(solution)/shard_map/pallas_call | solution.py:230
  3.3 0.0 copy-start
  3.3 0.0 copy-start.2
  3.3 3.0 %collective-permute-start = (bf16[3,192,384]{2,1,0:T(8,128)(2,1)}, bf16[3,192,384]{2,1,0:T(8,128)(2,1)S(1)}, u32[]{:S(2)}, u32[]{:S(2)}) collective-permute-start(bf16[3,192,384]{2,1,0:T(8,128)(2,1)} %get-tuple-element.51), channel_id=1, source_target_pairs={{0,4},{4,0},{8,12},{12,8},{1,5},{5,1},{9,13},{13,9},{2,6},{6,2},{1... | collective-permute-start | bytes 1327112 | tf_op jit(solution)/shard_map/ppermute | solution.py:460
  6.3 1.5 %collective-permute-start.1 = (bf16[2,192,384]{2,1,0:T(8,128)(2,1)}, bf16[2,192,384]{2,1,0:T(8,128)(2,1)S(1)}, u32[]{:S(2)}, u32[]{:S(2)}) collective-permute-start(bf16[2,192,384]{2,1,0:T(8,128)(2,1)} %get-tuple-element.52.refs_0_), channel_id=1, source_target_pairs={{0,8},{4,12},{8,0},{12,4},{1,9},{5,13},{9,1},{13,5},{2,10},{6,14},... | collective-permute-start | bytes 884744 | tf_op jit(solution)/shard_map/ppermute | solution.py:460
  7.9 0.5 collective-permute-start.2
  8.4 1.6 %collective-permute-start.3 = (bf16[1,192,768]{2,1,0:T(8,128)(2,1)S(1)}, bf16[1,192,768]{2,1,0:T(8,128)(2,1)S(1)}, u32[]{:S(2)}, u32[]{:S(2)}) collective-permute-start(bf16[1,192,768]{2,1,0:T(8,128)(2,1)S(1)} %copy-done.1), channel_id=1, source_target_pairs={{0,1},{1,5},{2,3},{3,7},{4,0},{5,4},{6,2},{7,6},{8,9},{9,13},{10,1... | collective-permute-start | bytes 884744 | tf_op jit(solution)/shard_map/ppermute | solution.py:482
  9.9 2.6 %collective-permute-start.4 = (bf16[1,192,768]{2,1,0:T(8,128)(2,1)S(1)}, bf16[1,192,768]{2,1,0:T(8,128)(2,1)S(1)}, u32[]{:S(2)}, u32[]{:S(2)}) collective-permute-start(bf16[1,192,768]{2,1,0:T(8,128)(2,1)S(1)} %copy-done.1), channel_id=1, source_target_pairs={{0,2},{1,6},{2,0},{3,4},{4,3},{5,7},{6,1},{7,5},{8,10},{9,14},{10,... | collective-permute-start | bytes 884744 | tf_op jit(solution)/shard_map/ppermute | solution.py:482
  12.5 3.9 %collective-permute-done.1.refs_2_ = bf16[2,192,384]{2,1,0:T(8,128)(2,1)S(1)} collective-permute-done((bf16[2,192,384]{2,1,0:T(8,128)(2,1)}, bf16[2,192,384]{2,1,0:T(8,128)(2,1)S(1)}, u32[]{:S(2)}, u32[]{:S(2)}) %collective-permute-start.1) | collective-permute-done | bytes 294944 | tf_op jit(solution)/shard_map/ppermute | solution.py:460
  16.5 4.9 %collective-permute-done.2.refs_0_ = bf16[192,768]{1,0:T(8,128)(2,1)S(1)} collective-permute-done((bf16[192,768]{1,0:T(8,128)(2,1)}, bf16[192,768]{1,0:T(8,128)(2,1)S(1)}, u32[]{:S(2)}, u32[]{:S(2)}) %collective-permute-start.2) | collective-permute-done | bytes 294944 | tf_op jit(solution)/shard_map/ppermute | solution.py:460
  21.3 1.7 %collective-permute-done.3.refs_5_ = bf16[1,192,768]{2,1,0:T(8,128)(2,1)S(1)} collective-permute-done((bf16[1,192,768]{2,1,0:T(8,128)(2,1)S(1)}, bf16[1,192,768]{2,1,0:T(8,128)(2,1)S(1)}, u32[]{:S(2)}, u32[]{:S(2)}) %collective-permute-start.3) | collective-permute-done | bytes 294944 | tf_op jit(solution)/shard_map/ppermute | solution.py:482
  23.0 1.8 %collective-permute-done.4.refs_6_ = bf16[1,192,768]{2,1,0:T(8,128)(2,1)S(1)} collective-permute-done((bf16[1,192,768]{2,1,0:T(8,128)(2,1)S(1)}, bf16[1,192,768]{2,1,0:T(8,128)(2,1)S(1)}, u32[]{:S(2)}, u32[]{:S(2)}) %collective-permute-start.4) | collective-permute-done | bytes 294944 | tf_op jit(solution)/shard_map/ppermute | solution.py:482
  24.8 0.0 collective-permute-done.refs_1_
  24.8 1.6 %collective-permute-start.7 = (bf16[2,192,384]{2,1,0:T(8,128)(2,1)S(1)}, bf16[2,192,384]{2,1,0:T(8,128)(2,1)S(1)}, u32[]{:S(2)}, u32[]{:S(2)}) collective-permute-start(bf16[2,192,384]{2,1,0:T(8,128)(2,1)S(1)} %slice.3), channel_id=1, source_target_pairs={{0,8},{4,12},{8,0},{12,4},{1,9},{5,13},{9,1},{13,5},{2,10},{6,14},... | collective-permute-start | bytes 884744 | tf_op jit(solution)/shard_map/ppermute | solution.py:460
  26.4 0.0 collective-permute-start.6
  26.4 0.5 collective-permute-start.5
  27.6 2.1 %collective-permute-start.10 = (bf16[1,192,768]{2,1,0:T(8,128)(2,1)S(1)}, bf16[1,192,768]{2,1,0:T(8,128)(2,1)S(1)}, u32[]{:S(2)}, u32[]{:S(2)}) collective-permute-start(bf16[1,192,768]{2,1,0:T(8,128)(2,1)S(1)} %copy-done.1), channel_id=1, source_target_pairs={{0,3},{1,7},{2,1},{3,5},{4,2},{5,6},{6,0},{7,4},{8,11},{9,15},{10,... | collective-permute-start | bytes 884744 | tf_op jit(solution)/shard_map/ppermute | solution.py:482
  29.7 0.7 collective-permute-start.9
  30.4 4.4 %collective-permute-done.7.refs_3_ = bf16[2,192,384]{2,1,0:T(8,128)(2,1)S(1)} collective-permute-done((bf16[2,192,384]{2,1,0:T(8,128)(2,1)S(1)}, bf16[2,192,384]{2,1,0:T(8,128)(2,1)S(1)}, u32[]{:S(2)}, u32[]{:S(2)}) %collective-permute-start.7) | collective-permute-done | bytes 294944 | tf_op jit(solution)/shard_map/ppermute | solution.py:460
  34.8 1.0 copy-done.3
  35.8 0.9 copy-done.5
  36.7 2.0 %shard_map.119 = (bf16[2,192,384]{2,1,0:T(8,128)(2,1)S(1)}, f32[3,384]{1,0:T(4,128)S(1)}) custom-call(s32[1]{0:T(128)S(6)} %copy.13.len_ref, bf16[2,192,384]{2,1,0:T(8,128)(2,1)S(1)} %copy-done.3, bf16[3,192,384]{2,1,0:T(8,128)(2,1)S(1)} %collective-permute-done.refs_1_, bf16[2,192,384]{2,1,0:T(8,128)(2,1)S(1)} %collective-permute-done.1.refs_2_, ...), custom_call_target="tpu_custom_call" | custom-call | flops 452984832 | bytes 1774084 | tf_op jit(solution)/shard_map/pallas_call | solution.py:230
  38.7 0.0 collective-permute-done.6.refs_2_
  38.7 0.5 collective-permute-done.5.refs_1_
  39.3 0.0 collective-permute-start.8
  39.3 0.0 collective-permute-start.11
  39.3 5.2 %collective-permute-done.10.refs_7_ = bf16[1,192,768]{2,1,0:T(8,128)(2,1)S(1)} collective-permute-done((bf16[1,192,768]{2,1,0:T(8,128)(2,1)S(1)}, bf16[1,192,768]{2,1,0:T(8,128)(2,1)S(1)}, u32[]{:S(2)}, u32[]{:S(2)}) %collective-permute-start.10) | collective-permute-done | bytes 294944 | tf_op jit(solution)/shard_map/ppermute | solution.py:482
  44.5 0.0 collective-permute-done.9.refs_4_
  44.5 0.0 collective-permute-done.8.refs_3_
  44.5 1.4 %shard_map.120 = (f32[2,192,384]{2,1,0:T(8,128)S(1)}, bf16[2,192,384]{2,1,0:T(8,128)(2,1)S(1)}, bf16[4,192,768]{2,1,0:T(8,128)(2,1)S(1)}, bf16[768,768]{1,0:T(8,128)(2,1)S(1)}) custom-call(f32[1,3072]{1,0:T(1,128)S(1)} %copy-done.2, bf16[768,768]{1,0:T(8,128)(2,1)S(1)} %copy-done, bf16[192,768]{1,0:T(8,128)(2,1)S(1)} %collective-permute-done.2.refs_0_, ...), custom_call_target="tpu_custom_call" | custom-call | flops 905969664 | bytes 6795264 | tf_op jit(solution)/shard_map/pallas_call | solution.py:230
  45.9 4.8 %collective-permute-done.11.other_ref = bf16[2,192,384]{2,1,0:T(8,128)(2,1)S(1)} collective-permute-done((bf16[2,192,384]{2,1,0:T(8,128)(2,1)S(1)}, bf16[2,192,384]{2,1,0:T(8,128)(2,1)S(1)}, u32[]{:S(2)}, u32[]{:S(2)}) %collective-permute-start.11) | collective-permute-done | bytes 294944 | tf_op jit(solution)/shard_map/ppermute | solution.py:460
  50.7 1.2 %shard_map.121 = (f32[192,768]{1,0:T(8,128)S(1)}, bf16[192,768]{1,0:T(8,128)(2,1)S(1)}, bf16[192,768]{1,0:T(8,128)(2,1)S(1)}, bf16[192,768]{1,0:T(8,128)(2,1)S(1)}, bf16[384,768]{1,0:T(8,128)(2,1)S(1)}) custom-call(bf16[768,768]{1,0:T(8,128)(2,1)S(1)} %copy-done, bf16[768,768]{1,0:T(8,128)(2,1)S(1)} %get-tuple-element.66.w2_ref, ...), custom_call_target="tpu_custom_call" | custom-call | flops 905969664 | bytes 5013504 | tf_op jit(solution)/shard_map/pallas_call | solution.py:230
  51.9 2.0 %shard_map.123 = (f32[2,384,768]{2,1,0:T(8,128)S(1)}, bf16[2,384,768]{2,1,0:T(8,128)(2,1)S(1)}) custom-call(f32[1,3072]{1,0:T(1,128)S(1)} %copy-done.2, bf16[384,768]{1,0:T(8,128)(2,1)S(1)} %get-tuple-element.72.all_ref, bf16[4,192,768]{2,1,0:T(8,128)(2,1)S(1)} %get-tuple-element.73.cot_ref), custom_call_target="tpu_custom_call" | custom-call | flops 905969664 | bytes 5320704 | tf_op jit(solution)/shard_map/pallas_call | solution.py:230
  54.0 0.1 collective-permute-start.16
  54.1 2.8 %collective-permute-done.16.other_ref = bf16[2,384,768]{2,1,0:T(8,128)(2,1)S(1)} collective-permute-done((bf16[2,384,768]{2,1,0:T(8,128)(2,1)S(1)}, bf16[2,384,768]{2,1,0:T(8,128)(2,1)S(1)}, u32[]{:S(2)}, u32[]{:S(2)}) %collective-permute-start.16) | collective-permute-done | bytes 1179680 | tf_op jit(solution)/shard_map/ppermute | solution.py:463
  56.9 0.3 shard_map.124
  57.1 1.6 %collective-permute-start.17 = (bf16[384,768]{1,0:T(8,128)(2,1)S(1)}, bf16[384,768]{1,0:T(8,128)(2,1)S(1)}, u32[]{:S(2)}, u32[]{:S(2)}) collective-permute-start(bf16[384,768]{1,0:T(8,128)(2,1)S(1)} %get-tuple-element.77), channel_id=1, source_target_pairs={{0,8},{4,12},{8,0},{12,4},{1,9},{5,13},{9,1},{13,5},{2,10},{6,14},... | collective-permute-start | bytes 1769480 | tf_op jit(solution)/shard_map/ppermute | solution.py:460
  58.7 0.7 collective-permute-start.12
  59.5 3.9 %collective-permute-start.13 = (bf16[192,768]{1,0:T(8,128)(2,1)S(1)}, bf16[192,768]{1,0:T(8,128)(2,1)S(1)}, u32[]{:S(2)}, u32[]{:S(2)}) collective-permute-start(bf16[192,768]{1,0:T(8,128)(2,1)S(1)} %get-tuple-element.70), channel_id=1, source_target_pairs={{0,2},{1,3},{2,0},{3,1},{4,6},{5,7},{6,4},{7,5},{8,10},{9,11},{10,... | collective-permute-start | bytes 884744 | tf_op jit(solution)/shard_map/ppermute | solution.py:460
  63.4 0.0 collective-permute-start.14
  63.4 9.2 %collective-permute-done.17.other_ref = bf16[384,768]{1,0:T(8,128)(2,1)S(1)} collective-permute-done((bf16[384,768]{1,0:T(8,128)(2,1)S(1)}, bf16[384,768]{1,0:T(8,128)(2,1)S(1)}, u32[]{:S(2)}, u32[]{:S(2)}) %collective-permute-start.17) | collective-permute-done | bytes 589856 | tf_op jit(solution)/shard_map/ppermute | solution.py:460
  72.6 0.1 shard_map.125.own_ref
  72.7 0.1 collective-permute-start.18
  72.8 0.8 copy-done.4
  73.5 0.0 copy-done.6
  73.6 2.8 %shard_map.128 = (bf16[192,384]{1,0:T(8,128)(2,1)S(1)}, bf16[192,384]{1,0:T(8,128)(2,1)S(1)}, f32[2,192,384]{2,1,0:T(8,128)S(1)}, f32[2,192,384]{2,1,0:T(8,128)S...) custom-call(s32[1]{0:T(128)S(6)} %copy.13.len_ref, f32[3,384]{1,0:T(4,128)S(1)} %get-tuple-element.80.lse_ref, ...), custom_call_target="tpu_custom_call" | custom-call | flops 1132462080 | bytes 4723204 | tf_op jit(solution)/shard_map/pallas_call | solution.py:230
  76.4 1.6 %collective-permute-start.20 = (bf16[2,192,384]{2,1,0:T(8,128)(2,1)S(1)}, bf16[2,192,384]{2,1,0:T(8,128)(2,1)S(1)}, u32[]{:S(2)}, u32[]{:S(2)}) collective-permute-start(bf16[2,192,384]{2,1,0:T(8,128)(2,1)S(1)} %get-tuple-element.84), channel_id=1, source_target_pairs={{0,8},{4,12},{8,0},{12,4},{1,9},{5,13},{9,1},{13,5},{2,10},{6,14},... | collective-permute-start | bytes 884744 | tf_op jit(solution)/shard_map/ppermute | solution.py:460
  78.0 0.0 collective-permute-done.12.refs_0_
  78.0 5.9 %collective-permute-done.13.refs_1_ = bf16[192,768]{1,0:T(8,128)(2,1)S(1)} collective-permute-done((bf16[192,768]{1,0:T(8,128)(2,1)S(1)}, bf16[192,768]{1,0:T(8,128)(2,1)S(1)}, u32[]{:S(2)}, u32[]{:S(2)}) %collective-permute-start.13) | collective-permute-done | bytes 294944 | tf_op jit(solution)/shard_map/ppermute | solution.py:460
  83.9 0.2 shard_map.122
  84.1 0.7 collective-permute-start.15
  84.8 0.6 collective-permute-start.22
  85.3 0.0 collective-permute-done.21.dq_other_ref
  85.3 0.1 collective-permute-done.20.other_ref
  85.4 0.1 shard_map.129
  85.5 8.2 %collective-permute-start.23 = (bf16[2,192,384]{2,1,0:T(8,128)(2,1)S(1)}, bf16[2,192,384]{2,1,0:T(8,128)(2,1)S(1)}, u32[]{:S(2)}, u32[]{:S(2)}) collective-permute-start(bf16[2,192,384]{2,1,0:T(8,128)(2,1)S(1)} %shard_map.129), channel_id=1, source_target_pairs={{0,4},{4,0},{8,12},{12,8},{1,5},{5,1},{9,13},{13,9},{2,6},{6,2},{1... | collective-permute-start | bytes 884744 | tf_op jit(solution)/shard_map/ppermute | solution.py:460
  93.7 1.6 %shard_map.126 = f32[768,768]{1,0:T(8,128)} custom-call(bf16[384,768]{1,0:T(8,128)(2,1)S(1)} %shard_map.125.own_ref, bf16[384,768]{1,0:T(8,128)(2,1)S(1)} %collective-permute-done.18.other_ref), custom_call_target="tpu_custom_call" | custom-call | bytes 3538944 | tf_op jit(solution)/shard_map/pallas_call | solution.py:230
  95.2 0.8 shard_map.127
  96.0 4.9 %all-to-all-start = ((f32[4,1,768]{2,1,0:T(1,128)}), f32[4,1,768]{2,1,0:T(1,128)S(1)}, u32[]{:S(2)}, u32[]{:S(2)}) async-start(f32[4,1,768]{2,1,0:T(1,128)} %get-tuple-element.95), calls=%async_computation | async-start | bytes 24576 | tf_op jit(solution)/shard_map/all_to_all | solution.py:583
  101.0 0.0 collective-permute-done.22.part_ref
  101.0 1.8 %collective-permute-done.23.other_ref = bf16[2,192,384]{2,1,0:T(8,128)(2,1)S(1)} collective-permute-done((bf16[2,192,384]{2,1,0:T(8,128)(2,1)S(1)}, bf16[2,192,384]{2,1,0:T(8,128)(2,1)S(1)}, u32[]{:S(2)}, u32[]{:S(2)}) %collective-permute-start.23) | collective-permute-done | bytes 294944 | tf_op jit(solution)/shard_map/ppermute | solution.py:460
  102.7 1.0 shard_map.130
  103.7 1.9 %all-to-all-done = f32[4,1,768]{2,1,0:T(1,128)S(1)} async-done(((f32[4,1,768]{2,1,0:T(1,128)}), f32[4,1,768]{2,1,0:T(1,128)S(1)}, u32[]{:S(2)}, u32[]{:S(2)}) %all-to-all-start) | async-done | bytes 12320 | tf_op jit(solution)/shard_map/all_to_all | solution.py:583
  105.7 0.6 reduce_sum.12
  (16 shorter events, 0.1 us)
Async XLA Ops:
  0.6 7.7 %copy-start.1 = (bf16[1,192,768]{2,1,0:T(8,128)(2,1)S(1)}, bf16[1,192,768]{2,1,0:T(8,128)(2,1)}, u32[]{:S(2)}) copy-start(bf16[1,192,768]{2,1,0:T(8,128)(2,1)} %cot_ref.1) | copy-start | bytes 884740
  3.3 41.2 %copy-start = (bf16[768,768]{1,0:T(8,128)(2,1)S(1)}, bf16[768,768]{1,0:T(8,128)(2,1)}, u32[]{:S(2)}) copy-start(bf16[768,768]{1,0:T(8,128)(2,1)} %w_ref.5) | copy-start | bytes 3538948
  3.3 41.2 %copy-start.2 = (f32[1,3072]{1,0:T(1,128)S(1)}, f32[1,3072]{1,0:T(1,128)}, u32[]{:S(2)}) copy-start(f32[1,3072]{1,0:T(1,128)} %gate_ref.5) | copy-start | bytes 36868
  3.3 21.5 %collective-permute-start = (bf16[3,192,384]{2,1,0:T(8,128)(2,1)}, bf16[3,192,384]{2,1,0:T(8,128)(2,1)S(1)}, u32[]{:S(2)}, u32[]{:S(2)}) collective-permute-start(bf16[3,192,384]{2,1,0:T(8,128)(2,1)} %get-tuple-element.51), channel_id=1, source_target_pairs={{0,4},{4,0},{8,12},{12,8},{1,5},{5,1},{9,13},{13,9},{2,6},{6,2},{1... | collective-permute-start | bytes 1327112 | tf_op jit(solution)/shard_map/ppermute | solution.py:460
  6.3 10.1 %collective-permute-start.1 = (bf16[2,192,384]{2,1,0:T(8,128)(2,1)}, bf16[2,192,384]{2,1,0:T(8,128)(2,1)S(1)}, u32[]{:S(2)}, u32[]{:S(2)}) collective-permute-start(bf16[2,192,384]{2,1,0:T(8,128)(2,1)} %get-tuple-element.52.refs_0_), channel_id=1, source_target_pairs={{0,8},{4,12},{8,0},{12,4},{1,9},{5,13},{9,1},{13,5},{2,10},{6,14},... | collective-permute-start | bytes 884744 | tf_op jit(solution)/shard_map/ppermute | solution.py:460
  7.9 13.5 %collective-permute-start.2 = (bf16[192,768]{1,0:T(8,128)(2,1)}, bf16[192,768]{1,0:T(8,128)(2,1)S(1)}, u32[]{:S(2)}, u32[]{:S(2)}) collective-permute-start(bf16[192,768]{1,0:T(8,128)(2,1)} %get-tuple-element.53), channel_id=1, source_target_pairs={{0,8},{4,12},{8,0},{12,4},{1,9},{5,13},{9,1},{13,5},{2,10},{6,14},... | collective-permute-start | bytes 884744 | tf_op jit(solution)/shard_map/ppermute | solution.py:460
  8.4 14.7 %collective-permute-start.3 = (bf16[1,192,768]{2,1,0:T(8,128)(2,1)S(1)}, bf16[1,192,768]{2,1,0:T(8,128)(2,1)S(1)}, u32[]{:S(2)}, u32[]{:S(2)}) collective-permute-start(bf16[1,192,768]{2,1,0:T(8,128)(2,1)S(1)} %copy-done.1), channel_id=1, source_target_pairs={{0,1},{1,5},{2,3},{3,7},{4,0},{5,4},{6,2},{7,6},{8,9},{9,13},{10,1... | collective-permute-start | bytes 884744 | tf_op jit(solution)/shard_map/ppermute | solution.py:482
  9.9 14.8 %collective-permute-start.4 = (bf16[1,192,768]{2,1,0:T(8,128)(2,1)S(1)}, bf16[1,192,768]{2,1,0:T(8,128)(2,1)S(1)}, u32[]{:S(2)}, u32[]{:S(2)}) collective-permute-start(bf16[1,192,768]{2,1,0:T(8,128)(2,1)S(1)} %copy-done.1), channel_id=1, source_target_pairs={{0,2},{1,6},{2,0},{3,4},{4,3},{5,7},{6,1},{7,5},{8,10},{9,14},{10,... | collective-permute-start | bytes 884744 | tf_op jit(solution)/shard_map/ppermute | solution.py:482
  24.8 10.0 %collective-permute-start.7 = (bf16[2,192,384]{2,1,0:T(8,128)(2,1)S(1)}, bf16[2,192,384]{2,1,0:T(8,128)(2,1)S(1)}, u32[]{:S(2)}, u32[]{:S(2)}) collective-permute-start(bf16[2,192,384]{2,1,0:T(8,128)(2,1)S(1)} %slice.3), channel_id=1, source_target_pairs={{0,8},{4,12},{8,0},{12,4},{1,9},{5,13},{9,1},{13,5},{2,10},{6,14},... | collective-permute-start | bytes 884744 | tf_op jit(solution)/shard_map/ppermute | solution.py:460
  26.4 12.3 %collective-permute-start.6 = (bf16[192,768]{1,0:T(8,128)(2,1)S(1)}, bf16[192,768]{1,0:T(8,128)(2,1)S(1)}, u32[]{:S(2)}, u32[]{:S(2)}) collective-permute-start(bf16[192,768]{1,0:T(8,128)(2,1)S(1)} %collective-permute-done.2.refs_0_), channel_id=1, source_target_pairs={{0,16},{16,0},{1,17},{17,1},{2,18},{18,2},{3,19},{19,3},{4,20},{20... | collective-permute-start | bytes 884744 | tf_op jit(solution)/shard_map/ppermute | solution.py:463
  26.4 12.9 %collective-permute-start.5 = (bf16[192,768]{1,0:T(8,128)(2,1)}, bf16[192,768]{1,0:T(8,128)(2,1)S(1)}, u32[]{:S(2)}, u32[]{:S(2)}) collective-permute-start(bf16[192,768]{1,0:T(8,128)(2,1)} %get-tuple-element.56), channel_id=1, source_target_pairs={{0,8},{4,12},{8,0},{12,4},{1,9},{5,13},{9,1},{13,5},{2,10},{6,14},... | collective-permute-start | bytes 884744 | tf_op jit(solution)/shard_map/ppermute | solution.py:460
  27.6 16.9 %collective-permute-start.10 = (bf16[1,192,768]{2,1,0:T(8,128)(2,1)S(1)}, bf16[1,192,768]{2,1,0:T(8,128)(2,1)S(1)}, u32[]{:S(2)}, u32[]{:S(2)}) collective-permute-start(bf16[1,192,768]{2,1,0:T(8,128)(2,1)S(1)} %copy-done.1), channel_id=1, source_target_pairs={{0,3},{1,7},{2,1},{3,5},{4,2},{5,6},{6,0},{7,4},{8,11},{9,15},{10,... | collective-permute-start | bytes 884744 | tf_op jit(solution)/shard_map/ppermute | solution.py:482
  29.7 14.8 %collective-permute-start.9 = (bf16[1,192,768]{2,1,0:T(8,128)(2,1)S(1)}, bf16[1,192,768]{2,1,0:T(8,128)(2,1)S(1)}, u32[]{:S(2)}, u32[]{:S(2)}) collective-permute-start(bf16[1,192,768]{2,1,0:T(8,128)(2,1)S(1)} %copy-done.1), channel_id=1, source_target_pairs={{0,0},{1,4},{2,2},{3,6},{4,1},{5,5},{6,3},{7,7},{8,8},{9,12},{10,1... | collective-permute-start | bytes 884744 | tf_op jit(solution)/shard_map/ppermute | solution.py:482
  34.8 1.0 copy-start.3
  35.8 0.9 copy-start.5
  39.3 5.2 %collective-permute-start.8 = (bf16[192,768]{1,0:T(8,128)(2,1)S(1)}, bf16[192,768]{1,0:T(8,128)(2,1)S(1)}, u32[]{:S(2)}, u32[]{:S(2)}) collective-permute-start(bf16[192,768]{1,0:T(8,128)(2,1)S(1)} %collective-permute-done.5.refs_1_), channel_id=1, source_target_pairs={{0,16},{16,0},{1,17},{17,1},{2,18},{18,2},{3,19},{19,3},{4,20},{20... | collective-permute-start | bytes 884744 | tf_op jit(solution)/shard_map/ppermute | solution.py:463
  39.3 11.4 %collective-permute-start.11 = (bf16[2,192,384]{2,1,0:T(8,128)(2,1)S(1)}, bf16[2,192,384]{2,1,0:T(8,128)(2,1)S(1)}, u32[]{:S(2)}, u32[]{:S(2)}) collective-permute-start(bf16[2,192,384]{2,1,0:T(8,128)(2,1)S(1)} %get-tuple-element.67.o_ref), channel_id=1, source_target_pairs={{0,4},{4,0},{8,12},{12,8},{1,5},{5,1},{9,13},{13,9},{2,6},{6,2},{1... | collective-permute-start | bytes 884744 | tf_op jit(solution)/shard_map/ppermute | solution.py:460
  54.0 2.9 %collective-permute-start.16 = (bf16[2,384,768]{2,1,0:T(8,128)(2,1)S(1)}, bf16[2,384,768]{2,1,0:T(8,128)(2,1)S(1)}, u32[]{:S(2)}, u32[]{:S(2)}) collective-permute-start(bf16[2,384,768]{2,1,0:T(8,128)(2,1)S(1)} %get-tuple-element.75), channel_id=1, source_target_pairs={{0,16},{16,0},{1,17},{17,1},{2,18},{18,2},{3,19},{19,3},{4,20},{20... | collective-permute-start | bytes 3538952 | tf_op jit(solution)/shard_map/ppermute | solution.py:463
  57.1 15.4 %collective-permute-start.17 = (bf16[384,768]{1,0:T(8,128)(2,1)S(1)}, bf16[384,768]{1,0:T(8,128)(2,1)S(1)}, u32[]{:S(2)}, u32[]{:S(2)}) collective-permute-start(bf16[384,768]{1,0:T(8,128)(2,1)S(1)} %get-tuple-element.77), channel_id=1, source_target_pairs={{0,8},{4,12},{8,0},{12,4},{1,9},{5,13},{9,1},{13,5},{2,10},{6,14},... | collective-permute-start | bytes 1769480 | tf_op jit(solution)/shard_map/ppermute | solution.py:460
  58.7 14.0 %collective-permute-start.19 = (bf16[2,192,384]{2,1,0:T(8,128)(2,1)S(1)}, bf16[2,192,384]{2,1,0:T(8,128)(2,1)S(1)}, u32[]{:S(2)}, u32[]{:S(2)}) collective-permute-start(bf16[2,192,384]{2,1,0:T(8,128)(2,1)S(1)} %get-tuple-element.82), channel_id=1, source_target_pairs={{0,4},{4,0},{8,12},{12,8},{1,5},{5,1},{9,13},{13,9},{2,6},{6,2},{1... | collective-permute-start | bytes 884744 | tf_op jit(solution)/shard_map/ppermute | solution.py:460
  58.7 19.2 %collective-permute-start.12 = (bf16[192,768]{1,0:T(8,128)(2,1)S(1)}, bf16[192,768]{1,0:T(8,128)(2,1)S(1)}, u32[]{:S(2)}, u32[]{:S(2)}) collective-permute-start(bf16[192,768]{1,0:T(8,128)(2,1)S(1)} %get-tuple-element.69), channel_id=1, source_target_pairs={{0,1},{1,0},{2,3},{3,2},{4,5},{5,4},{6,7},{7,6},{8,9},{9,8},{10,11... | collective-permute-start | bytes 884744 | tf_op jit(solution)/shard_map/ppermute | solution.py:460
  59.5 24.4 %collective-permute-start.13 = (bf16[192,768]{1,0:T(8,128)(2,1)S(1)}, bf16[192,768]{1,0:T(8,128)(2,1)S(1)}, u32[]{:S(2)}, u32[]{:S(2)}) collective-permute-start(bf16[192,768]{1,0:T(8,128)(2,1)S(1)} %get-tuple-element.70), channel_id=1, source_target_pairs={{0,2},{1,3},{2,0},{3,1},{4,6},{5,7},{6,4},{7,5},{8,10},{9,11},{10,... | collective-permute-start | bytes 884744 | tf_op jit(solution)/shard_map/ppermute | solution.py:460
  63.4 20.6 %collective-permute-start.14 = (bf16[192,768]{1,0:T(8,128)(2,1)S(1)}, bf16[192,768]{1,0:T(8,128)(2,1)S(1)}, u32[]{:S(2)}, u32[]{:S(2)}) collective-permute-start(bf16[192,768]{1,0:T(8,128)(2,1)S(1)} %get-tuple-element.71), channel_id=1, source_target_pairs={{0,3},{1,2},{2,1},{3,0},{4,7},{5,6},{6,5},{7,4},{8,11},{9,10},{10,... | collective-permute-start | bytes 884744 | tf_op jit(solution)/shard_map/ppermute | solution.py:460
  72.6 1.0 copy-start.4
  72.6 1.0 copy-start.6
  72.7 21.0 %collective-permute-start.18 = (bf16[384,768]{1,0:T(8,128)(2,1)S(1)}, bf16[384,768]{1,0:T(8,128)(2,1)S(1)}, u32[]{:S(2)}, u32[]{:S(2)}) collective-permute-start(bf16[384,768]{1,0:T(8,128)(2,1)S(1)} %shard_map.125.own_ref), channel_id=1, source_target_pairs={{0,16},{16,0},{1,17},{17,1},{2,18},{18,2},{3,19},{19,3},{4,20},{20... | collective-permute-start | bytes 1769480 | tf_op jit(solution)/shard_map/ppermute | solution.py:463
  76.4 9.0 %collective-permute-start.20 = (bf16[2,192,384]{2,1,0:T(8,128)(2,1)S(1)}, bf16[2,192,384]{2,1,0:T(8,128)(2,1)S(1)}, u32[]{:S(2)}, u32[]{:S(2)}) collective-permute-start(bf16[2,192,384]{2,1,0:T(8,128)(2,1)S(1)} %get-tuple-element.84), channel_id=1, source_target_pairs={{0,8},{4,12},{8,0},{12,4},{1,9},{5,13},{9,1},{13,5},{2,10},{6,14},... | collective-permute-start | bytes 884744 | tf_op jit(solution)/shard_map/ppermute | solution.py:460
  78.0 7.4 %collective-permute-start.21 = (bf16[192,384]{1,0:T(8,128)(2,1)S(1)}, bf16[192,384]{1,0:T(8,128)(2,1)S(1)}, u32[]{:S(2)}, u32[]{:S(2)}) collective-permute-start(bf16[192,384]{1,0:T(8,128)(2,1)S(1)} %get-tuple-element.85), channel_id=1, source_target_pairs={{0,4},{4,0},{8,12},{12,8},{1,5},{5,1},{9,13},{13,9},{2,6},{6,2},{1... | collective-permute-start | bytes 442376 | tf_op jit(solution)/shard_map/ppermute | solution.py:460
  84.1 11.2 %collective-permute-start.15 = (bf16[192,768]{1,0:T(8,128)(2,1)S(1)}, bf16[192,768]{1,0:T(8,128)(2,1)S(1)}, u32[]{:S(2)}, u32[]{:S(2)}) collective-permute-start(bf16[192,768]{1,0:T(8,128)(2,1)S(1)} %shard_map.122), channel_id=1, source_target_pairs={{0,0},{1,4},{2,2},{3,6},{4,1},{5,5},{6,3},{7,7},{8,8},{9,12},{10,1... | collective-permute-start | bytes 884744 | tf_op jit(solution)/shard_map/ppermute | solution.py:576
  84.8 16.2 %collective-permute-start.22 = (bf16[2,192,384]{2,1,0:T(8,128)(2,1)S(1)}, bf16[2,192,384]{2,1,0:T(8,128)(2,1)S(1)}, u32[]{:S(2)}, u32[]{:S(2)}) collective-permute-start(bf16[2,192,384]{2,1,0:T(8,128)(2,1)S(1)} %get-tuple-element.88), channel_id=1, source_target_pairs={{0,8},{4,12},{8,0},{12,4},{1,9},{5,13},{9,1},{13,5},{2,10},{6,14},... | collective-permute-start | bytes 884744 | tf_op jit(solution)/shard_map/ppermute | solution.py:460
  85.5 17.3 %collective-permute-start.23 = (bf16[2,192,384]{2,1,0:T(8,128)(2,1)S(1)}, bf16[2,192,384]{2,1,0:T(8,128)(2,1)S(1)}, u32[]{:S(2)}, u32[]{:S(2)}) collective-permute-start(bf16[2,192,384]{2,1,0:T(8,128)(2,1)S(1)} %shard_map.129), channel_id=1, source_target_pairs={{0,4},{4,0},{8,12},{12,8},{1,5},{5,1},{9,13},{13,9},{2,6},{6,2},{1... | collective-permute-start | bytes 884744 | tf_op jit(solution)/shard_map/ppermute | solution.py:460
  96.0 9.6 %all-to-all-start = ((f32[4,1,768]{2,1,0:T(1,128)}), f32[4,1,768]{2,1,0:T(1,128)S(1)}, u32[]{:S(2)}, u32[]{:S(2)}) async-start(f32[4,1,768]{2,1,0:T(1,128)} %get-tuple-element.95), calls=%async_computation | async-start | bytes 24576 | tf_op jit(solution)/shard_map/all_to_all | solution.py:583

commit v6 on v5

--- a/solution.py
+++ b/solution.py
@@ -511,9 +511,8 @@
         flops=6 * unit_flops,
         smem=(0,),
     )
-    near_b, far_a, attended = lax.optimization_barrier(
-        (permute(near_b, "seq", 2), swap(near_a), attended)
-    )
+    near_b, attended = lax.optimization_barrier((permute(near_b, "seq", 2), attended))
+    far_a = swap(near_a)
     cots = (turn(cot_late, 0), cot_1, cot_2, turn(cot_late, 3))
     heads = (attended, permute(attended, "seq", 1))
     grad_own, grad_send, cot_all, weight_y = call(

time: 107 us -> 105 us (0.981)
  waiting for transfers between devices: 49 us -> 47 us
    ppermute x4, waiting for transfers between devices: 8.64 us -> 6.72 us  [turn(): lax.ppermute(value, both, [(a * n + b, (a & 2 | b & 1) * n + (b ^ k ^ (a...]
where the time goes in v6:
time: 105 us; the launch traced here: 104 us
  waiting for transfers between devices  47 us (45%)
  starting transfers between devices  36.6 us (35%)
  Pallas kernels  16 us (15%)
  local copies, waits for them, and re-layouts  3.3 us (3%)
  between operations  1.47 us (1%)
    ppermute x15, waiting for transfers between devices, permute(): return lax.ppermute(value, axes, xor_pairs(n, k))  35.5 us
    ppermute x15, starting transfers between devices, permute(): return lax.ppermute(value, axes, xor_pairs(n, k))  23.8 us
    pallas_call x13, Pallas kernels, call(): pl.pallas_call(kernel, out_shape=out_shape, in_specs=[pl.BlockSpec(memory...  16 us
    ppermute x4, starting transfers between devices, turn(): lax.ppermute(value, both, [(a * n + b, (a & 2 | b & 1) * n + (b ^ k ^ (a...  6.98 us
    ppermute x4, waiting for transfers between devices, turn(): lax.ppermute(value, both, [(a * n + b, (a & 2 | b & 1) * n + (b ^ k ^ (a...  6.72 us
    all_to_all x1, starting transfers between devices, square_shards(): lax.all_to_all(grad_gate, 'seq', 0, 0, tiled=True)  4.94 us
    ppermute x4, waiting for transfers between devices, swap(): return lax.ppermute(value, 'dp', xor_pairs(2, 1))  2.84 us
    unnamed x14, local copies, waits for them, and re-layouts  2.69 us
  transfers between devices with their start and end apart: 25, of which 14 were waited for; matrix products, arithmetic and copies ran while one was open for 0% of the time, Pallas kernels for 9%

profile of v6, /device:TPU:0, one launch (start us, length us, event | category | flops | bytes accessed | tf_op | source)
XLA Modules:
  0.0 104.4 jit_solution(9433504679789546828)
XLA Ops:
  0.6 2.7 %shard_map.118 = (bf16[2,192,384]{2,1,0:T(8,128)(2,1)}, bf16[192,384]{1,0:T(8,128)(2,1)}, bf16[3,192,384]{2,1,0:T(8,128)(2,1)}, bf16[192,768]{1,0:T(8,128)(2,1)}, bf16[192,768]{1,0:T(8,128)(2,1)}) custom-call(bf16[1,192,768]{2,1,0:T(8,128)(2,1)} %q_ref.1, bf16[1,192,768]{2,1,0:T(8,128)(2,1)} %k_ref.1, bf16[1,192,768]{2,1,0:T(8,128)(2,1)} %v_ref.1, ...), custom_call_target="tpu_custom_call" | custom-call | bytes 3538944 | tf_op jit(solution)/shard_map/pallas_call | solution.py:230
  3.3 0.0 copy-start
  3.3 0.0 copy-start.2
  3.3 3.0 %collective-permute-start = (bf16[3,192,384]{2,1,0:T(8,128)(2,1)}, bf16[3,192,384]{2,1,0:T(8,128)(2,1)S(1)}, u32[]{:S(2)}, u32[]{:S(2)}) collective-permute-start(bf16[3,192,384]{2,1,0:T(8,128)(2,1)} %get-tuple-element.50), channel_id=1, source_target_pairs={{0,4},{4,0},{8,12},{12,8},{1,5},{5,1},{9,13},{13,9},{2,6},{6,2},{1... | collective-permute-start | bytes 1327112 | tf_op jit(solution)/shard_map/ppermute | solution.py:460
  6.3 1.5 %collective-permute-start.1 = (bf16[2,192,384]{2,1,0:T(8,128)(2,1)}, bf16[2,192,384]{2,1,0:T(8,128)(2,1)S(1)}, u32[]{:S(2)}, u32[]{:S(2)}) collective-permute-start(bf16[2,192,384]{2,1,0:T(8,128)(2,1)} %get-tuple-element.51.refs_0_), channel_id=1, source_target_pairs={{0,8},{4,12},{8,0},{12,4},{1,9},{5,13},{9,1},{13,5},{2,10},{6,14},... | collective-permute-start | bytes 884744 | tf_op jit(solution)/shard_map/ppermute | solution.py:460
  7.9 0.5 collective-permute-start.2
  8.4 1.6 %collective-permute-start.3 = (bf16[1,192,768]{2,1,0:T(8,128)(2,1)S(1)}, bf16[1,192,768]{2,1,0:T(8,128)(2,1)S(1)}, u32[]{:S(2)}, u32[]{:S(2)}) collective-permute-start(bf16[1,192,768]{2,1,0:T(8,128)(2,1)S(1)} %copy-done.1), channel_id=1, source_target_pairs={{0,1},{1,5},{2,3},{3,7},{4,0},{5,4},{6,2},{7,6},{8,9},{9,13},{10,1... | collective-permute-start | bytes 884744 | tf_op jit(solution)/shard_map/ppermute | solution.py:482
  9.9 2.6 %collective-permute-start.4 = (bf16[1,192,768]{2,1,0:T(8,128)(2,1)S(1)}, bf16[1,192,768]{2,1,0:T(8,128)(2,1)S(1)}, u32[]{:S(2)}, u32[]{:S(2)}) collective-permute-start(bf16[1,192,768]{2,1,0:T(8,128)(2,1)S(1)} %copy-done.1), channel_id=1, source_target_pairs={{0,2},{1,6},{2,0},{3,4},{4,3},{5,7},{6,1},{7,5},{8,10},{9,14},{10,... | collective-permute-start | bytes 884744 | tf_op jit(solution)/shard_map/ppermute | solution.py:482
  12.5 3.9 %collective-permute-done.1.refs_2_ = bf16[2,192,384]{2,1,0:T(8,128)(2,1)S(1)} collective-permute-done((bf16[2,192,384]{2,1,0:T(8,128)(2,1)}, bf16[2,192,384]{2,1,0:T(8,128)(2,1)S(1)}, u32[]{:S(2)}, u32[]{:S(2)}) %collective-permute-start.1) | collective-permute-done | bytes 294944 | tf_op jit(solution)/shard_map/ppermute | solution.py:460
  16.5 4.9 %collective-permute-done.2.refs_0_ = bf16[192,768]{1,0:T(8,128)(2,1)S(1)} collective-permute-done((bf16[192,768]{1,0:T(8,128)(2,1)}, bf16[192,768]{1,0:T(8,128)(2,1)S(1)}, u32[]{:S(2)}, u32[]{:S(2)}) %collective-permute-start.2) | collective-permute-done | bytes 294944 | tf_op jit(solution)/shard_map/ppermute | solution.py:460
  21.3 1.7 %collective-permute-done.3.refs_5_ = bf16[1,192,768]{2,1,0:T(8,128)(2,1)S(1)} collective-permute-done((bf16[1,192,768]{2,1,0:T(8,128)(2,1)S(1)}, bf16[1,192,768]{2,1,0:T(8,128)(2,1)S(1)}, u32[]{:S(2)}, u32[]{:S(2)}) %collective-permute-start.3) | collective-permute-done | bytes 294944 | tf_op jit(solution)/shard_map/ppermute | solution.py:482
  23.0 1.8 %collective-permute-done.4.refs_6_ = bf16[1,192,768]{2,1,0:T(8,128)(2,1)S(1)} collective-permute-done((bf16[1,192,768]{2,1,0:T(8,128)(2,1)S(1)}, bf16[1,192,768]{2,1,0:T(8,128)(2,1)S(1)}, u32[]{:S(2)}, u32[]{:S(2)}) %collective-permute-start.4) | collective-permute-done | bytes 294944 | tf_op jit(solution)/shard_map/ppermute | solution.py:482
  24.8 0.0 collective-permute-done.refs_1_
  24.8 1.6 %collective-permute-start.6 = (bf16[2,192,384]{2,1,0:T(8,128)(2,1)S(1)}, bf16[2,192,384]{2,1,0:T(8,128)(2,1)S(1)}, u32[]{:S(2)}, u32[]{:S(2)}) collective-permute-start(bf16[2,192,384]{2,1,0:T(8,128)(2,1)S(1)} %slice.3), channel_id=1, source_target_pairs={{0,8},{4,12},{8,0},{12,4},{1,9},{5,13},{9,1},{13,5},{2,10},{6,14},... | collective-permute-start | bytes 884744 | tf_op jit(solution)/shard_map/ppermute | solution.py:460
  26.4 0.5 collective-permute-start.5
  27.6 2.1 %collective-permute-start.10 = (bf16[1,192,768]{2,1,0:T(8,128)(2,1)S(1)}, bf16[1,192,768]{2,1,0:T(8,128)(2,1)S(1)}, u32[]{:S(2)}, u32[]{:S(2)}) collective-permute-start(bf16[1,192,768]{2,1,0:T(8,128)(2,1)S(1)} %copy-done.1), channel_id=1, source_target_pairs={{0,3},{1,7},{2,1},{3,5},{4,2},{5,6},{6,0},{7,4},{8,11},{9,15},{10,... | collective-permute-start | bytes 884744 | tf_op jit(solution)/shard_map/ppermute | solution.py:482
  29.7 0.7 collective-permute-start.9
  30.4 0.1 collective-permute-start.7
  30.5 4.4 %collective-permute-done.6.refs_3_ = bf16[2,192,384]{2,1,0:T(8,128)(2,1)S(1)} collective-permute-done((bf16[2,192,384]{2,1,0:T(8,128)(2,1)S(1)}, bf16[2,192,384]{2,1,0:T(8,128)(2,1)S(1)}, u32[]{:S(2)}, u32[]{:S(2)}) %collective-permute-start.6) | collective-permute-done | bytes 294944 | tf_op jit(solution)/shard_map/ppermute | solution.py:460
  34.8 1.0 copy-done.3
  35.8 0.9 copy-done.5
  36.7 2.0 %shard_map.119 = (bf16[2,192,384]{2,1,0:T(8,128)(2,1)S(1)}, f32[3,384]{1,0:T(4,128)S(1)}) custom-call(s32[1]{0:T(128)S(6)} %copy.13.len_ref, bf16[2,192,384]{2,1,0:T(8,128)(2,1)S(1)} %copy-done.3, bf16[3,192,384]{2,1,0:T(8,128)(2,1)S(1)} %collective-permute-done.refs_1_, bf16[2,192,384]{2,1,0:T(8,128)(2,1)S(1)} %collective-permute-done.1.refs_2_, ...), custom_call_target="tpu_custom_call" | custom-call | flops 452984832 | bytes 1774084 | tf_op jit(solution)/shard_map/pallas_call | solution.py:230
  38.7 0.6 collective-permute-done.5.refs_1_
  39.3 3.3 %collective-permute-done.10.refs_7_ = bf16[1,192,768]{2,1,0:T(8,128)(2,1)S(1)} collective-permute-done((bf16[1,192,768]{2,1,0:T(8,128)(2,1)S(1)}, bf16[1,192,768]{2,1,0:T(8,128)(2,1)S(1)}, u32[]{:S(2)}, u32[]{:S(2)}) %collective-permute-start.10) | collective-permute-done | bytes 294944 | tf_op jit(solution)/shard_map/ppermute | solution.py:482
  42.6 0.0 collective-permute-done.7.refs_2_
  42.6 0.0 collective-permute-done.9.refs_4_
  42.6 0.0 collective-permute-done.8.refs_3_
  42.6 1.4 %shard_map.120 = (f32[2,192,384]{2,1,0:T(8,128)S(1)}, bf16[2,192,384]{2,1,0:T(8,128)(2,1)S(1)}, bf16[4,192,768]{2,1,0:T(8,128)(2,1)S(1)}, bf16[768,768]{1,0:T(8,128)(2,1)S(1)}) custom-call(f32[1,3072]{1,0:T(1,128)S(1)} %copy-done.2, bf16[768,768]{1,0:T(8,128)(2,1)S(1)} %copy-done, bf16[192,768]{1,0:T(8,128)(2,1)S(1)} %collective-permute-done.2.refs_0_, ...), custom_call_target="tpu_custom_call" | custom-call | flops 905969664 | bytes 6795264 | tf_op jit(solution)/shard_map/pallas_call | solution.py:230
  44.0 4.9 %collective-permute-done.11.other_ref = bf16[2,192,384]{2,1,0:T(8,128)(2,1)S(1)} collective-permute-done((bf16[2,192,384]{2,1,0:T(8,128)(2,1)S(1)}, bf16[2,192,384]{2,1,0:T(8,128)(2,1)S(1)}, u32[]{:S(2)}, u32[]{:S(2)}) %collective-permute-start.11) | collective-permute-done | bytes 294944 | tf_op jit(solution)/shard_map/ppermute | solution.py:460
  48.9 1.2 %shard_map.121 = (f32[192,768]{1,0:T(8,128)S(1)}, bf16[192,768]{1,0:T(8,128)(2,1)S(1)}, bf16[192,768]{1,0:T(8,128)(2,1)S(1)}, bf16[192,768]{1,0:T(8,128)(2,1)S(1)}, bf16[384,768]{1,0:T(8,128)(2,1)S(1)}) custom-call(bf16[768,768]{1,0:T(8,128)(2,1)S(1)} %copy-done, bf16[768,768]{1,0:T(8,128)(2,1)S(1)} %get-tuple-element.64.w2_ref, ...), custom_call_target="tpu_custom_call" | custom-call | flops 905969664 | bytes 5013504 | tf_op jit(solution)/shard_map/pallas_call | solution.py:230
  50.1 2.0 %shard_map.123 = (f32[2,384,768]{2,1,0:T(8,128)S(1)}, bf16[2,384,768]{2,1,0:T(8,128)(2,1)S(1)}) custom-call(f32[1,3072]{1,0:T(1,128)S(1)} %copy-done.2, bf16[384,768]{1,0:T(8,128)(2,1)S(1)} %get-tuple-element.70.all_ref, bf16[4,192,768]{2,1,0:T(8,128)(2,1)S(1)} %get-tuple-element.71.cot_ref), custom_call_target="tpu_custom_call" | custom-call | flops 905969664 | bytes 5320704 | tf_op jit(solution)/shard_map/pallas_call | solution.py:230
  52.1 0.1 collective-permute-start.16
  52.2 2.8 %collective-permute-done.16.other_ref = bf16[2,384,768]{2,1,0:T(8,128)(2,1)S(1)} collective-permute-done((bf16[2,384,768]{2,1,0:T(8,128)(2,1)S(1)}, bf16[2,384,768]{2,1,0:T(8,128)(2,1)S(1)}, u32[]{:S(2)}, u32[]{:S(2)}) %collective-permute-start.16) | collective-permute-done | bytes 1179680 | tf_op jit(solution)/shard_map/ppermute | solution.py:463
  55.1 0.3 shard_map.124
  55.3 1.6 %collective-permute-start.17 = (bf16[384,768]{1,0:T(8,128)(2,1)S(1)}, bf16[384,768]{1,0:T(8,128)(2,1)S(1)}, u32[]{:S(2)}, u32[]{:S(2)}) collective-permute-start(bf16[384,768]{1,0:T(8,128)(2,1)S(1)} %get-tuple-element.75), channel_id=1, source_target_pairs={{0,8},{4,12},{8,0},{12,4},{1,9},{5,13},{9,1},{13,5},{2,10},{6,14},... | collective-permute-start | bytes 1769480 | tf_op jit(solution)/shard_map/ppermute | solution.py:460
  56.9 0.1 collective-permute-start.19
  57.0 1.1 %collective-permute-start.12 = (bf16[192,768]{1,0:T(8,128)(2,1)S(1)}, bf16[192,768]{1,0:T(8,128)(2,1)S(1)}, u32[]{:S(2)}, u32[]{:S(2)}) collective-permute-start(bf16[192,768]{1,0:T(8,128)(2,1)S(1)} %get-tuple-element.67), channel_id=1, source_target_pairs={{0,1},{1,0},{2,3},{3,2},{4,5},{5,4},{6,7},{7,6},{8,9},{9,8},{10,11... | collective-permute-start | bytes 884744 | tf_op jit(solution)/shard_map/ppermute | solution.py:460
  58.1 3.4 %collective-permute-start.13 = (bf16[192,768]{1,0:T(8,128)(2,1)S(1)}, bf16[192,768]{1,0:T(8,128)(2,1)S(1)}, u32[]{:S(2)}, u32[]{:S(2)}) collective-permute-start(bf16[192,768]{1,0:T(8,128)(2,1)S(1)} %get-tuple-element.68), channel_id=1, source_target_pairs={{0,2},{1,3},{2,0},{3,1},{4,6},{5,7},{6,4},{7,5},{8,10},{9,11},{10,... | collective-permute-start | bytes 884744 | tf_op jit(solution)/shard_map/ppermute | solution.py:460
  61.5 0.0 collective-permute-start.14
  61.5 9.2 %collective-permute-done.17.other_ref = bf16[384,768]{1,0:T(8,128)(2,1)S(1)} collective-permute-done((bf16[384,768]{1,0:T(8,128)(2,1)S(1)}, bf16[384,768]{1,0:T(8,128)(2,1)S(1)}, u32[]{:S(2)}, u32[]{:S(2)}) %collective-permute-start.17) | collective-permute-done | bytes 589856 | tf_op jit(solution)/shard_map/ppermute | solution.py:460
  70.8 0.1 shard_map.125.own_ref
  70.9 0.1 collective-permute-start.18
  70.9 0.0 collective-permute-done.19.other_ref
  71.0 0.8 copy-done.4
  71.7 0.0 copy-done.6
  71.8 2.8 %shard_map.128 = (bf16[192,384]{1,0:T(8,128)(2,1)S(1)}, bf16[192,384]{1,0:T(8,128)(2,1)S(1)}, f32[2,192,384]{2,1,0:T(8,128)S(1)}, f32[2,192,384]{2,1,0:T(8,128)S...) custom-call(s32[1]{0:T(128)S(6)} %copy.13.len_ref, f32[3,384]{1,0:T(4,128)S(1)} %get-tuple-element.78.lse_ref, ...), custom_call_target="tpu_custom_call" | custom-call | flops 1132462080 | bytes 4723204 | tf_op jit(solution)/shard_map/pallas_call | solution.py:230
  74.5 1.6 %collective-permute-start.20 = (bf16[2,192,384]{2,1,0:T(8,128)(2,1)S(1)}, bf16[2,192,384]{2,1,0:T(8,128)(2,1)S(1)}, u32[]{:S(2)}, u32[]{:S(2)}) collective-permute-start(bf16[2,192,384]{2,1,0:T(8,128)(2,1)S(1)} %get-tuple-element.82), channel_id=1, source_target_pairs={{0,8},{4,12},{8,0},{12,4},{1,9},{5,13},{9,1},{13,5},{2,10},{6,14},... | collective-permute-start | bytes 884744 | tf_op jit(solution)/shard_map/ppermute | solution.py:460
  76.1 0.1 collective-permute-start.21
  76.3 5.8 %collective-permute-done.13.refs_1_ = bf16[192,768]{1,0:T(8,128)(2,1)S(1)} collective-permute-done((bf16[192,768]{1,0:T(8,128)(2,1)S(1)}, bf16[192,768]{1,0:T(8,128)(2,1)S(1)}, u32[]{:S(2)}, u32[]{:S(2)}) %collective-permute-start.13) | collective-permute-done | bytes 294944 | tf_op jit(solution)/shard_map/ppermute | solution.py:460
  82.1 0.0 collective-permute-done.14.refs_2_
  82.1 0.2 shard_map.122
  82.2 0.7 collective-permute-start.15
  82.9 0.6 collective-permute-start.22
  83.5 0.0 collective-permute-done.21.dq_other_ref
  83.5 0.1 collective-permute-done.20.other_ref
  83.6 0.1 shard_map.129
  83.7 8.2 %collective-permute-start.23 = (bf16[2,192,384]{2,1,0:T(8,128)(2,1)S(1)}, bf16[2,192,384]{2,1,0:T(8,128)(2,1)S(1)}, u32[]{:S(2)}, u32[]{:S(2)}) collective-permute-start(bf16[2,192,384]{2,1,0:T(8,128)(2,1)S(1)} %shard_map.129), channel_id=1, source_target_pairs={{0,4},{4,0},{8,12},{12,8},{1,5},{5,1},{9,13},{13,9},{2,6},{6,2},{1... | collective-permute-start | bytes 884744 | tf_op jit(solution)/shard_map/ppermute | solution.py:460
  91.8 1.6 %shard_map.126 = f32[768,768]{1,0:T(8,128)} custom-call(bf16[384,768]{1,0:T(8,128)(2,1)S(1)} %shard_map.125.own_ref, bf16[384,768]{1,0:T(8,128)(2,1)S(1)} %collective-permute-done.18.other_ref), custom_call_target="tpu_custom_call" | custom-call | bytes 3538944 | tf_op jit(solution)/shard_map/pallas_call | solution.py:230
  93.4 0.8 shard_map.127
  94.2 4.9 %all-to-all-start = ((f32[4,1,768]{2,1,0:T(1,128)}), f32[4,1,768]{2,1,0:T(1,128)S(1)}, u32[]{:S(2)}, u32[]{:S(2)}) async-start(f32[4,1,768]{2,1,0:T(1,128)} %get-tuple-element.93), calls=%async_computation | async-start | bytes 24576 | tf_op jit(solution)/shard_map/all_to_all | solution.py:582
  99.1 1.8 %collective-permute-done.23.other_ref = bf16[2,192,384]{2,1,0:T(8,128)(2,1)S(1)} collective-permute-done((bf16[2,192,384]{2,1,0:T(8,128)(2,1)S(1)}, bf16[2,192,384]{2,1,0:T(8,128)(2,1)S(1)}, u32[]{:S(2)}, u32[]{:S(2)}) %collective-permute-start.23) | collective-permute-done | bytes 294944 | tf_op jit(solution)/shard_map/ppermute | solution.py:460
  100.9 1.0 shard_map.130
  101.9 1.9 %all-to-all-done = f32[4,1,768]{2,1,0:T(1,128)S(1)} async-done(((f32[4,1,768]{2,1,0:T(1,128)}), f32[4,1,768]{2,1,0:T(1,128)S(1)}, u32[]{:S(2)}, u32[]{:S(2)}) %all-to-all-start) | async-done | bytes 12320 | tf_op jit(solution)/shard_map/all_to_all | solution.py:582
  103.9 0.6 reduce_sum.12
  (16 shorter events, 0.1 us)
Async XLA Ops:
  0.6 7.7 %copy-start.1 = (bf16[1,192,768]{2,1,0:T(8,128)(2,1)S(1)}, bf16[1,192,768]{2,1,0:T(8,128)(2,1)}, u32[]{:S(2)}) copy-start(bf16[1,192,768]{2,1,0:T(8,128)(2,1)} %cot_ref.1) | copy-start | bytes 884740
  3.3 39.3 %copy-start = (bf16[768,768]{1,0:T(8,128)(2,1)S(1)}, bf16[768,768]{1,0:T(8,128)(2,1)}, u32[]{:S(2)}) copy-start(bf16[768,768]{1,0:T(8,128)(2,1)} %w_ref.5) | copy-start | bytes 3538948
  3.3 39.3 %copy-start.2 = (f32[1,3072]{1,0:T(1,128)S(1)}, f32[1,3072]{1,0:T(1,128)}, u32[]{:S(2)}) copy-start(f32[1,3072]{1,0:T(1,128)} %gate_ref.5) | copy-start | bytes 36868
  3.3 21.5 %collective-permute-start = (bf16[3,192,384]{2,1,0:T(8,128)(2,1)}, bf16[3,192,384]{2,1,0:T(8,128)(2,1)S(1)}, u32[]{:S(2)}, u32[]{:S(2)}) collective-permute-start(bf16[3,192,384]{2,1,0:T(8,128)(2,1)} %get-tuple-element.50), channel_id=1, source_target_pairs={{0,4},{4,0},{8,12},{12,8},{1,5},{5,1},{9,13},{13,9},{2,6},{6,2},{1... | collective-permute-start | bytes 1327112 | tf_op jit(solution)/shard_map/ppermute | solution.py:460
  6.3 10.1 %collective-permute-start.1 = (bf16[2,192,384]{2,1,0:T(8,128)(2,1)}, bf16[2,192,384]{2,1,0:T(8,128)(2,1)S(1)}, u32[]{:S(2)}, u32[]{:S(2)}) collective-permute-start(bf16[2,192,384]{2,1,0:T(8,128)(2,1)} %get-tuple-element.51.refs_0_), channel_id=1, source_target_pairs={{0,8},{4,12},{8,0},{12,4},{1,9},{5,13},{9,1},{13,5},{2,10},{6,14},... | collective-permute-start | bytes 884744 | tf_op jit(solution)/shard_map/ppermute | solution.py:460
  7.9 13.5 %collective-permute-start.2 = (bf16[192,768]{1,0:T(8,128)(2,1)}, bf16[192,768]{1,0:T(8,128)(2,1)S(1)}, u32[]{:S(2)}, u32[]{:S(2)}) collective-permute-start(bf16[192,768]{1,0:T(8,128)(2,1)} %get-tuple-element.52), channel_id=1, source_target_pairs={{0,8},{4,12},{8,0},{12,4},{1,9},{5,13},{9,1},{13,5},{2,10},{6,14},... | collective-permute-start | bytes 884744 | tf_op jit(solution)/shard_map/ppermute | solution.py:460
  8.4 14.7 %collective-permute-start.3 = (bf16[1,192,768]{2,1,0:T(8,128)(2,1)S(1)}, bf16[1,192,768]{2,1,0:T(8,128)(2,1)S(1)}, u32[]{:S(2)}, u32[]{:S(2)}) collective-permute-start(bf16[1,192,768]{2,1,0:T(8,128)(2,1)S(1)} %copy-done.1), channel_id=1, source_target_pairs={{0,1},{1,5},{2,3},{3,7},{4,0},{5,4},{6,2},{7,6},{8,9},{9,13},{10,1... | collective-permute-start | bytes 884744 | tf_op jit(solution)/shard_map/ppermute | solution.py:482
  9.9 14.8 %collective-permute-start.4 = (bf16[1,192,768]{2,1,0:T(8,128)(2,1)S(1)}, bf16[1,192,768]{2,1,0:T(8,128)(2,1)S(1)}, u32[]{:S(2)}, u32[]{:S(2)}) collective-permute-start(bf16[1,192,768]{2,1,0:T(8,128)(2,1)S(1)} %copy-done.1), channel_id=1, source_target_pairs={{0,2},{1,6},{2,0},{3,4},{4,3},{5,7},{6,1},{7,5},{8,10},{9,14},{10,... | collective-permute-start | bytes 884744 | tf_op jit(solution)/shard_map/ppermute | solution.py:482
  24.8 10.0 %collective-permute-start.6 = (bf16[2,192,384]{2,1,0:T(8,128)(2,1)S(1)}, bf16[2,192,384]{2,1,0:T(8,128)(2,1)S(1)}, u32[]{:S(2)}, u32[]{:S(2)}) collective-permute-start(bf16[2,192,384]{2,1,0:T(8,128)(2,1)S(1)} %slice.3), channel_id=1, source_target_pairs={{0,8},{4,12},{8,0},{12,4},{1,9},{5,13},{9,1},{13,5},{2,10},{6,14},... | collective-permute-start | bytes 884744 | tf_op jit(solution)/shard_map/ppermute | solution.py:460
  26.4 12.9 %collective-permute-start.5 = (bf16[192,768]{1,0:T(8,128)(2,1)}, bf16[192,768]{1,0:T(8,128)(2,1)S(1)}, u32[]{:S(2)}, u32[]{:S(2)}) collective-permute-start(bf16[192,768]{1,0:T(8,128)(2,1)} %get-tuple-element.55), channel_id=1, source_target_pairs={{0,8},{4,12},{8,0},{12,4},{1,9},{5,13},{9,1},{13,5},{2,10},{6,14},... | collective-permute-start | bytes 884744 | tf_op jit(solution)/shard_map/ppermute | solution.py:460
  27.6 15.0 %collective-permute-start.10 = (bf16[1,192,768]{2,1,0:T(8,128)(2,1)S(1)}, bf16[1,192,768]{2,1,0:T(8,128)(2,1)S(1)}, u32[]{:S(2)}, u32[]{:S(2)}) collective-permute-start(bf16[1,192,768]{2,1,0:T(8,128)(2,1)S(1)} %copy-done.1), channel_id=1, source_target_pairs={{0,3},{1,7},{2,1},{3,5},{4,2},{5,6},{6,0},{7,4},{8,11},{9,15},{10,... | collective-permute-start | bytes 884744 | tf_op jit(solution)/shard_map/ppermute | solution.py:482
  29.7 12.8 %collective-permute-start.9 = (bf16[1,192,768]{2,1,0:T(8,128)(2,1)S(1)}, bf16[1,192,768]{2,1,0:T(8,128)(2,1)S(1)}, u32[]{:S(2)}, u32[]{:S(2)}) collective-permute-start(bf16[1,192,768]{2,1,0:T(8,128)(2,1)S(1)} %copy-done.1), channel_id=1, source_target_pairs={{0,0},{1,4},{2,2},{3,6},{4,1},{5,5},{6,3},{7,7},{8,8},{9,12},{10,1... | collective-permute-start | bytes 884744 | tf_op jit(solution)/shard_map/ppermute | solution.py:482
  30.4 12.2 %collective-permute-start.7 = (bf16[192,768]{1,0:T(8,128)(2,1)S(1)}, bf16[192,768]{1,0:T(8,128)(2,1)S(1)}, u32[]{:S(2)}, u32[]{:S(2)}) collective-permute-start(bf16[192,768]{1,0:T(8,128)(2,1)S(1)} %collective-permute-done.2.refs_0_), channel_id=1, source_target_pairs={{0,16},{16,0},{1,17},{17,1},{2,18},{18,2},{3,19},{19,3},{4,20},{20... | collective-permute-start | bytes 884744 | tf_op jit(solution)/shard_map/ppermute | solution.py:463
  34.8 1.0 copy-start.3
  35.8 0.9 copy-start.5
  39.3 3.3 %collective-permute-start.8 = (bf16[192,768]{1,0:T(8,128)(2,1)S(1)}, bf16[192,768]{1,0:T(8,128)(2,1)S(1)}, u32[]{:S(2)}, u32[]{:S(2)}) collective-permute-start(bf16[192,768]{1,0:T(8,128)(2,1)S(1)} %collective-permute-done.5.refs_1_), channel_id=1, source_target_pairs={{0,16},{16,0},{1,17},{17,1},{2,18},{18,2},{3,19},{19,3},{4,20},{20... | collective-permute-start | bytes 884744 | tf_op jit(solution)/shard_map/ppermute | solution.py:463
  39.3 9.6 %collective-permute-start.11 = (bf16[2,192,384]{2,1,0:T(8,128)(2,1)S(1)}, bf16[2,192,384]{2,1,0:T(8,128)(2,1)S(1)}, u32[]{:S(2)}, u32[]{:S(2)}) collective-permute-start(bf16[2,192,384]{2,1,0:T(8,128)(2,1)S(1)} %get-tuple-element.65.o_ref), channel_id=1, source_target_pairs={{0,4},{4,0},{8,12},{12,8},{1,5},{5,1},{9,13},{13,9},{2,6},{6,2},{1... | collective-permute-start | bytes 884744 | tf_op jit(solution)/shard_map/ppermute | solution.py:460
  52.1 2.9 %collective-permute-start.16 = (bf16[2,384,768]{2,1,0:T(8,128)(2,1)S(1)}, bf16[2,384,768]{2,1,0:T(8,128)(2,1)S(1)}, u32[]{:S(2)}, u32[]{:S(2)}) collective-permute-start(bf16[2,384,768]{2,1,0:T(8,128)(2,1)S(1)} %get-tuple-element.73), channel_id=1, source_target_pairs={{0,16},{16,0},{1,17},{17,1},{2,18},{18,2},{3,19},{19,3},{4,20},{20... | collective-permute-start | bytes 3538952 | tf_op jit(solution)/shard_map/ppermute | solution.py:463
  55.3 15.4 %collective-permute-start.17 = (bf16[384,768]{1,0:T(8,128)(2,1)S(1)}, bf16[384,768]{1,0:T(8,128)(2,1)S(1)}, u32[]{:S(2)}, u32[]{:S(2)}) collective-permute-start(bf16[384,768]{1,0:T(8,128)(2,1)S(1)} %get-tuple-element.75), channel_id=1, source_target_pairs={{0,8},{4,12},{8,0},{12,4},{1,9},{5,13},{9,1},{13,5},{2,10},{6,14},... | collective-permute-start | bytes 1769480 | tf_op jit(solution)/shard_map/ppermute | solution.py:460
  56.9 14.0 %collective-permute-start.19 = (bf16[2,192,384]{2,1,0:T(8,128)(2,1)S(1)}, bf16[2,192,384]{2,1,0:T(8,128)(2,1)S(1)}, u32[]{:S(2)}, u32[]{:S(2)}) collective-permute-start(bf16[2,192,384]{2,1,0:T(8,128)(2,1)S(1)} %get-tuple-element.80), channel_id=1, source_target_pairs={{0,4},{4,0},{8,12},{12,8},{1,5},{5,1},{9,13},{13,9},{2,6},{6,2},{1... | collective-permute-start | bytes 884744 | tf_op jit(solution)/shard_map/ppermute | solution.py:460
  57.0 19.1 %collective-permute-start.12 = (bf16[192,768]{1,0:T(8,128)(2,1)S(1)}, bf16[192,768]{1,0:T(8,128)(2,1)S(1)}, u32[]{:S(2)}, u32[]{:S(2)}) collective-permute-start(bf16[192,768]{1,0:T(8,128)(2,1)S(1)} %get-tuple-element.67), channel_id=1, source_target_pairs={{0,1},{1,0},{2,3},{3,2},{4,5},{5,4},{6,7},{7,6},{8,9},{9,8},{10,11... | collective-permute-start | bytes 884744 | tf_op jit(solution)/shard_map/ppermute | solution.py:460
  58.1 24.0 %collective-permute-start.13 = (bf16[192,768]{1,0:T(8,128)(2,1)S(1)}, bf16[192,768]{1,0:T(8,128)(2,1)S(1)}, u32[]{:S(2)}, u32[]{:S(2)}) collective-permute-start(bf16[192,768]{1,0:T(8,128)(2,1)S(1)} %get-tuple-element.68), channel_id=1, source_target_pairs={{0,2},{1,3},{2,0},{3,1},{4,6},{5,7},{6,4},{7,5},{8,10},{9,11},{10,... | collective-permute-start | bytes 884744 | tf_op jit(solution)/shard_map/ppermute | solution.py:460
  61.5 20.6 %collective-permute-start.14 = (bf16[192,768]{1,0:T(8,128)(2,1)S(1)}, bf16[192,768]{1,0:T(8,128)(2,1)S(1)}, u32[]{:S(2)}, u32[]{:S(2)}) collective-permute-start(bf16[192,768]{1,0:T(8,128)(2,1)S(1)} %get-tuple-element.69), channel_id=1, source_target_pairs={{0,3},{1,2},{2,1},{3,0},{4,7},{5,6},{6,5},{7,4},{8,11},{9,10},{10,... | collective-permute-start | bytes 884744 | tf_op jit(solution)/shard_map/ppermute | solution.py:460
  70.8 1.0 copy-start.4
  70.8 1.0 copy-start.6
  70.9 21.0 %collective-permute-start.18 = (bf16[384,768]{1,0:T(8,128)(2,1)S(1)}, bf16[384,768]{1,0:T(8,128)(2,1)S(1)}, u32[]{:S(2)}, u32[]{:S(2)}) collective-permute-start(bf16[384,768]{1,0:T(8,128)(2,1)S(1)} %shard_map.125.own_ref), channel_id=1, source_target_pairs={{0,16},{16,0},{1,17},{17,1},{2,18},{18,2},{3,19},{19,3},{4,20},{20... | collective-permute-start | bytes 1769480 | tf_op jit(solution)/shard_map/ppermute | solution.py:463
  74.5 9.0 %collective-permute-start.20 = (bf16[2,192,384]{2,1,0:T(8,128)(2,1)S(1)}, bf16[2,192,384]{2,1,0:T(8,128)(2,1)S(1)}, u32[]{:S(2)}, u32[]{:S(2)}) collective-permute-start(bf16[2,192,384]{2,1,0:T(8,128)(2,1)S(1)} %get-tuple-element.82), channel_id=1, source_target_pairs={{0,8},{4,12},{8,0},{12,4},{1,9},{5,13},{9,1},{13,5},{2,10},{6,14},... | collective-permute-start | bytes 884744 | tf_op jit(solution)/shard_map/ppermute | solution.py:460
  76.1 7.4 %collective-permute-start.21 = (bf16[192,384]{1,0:T(8,128)(2,1)S(1)}, bf16[192,384]{1,0:T(8,128)(2,1)S(1)}, u32[]{:S(2)}, u32[]{:S(2)}) collective-permute-start(bf16[192,384]{1,0:T(8,128)(2,1)S(1)} %get-tuple-element.83), channel_id=1, source_target_pairs={{0,4},{4,0},{8,12},{12,8},{1,5},{5,1},{9,13},{13,9},{2,6},{6,2},{1... | collective-permute-start | bytes 442376 | tf_op jit(solution)/shard_map/ppermute | solution.py:460
  82.2 11.2 %collective-permute-start.15 = (bf16[192,768]{1,0:T(8,128)(2,1)S(1)}, bf16[192,768]{1,0:T(8,128)(2,1)S(1)}, u32[]{:S(2)}, u32[]{:S(2)}) collective-permute-start(bf16[192,768]{1,0:T(8,128)(2,1)S(1)} %shard_map.122), channel_id=1, source_target_pairs={{0,0},{1,4},{2,2},{3,6},{4,1},{5,5},{6,3},{7,7},{8,8},{9,12},{10,1... | collective-permute-start | bytes 884744 | tf_op jit(solution)/shard_map/ppermute | solution.py:575
  82.9 16.2 %collective-permute-start.22 = (bf16[2,192,384]{2,1,0:T(8,128)(2,1)S(1)}, bf16[2,192,384]{2,1,0:T(8,128)(2,1)S(1)}, u32[]{:S(2)}, u32[]{:S(2)}) collective-permute-start(bf16[2,192,384]{2,1,0:T(8,128)(2,1)S(1)} %get-tuple-element.86), channel_id=1, source_target_pairs={{0,8},{4,12},{8,0},{12,4},{1,9},{5,13},{9,1},{13,5},{2,10},{6,14},... | collective-permute-start | bytes 884744 | tf_op jit(solution)/shard_map/ppermute | solution.py:460
  83.7 17.3 %collective-permute-start.23 = (bf16[2,192,384]{2,1,0:T(8,128)(2,1)S(1)}, bf16[2,192,384]{2,1,0:T(8,128)(2,1)S(1)}, u32[]{:S(2)}, u32[]{:S(2)}) collective-permute-start(bf16[2,192,384]{2,1,0:T(8,128)(2,1)S(1)} %shard_map.129), channel_id=1, source_target_pairs={{0,4},{4,0},{8,12},{12,8},{1,5},{5,1},{9,13},{13,9},{2,6},{6,2},{1... | collective-permute-start | bytes 884744 | tf_op jit(solution)/shard_map/ppermute | solution.py:460
  94.2 9.6 %all-to-all-start = ((f32[4,1,768]{2,1,0:T(1,128)}), f32[4,1,768]{2,1,0:T(1,128)S(1)}, u32[]{:S(2)}, u32[]{:S(2)}) async-start(f32[4,1,768]{2,1,0:T(1,128)} %get-tuple-element.93), calls=%async_computation | async-start | bytes 24576 | tf_op jit(solution)/shard_map/all_to_all | solution.py:582
